TPU v7x, 32 devices: a whole 2x2x4 slice. The times are simulated.
32 devices in a mesh: fsdp: 4 (over z), ctx: 2 (over x), tp: 4 (over y, core).
Axes of the slice: x: 2, y: 2, z: 4, core: 2. Of those that a mesh axis runs over, the one named last changes fastest.
Arguments:
- hidden_in: bfloat16 [4, 1024, 1024], P('fsdp', 'ctx'), may hold values from -6 to 6
- lengths: int32 [4], P('fsdp'), may hold values from 513 to 1024, as said below
- positions: int32 [4, 1024], P('fsdp', 'ctx'), may hold values from 0 to 4092, as said below
- query_weight: bfloat16 [1024, 1024], P('fsdp', 'tp'), may hold values from -0.1875 to 0.1875
- key_weight: bfloat16 [1024, 512], P('fsdp', 'tp'), may hold values from -0.1875 to 0.1875
- value_weight: bfloat16 [1024, 512], P('fsdp', 'tp'), may hold values from -0.1875 to 0.1875
- output_weight: bfloat16 [1024, 1024], P('tp', 'fsdp'), may hold values from -3 to 3
- gate_weight: bfloat16 [1024, 4608], P('fsdp', 'tp'), may hold values from -0.1875 to 0.1875
- up_weight: bfloat16 [1024, 4608], P('fsdp', 'tp'), may hold values from -0.1875 to 0.1875
- down_weight: bfloat16 [4608, 1024], P('tp', 'fsdp'), may hold values from -0.09375 to 0.09375
- attention_gain: bfloat16 [1024], P('fsdp'), may hold values from 0.099609375 to 1.8984375
- feedforward_gain: bfloat16 [1024], P('fsdp'), may hold values from 0.099609375 to 1.8984375
- query_gain: bfloat16 [64], replicated, may hold values from 0.099609375 to 1.8984375
- key_gain: bfloat16 [64], replicated, may hold values from 0.099609375 to 1.8984375
- cotangent: bfloat16 [4, 1024, 1024], P('fsdp', 'ctx'), may hold values from -6 to 6
Outputs:
- block_out: bfloat16 [4, 1024, 1024], P('fsdp', 'ctx')
- input_grad: float32 [4, 1024, 1024], P('fsdp', 'ctx')
- query_weight_grad: float32 [1024, 1024], P('fsdp', 'tp')
- key_weight_grad: float32 [1024, 512], P('fsdp', 'tp')
- value_weight_grad: float32 [1024, 512], P('fsdp', 'tp')
- output_weight_grad: float32 [1024, 1024], P('tp', 'fsdp')
- gate_weight_grad: float32 [1024, 4608], P('fsdp', 'tp')
- up_weight_grad: float32 [1024, 4608], P('fsdp', 'tp')
- down_weight_grad: float32 [4608, 1024], P('tp', 'fsdp')
- attention_gain_grad: float32 [1024], P('fsdp')
- feedforward_gain_grad: float32 [1024], P('fsdp')
- query_gain_grad: float32 [64], replicated
- key_gain_grad: float32 [64], replicated
- rms_stats: float32 [4], replicated
Inputs may be any that keep to these rules, and one draw needn't show every extreme that they name: `lengths`: slots at and after a sequence's length are padding. In every draw one sequence has 1024 valid slots and another 1024 // 2 + 1. Along a sequence positions rise by 1 to 3 from slot to slot; the first lies below 1024.
All inputs are finite; a program needn't handle non-finite values.
Results may differ from a plain program's by a relative error of at most 0.013.
Values may be sent and summed in bfloat16 or wider, within the bound.
No kernel may reach another device: no remote copies, remote signals or barrier semaphores. Data moves between devices by JAX's collectives and lax.ppermute only.
A program may use at most 128 MiB of HBM per device.

v0:
```python
import jax
import jax.numpy as jnp
from jax import lax
from jax.sharding import PartitionSpec as P

HD = 64


epsilon = 1e-05
rope_base = 1000000.0


def product(left, right):
    return jnp.dot(left, right, preferred_element_type=jnp.float32)


def rows_product(left, right):
    return lax.dot_general(
        left, right, (((0,), (0,)), ((), ())), preferred_element_type=jnp.float32
    )


def cols_product(left, right):
    return lax.dot_general(
        left, right, (((1,), (1,)), ((), ())), preferred_element_type=jnp.float32
    )


def normalize(values, gain):
    inverse = lax.rsqrt(jnp.mean(values * values, axis=-1, keepdims=True) + epsilon)
    return values * inverse * gain


def rotate(values, cosine, sine):
    half = values.shape[-1] // 2
    first = values[..., :half]
    second = values[..., half:]
    return jnp.concatenate(
        [first * cosine - second * sine, second * cosine + first * sine], axis=-1
    )


def rope_tables(places, head_size):
    freqs = rope_base ** (-2.0 * jnp.arange(head_size // 2, dtype=jnp.float32) / head_size)
    angles = places.astype(jnp.float32)[:, None] * freqs[None, :]
    return (jnp.cos(angles)[:, None, :], jnp.sin(angles)[:, None, :])


def swiglu(gate, upper):
    return jax.nn.silu(gate) * upper


def shards(
    hidden_in,
    lengths,
    positions,
    query_weight,
    key_weight,
    value_weight,
    output_weight,
    gate_weight,
    up_weight,
    down_weight,
    attention_gain,
    feedforward_gain,
    query_gain,
    key_gain,
    cotangent,
):
    (
        query_full,
        key_full,
        value_full,
        output_full,
        gate_full,
        up_full,
        down_full,
        attention_full,
        feedforward_full,
    ) = (
        lax.all_gather(query_weight, "fsdp", axis=0, tiled=True),
        lax.all_gather(key_weight, "fsdp", axis=0, tiled=True),
        lax.all_gather(value_weight, "fsdp", axis=0, tiled=True),
        lax.all_gather(output_weight, "fsdp", axis=1, tiled=True),
        lax.all_gather(gate_weight, "fsdp", axis=0, tiled=True),
        lax.all_gather(up_weight, "fsdp", axis=0, tiled=True),
        lax.all_gather(down_weight, "fsdp", axis=1, tiled=True),
        lax.all_gather(attention_gain, "fsdp", axis=0, tiled=True),
        lax.all_gather(feedforward_gain, "fsdp", axis=0, tiled=True),
    )
    local = hidden_in.shape[1]
    every = local * lax.axis_size("ctx")
    length = lengths[0]
    query_slots = lax.axis_index("ctx") * local + jnp.arange(local, dtype=jnp.int32)
    key_slots = jnp.arange(every, dtype=jnp.int32)
    valid = (query_slots < length).astype(jnp.float32)
    allowed = (key_slots[None, :] <= query_slots[:, None]) & (key_slots[None, :] < length)
    heads_here = query_full.shape[1] // HD
    groups_here = key_full.shape[1] // HD
    group = heads_here // groups_here
    scale = HD ** (-0.5)
    cosine, sine = rope_tables(positions[0], HD)
    inputs = hidden_in[0].astype(jnp.float32)
    attention_scale = attention_full.astype(jnp.float32)
    normed_f, first_pull = jax.vjp(normalize, inputs, attention_scale)
    normed = normed_f.astype(jnp.bfloat16)
    query_raw = product(normed, query_full)
    key_raw = product(normed, key_full)
    value_raw = product(normed, value_full)

    def shape_heads(query_lin, key_lin, query_scale, key_scale):
        query_rot = rotate(
            normalize(query_lin.reshape(local, heads_here, HD), query_scale), cosine, sine
        )
        key_rot = rotate(
            normalize(key_lin.reshape(local, groups_here, HD), key_scale), cosine, sine
        )
        return (query_rot, key_rot)

    (query_rot, key_rot), heads_pull = jax.vjp(
        shape_heads,
        query_raw,
        key_raw,
        query_gain.astype(jnp.float32),
        key_gain.astype(jnp.float32),
    )
    query_low = query_rot.astype(jnp.bfloat16).reshape(local, groups_here, group, HD)
    key_low = key_rot.astype(jnp.bfloat16).reshape(local, groups_here * HD)
    value_low = value_raw.astype(jnp.bfloat16)
    key_every, value_every = (
        lax.all_gather(key_low, "ctx", axis=0, tiled=True),
        lax.all_gather(value_low, "ctx", axis=0, tiled=True),
    )
    key_every = key_every.reshape(every, groups_here, HD)
    value_every = value_every.reshape(every, groups_here, HD)
    scores = (
        jnp.einsum("qkgd,skd->kgqs", query_low, key_every, preferred_element_type=jnp.float32)
        * scale
    )
    probs = jax.nn.softmax(jnp.where(allowed, scores, -1e30), axis=-1)
    probs_low = probs.astype(jnp.bfloat16)
    mixed = jnp.einsum("kgqs,skd->qkgd", probs_low, value_every, preferred_element_type=jnp.float32)
    mixed_low = mixed.reshape(local, heads_here * HD).astype(jnp.bfloat16)
    attention_part = product(mixed_low, output_full)
    attention_branch = lax.psum(attention_part, "tp")
    middle = inputs + attention_branch
    normed_two_f, second_pull = jax.vjp(normalize, middle, feedforward_full.astype(jnp.float32))
    normed_two = normed_two_f.astype(jnp.bfloat16)
    gate = product(normed_two, gate_full)
    upper = product(normed_two, up_full)
    activated_f, swiglu_pull = jax.vjp(swiglu, gate, upper)
    activated = activated_f.astype(jnp.bfloat16)
    feedforward_part = product(activated, down_full)
    feedforward_branch = lax.psum(feedforward_part.astype(jnp.bfloat16), "tp").astype(jnp.float32)
    output = (middle + feedforward_branch) * valid[:, None]
    upstream = cotangent[0].astype(jnp.float32) * valid[:, None]
    branch_low = upstream.astype(jnp.bfloat16)
    down_grad = rows_product(activated, branch_low)
    activated_grad = cols_product(branch_low, down_full)
    gate_back, upper_back = swiglu_pull(activated_grad)
    gate_low = gate_back.astype(jnp.bfloat16)
    upper_low = upper_back.astype(jnp.bfloat16)
    gate_grad = rows_product(normed_two, gate_low)
    up_grad = rows_product(normed_two, upper_low)
    second_part = cols_product(gate_low, gate_full) + cols_product(upper_low, up_full)
    normed_two_grad = lax.psum(second_part, "tp")
    middle_back, feedforward_gain_grad = second_pull(normed_two_grad)
    middle_grad = upstream + middle_back
    attention_low = middle_grad.astype(jnp.bfloat16)
    output_grad = rows_product(mixed_low, attention_low)
    mixed_grad = (
        cols_product(attention_low, output_full)
        .astype(jnp.bfloat16)
        .reshape(local, groups_here, group, HD)
    )
    value_every_grad = jnp.einsum(
        "kgqs,qkgd->skd", probs_low, mixed_grad, preferred_element_type=jnp.float32
    )
    probs_grad = jnp.einsum(
        "qkgd,skd->kgqs", mixed_grad, value_every, preferred_element_type=jnp.float32
    )
    score_grad = (
        probs * (probs_grad - jnp.sum(probs * probs_grad, axis=-1, keepdims=True))
    ).astype(jnp.bfloat16)
    query_rot_grad = (
        jnp.einsum("kgqs,skd->qkgd", score_grad, key_every, preferred_element_type=jnp.float32)
        * scale
    )
    key_every_grad = (
        jnp.einsum("kgqs,qkgd->skd", score_grad, query_low, preferred_element_type=jnp.float32)
        * scale
    )
    key_back, value_back = (
        lax.psum_scatter(
            key_every_grad.reshape(every, groups_here * HD), "ctx", scatter_dimension=0, tiled=True
        ),
        lax.psum_scatter(
            value_every_grad.reshape(every, groups_here * HD),
            "ctx",
            scatter_dimension=0,
            tiled=True,
        ),
    )
    query_lin_grad, key_lin_grad, query_gain_part, key_gain_part = heads_pull(
        (query_rot_grad.reshape(local, heads_here, HD), key_back.reshape(local, groups_here, HD))
    )
    query_low_grad = query_lin_grad.astype(jnp.bfloat16)
    key_low_grad = key_lin_grad.astype(jnp.bfloat16)
    value_low_grad = value_back.astype(jnp.bfloat16)
    query_grad = rows_product(normed, query_low_grad)
    key_grad = rows_product(normed, key_low_grad)
    value_grad = rows_product(normed, value_low_grad)
    first_part = (
        cols_product(query_low_grad, query_full)
        + cols_product(key_low_grad, key_full)
        + cols_product(value_low_grad, value_full)
    )
    normed_grad, query_gain_sum, key_gain_sum = lax.psum(
        (first_part, query_gain_part, key_gain_part), "tp"
    )
    input_back, attention_gain_grad = first_pull(normed_grad)
    input_grad = middle_grad + input_back
    masked = valid[:, None]
    squares = jnp.stack(
        [
            jnp.sum(item * item * masked)
            for item in (inputs, attention_branch, middle, feedforward_branch)
        ]
    )
    square_total, count_total, query_gain_total, key_gain_total = lax.psum(
        (squares, jnp.sum(valid), query_gain_sum, key_gain_sum), ("fsdp", "ctx")
    )
    block_rows = output.astype(jnp.bfloat16)
    stats = jnp.sqrt(square_total / (count_total * inputs.shape[1]))
    (
        query_share,
        key_share,
        value_share,
        output_share,
        gate_share,
        up_share,
        down_share,
        attention_share,
        feedforward_share,
    ) = (
        lax.psum_scatter(query_grad, "fsdp", scatter_dimension=0, tiled=True),
        lax.psum_scatter(key_grad, "fsdp", scatter_dimension=0, tiled=True),
        lax.psum_scatter(value_grad, "fsdp", scatter_dimension=0, tiled=True),
        lax.psum_scatter(output_grad, "fsdp", scatter_dimension=1, tiled=True),
        lax.psum_scatter(gate_grad, "fsdp", scatter_dimension=0, tiled=True),
        lax.psum_scatter(up_grad, "fsdp", scatter_dimension=0, tiled=True),
        lax.psum_scatter(down_grad, "fsdp", scatter_dimension=1, tiled=True),
        lax.psum_scatter(attention_gain_grad, "fsdp", scatter_dimension=0, tiled=True),
        lax.psum_scatter(feedforward_gain_grad, "fsdp", scatter_dimension=0, tiled=True),
    )
    (
        query_share,
        key_share,
        value_share,
        output_share,
        gate_share,
        up_share,
        down_share,
        attention_share,
        feedforward_share,
    ) = lax.psum(
        (
            query_share,
            key_share,
            value_share,
            output_share,
            gate_share,
            up_share,
            down_share,
            attention_share,
            feedforward_share,
        ),
        "ctx",
    )
    return (
        block_rows[None],
        input_grad[None],
        query_share,
        key_share,
        value_share,
        output_share,
        gate_share,
        up_share,
        down_share,
        attention_share,
        feedforward_share,
        query_gain_total,
        key_gain_total,
        stats,
    )


def solution(mesh):
    in_specs = (
        P("fsdp", "ctx", None),
        P("fsdp"),
        P("fsdp", "ctx"),
        P("fsdp", "tp"),
        P("fsdp", "tp"),
        P("fsdp", "tp"),
        P("tp", "fsdp"),
        P("fsdp", "tp"),
        P("fsdp", "tp"),
        P("tp", "fsdp"),
        P("fsdp"),
        P("fsdp"),
        P(),
        P(),
        P("fsdp", "ctx", None),
    )
    out_specs = (
        P("fsdp", "ctx", None),
        P("fsdp", "ctx", None),
        P("fsdp", "tp"),
        P("fsdp", "tp"),
        P("fsdp", "tp"),
        P("tp", "fsdp"),
        P("fsdp", "tp"),
        P("fsdp", "tp"),
        P("tp", "fsdp"),
        P("fsdp"),
        P("fsdp"),
        P(),
        P(),
        P(),
    )
    return jax.shard_map(shards, mesh=mesh, in_specs=in_specs, out_specs=out_specs, check_vma=False)
```

profile of v0, /device:TPU:0, one launch (start us, length us, event | category | flops | bytes accessed | tf_op | source)
XLA Modules:
  0.0 973.6 jit_solution(9044124267426091301)
XLA Ops:
  14.0 12.6 %all-gather = bf16[4,1,256]{2,1,0:T(2,128)(2,1)S(1)} all-gather(bf16[1,1,256]{2,1,0:T(2,128)(2,1)S(1)} %reshape.288), channel_id=1, replica_groups=mesh['fsdp'=4,'ctx'=2,'tp'=4] {'fsdp'}, dimensions={0}, use_global_device_ids=true | all-gather | bytes 2560 | tf_op jit(solution)/shard_map/all_gather | solution.py:88
  26.6 14.1 %all_gather.36 = bf16[1024,128]{1,0:T(8,128)(2,1)S(1)} all-gather(bf16[256,128]{1,0:T(8,128)(2,1)} %param.19), channel_id=1, replica_groups=mesh['fsdp'=4,'ctx'=2,'tp'=4] {'fsdp'}, dimensions={0}, use_global_device_ids=true | all-gather | bytes 327680 | tf_op jit(solution)/shard_map/all_gather | solution.py:82
  40.7 14.5 %all_gather.34 = bf16[1024,128]{1,0:T(8,128)(2,1)S(1)} all-gather(bf16[256,128]{1,0:T(8,128)(2,1)} %param.20), channel_id=1, replica_groups=mesh['fsdp'=4,'ctx'=2,'tp'=4] {'fsdp'}, dimensions={0}, use_global_device_ids=true | all-gather | bytes 327680 | tf_op jit(solution)/shard_map/all_gather | solution.py:83
  71.9 15.8 %all_gather.38 = bf16[1024,256]{1,0:T(8,128)(2,1)S(1)} all-gather(bf16[256,256]{1,0:T(8,128)(2,1)S(1)} %copy-done.30), channel_id=1, replica_groups=mesh['fsdp'=4,'ctx'=2,'tp'=4] {'fsdp'}, dimensions={0}, use_global_device_ids=true | all-gather | bytes 655360 | tf_op jit(solution)/shard_map/all_gather | solution.py:81
  87.7 14.7 %all_gather.39 = bf16[256,1024]{1,0:T(8,128)(2,1)S(1)} all-gather(bf16[256,256]{1,0:T(8,128)(2,1)S(1)} %copy-done.31), channel_id=1, replica_groups=mesh['fsdp'=4,'ctx'=2,'tp'=4] {'fsdp'}, dimensions={1}, use_global_device_ids=true | all-gather | bytes 655360 | tf_op jit(solution)/shard_map/all_gather | solution.py:84
  118.5 9.3 all-gather.1
  128.5 38.9 %all-reduce.17.cloned.1.call-done = f32[512,1024]{1,0:T(8,128)} async-done(((f32[512,1024]{1,0:T(8,128)}), f32[512,1024]{1,0:T(8,128)}) %all-reduce.17.cloned.1.call-update) | async-done | bytes 2097168 | tf_op jit(solution)/shard_map/psum | solution.py:145
  176.7 41.6 %all-gather.6.cloned.1.call-done = bf16[1024,1152]{1,0:T(8,128)(2,1)} async-done(((bf16[256,1152]{1,0:T(8,128)(2,1)}), bf16[1024,1152]{1,0:T(8,128)(2,1)}) %all-gather.6.cloned.1.call-update) | async-done | bytes 2359312 | tf_op jit(solution)/shard_map/all_gather | solution.py:85
  223.1 45.7 %all-gather.10.cloned.1.call-done = bf16[1152,1024]{1,0:T(8,128)(2,1)} async-done(((bf16[1152,256]{1,0:T(8,128)(2,1)}), bf16[1152,1024]{1,0:T(8,128)(2,1)}) %all-gather.10.cloned.1.call-update) | async-done | bytes 2359312 | tf_op jit(solution)/shard_map/all_gather | solution.py:87
  268.8 6.8 multiply_convert_fusion
  285.9 44.9 %all-reduce.21.cloned.1.call-done = f32[512,1024]{1,0:T(8,128)} async-done(((f32[512,1024]{1,0:T(8,128)}), f32[512,1024]{1,0:T(8,128)}) %all-reduce.21.cloned.1.call-update) | async-done | bytes 2097168 | tf_op jit(solution)/shard_map/psum | solution.py:166
  334.7 35.3 %all-reduce.19.cloned.1.call-done = bf16[512,1024]{1,0:T(8,128)(2,1)} async-done(((bf16[512,1024]{1,0:T(8,128)(2,1)}), bf16[512,1024]{1,0:T(8,128)(2,1)}) %all-reduce.19.cloned.1.call-update) | async-done | bytes 1048592 | tf_op jit(solution)/shard_map/psum | solution.py:154
  387.4 7.0 fusion.3
  411.3 7.8 reduce-scatter.10.cloned.1.call-done
  453.5 17.3 %reduce-scatter.20.cloned.1.call-done = f32[256,256]{1,0:T(8,128)} async-done(((f32[256,1024]{1,0:T(8,128)}), f32[256,256]{1,0:T(8,128)}) %reduce-scatter.20.cloned.1.call-update) | async-done | bytes 262160 | tf_op jit(solution)/shard_map/reduce_scatter | solution.py:249
  470.8 22.6 %reduce-scatter.16.cloned.1.call-done = f32[256,128]{1,0:T(8,128)} async-done(((f32[1024,128]{1,0:T(8,128)}), f32[256,128]{1,0:T(8,128)}) %reduce-scatter.16.cloned.1.call-update) | async-done | bytes 131088 | tf_op jit(solution)/shard_map/reduce_scatter | solution.py:247
  493.4 27.8 %reduce-scatter.14.cloned.1.call-done = f32[256,256]{1,0:T(8,128)} async-done(((f32[1024,256]{1,0:T(8,128)}), f32[256,256]{1,0:T(8,128)}) %reduce-scatter.14.cloned.1.call-update) | async-done | bytes 262160 | tf_op jit(solution)/shard_map/reduce_scatter | solution.py:246
  521.2 86.2 %reduce-scatter.26.cloned.1.call-done = f32[1152,256]{1,0:T(8,128)} async-done(((f32[1152,1024]{1,0:T(8,128)}), f32[1152,256]{1,0:T(8,128)}) %reduce-scatter.26.cloned.1.call-update) | async-done | bytes 1179664 | tf_op jit(solution)/shard_map/reduce_scatter | solution.py:252
  607.3 88.2 %reduce-scatter.24.cloned.1.call-done = f32[256,1152]{1,0:T(8,128)} async-done(((f32[1024,1152]{1,0:T(8,128)}), f32[256,1152]{1,0:T(8,128)}) %reduce-scatter.24.cloned.1.call-update) | async-done | bytes 1179664 | tf_op jit(solution)/shard_map/reduce_scatter | solution.py:251
  695.6 88.1 %reduce-scatter.22.cloned.1.call-done = f32[256,1152]{1,0:T(8,128)} async-done(((f32[1024,1152]{1,0:T(8,128)}), f32[256,1152]{1,0:T(8,128)}) %reduce-scatter.22.cloned.1.call-update) | async-done | bytes 1179664 | tf_op jit(solution)/shard_map/reduce_scatter | solution.py:250
  793.0 45.7 %all-reduce.23.cloned.1.call-done = f32[512,1024]{1,0:T(8,128)} async-done(((f32[512,1024]{1,0:T(8,128)}), f32[512,1024]{1,0:T(8,128)}) %all-reduce.23.cloned.1.call-update) | async-done | bytes 2097168 | tf_op jit(solution)/shard_map/psum | solution.py:218
  842.0 11.9 %all-reduce.8 = (f32[1024]{0:T(1024)S(1)}, f32[1024]{0:T(1024)S(1)}) all-reduce(f32[1024]{0:T(1024)S(1)} %get-tuple-element.16, f32[1024]{0:T(1024)S(1)} %copy-done.44), channel_id=11, replica_groups=mesh['fsdp'=4,'ctx'=2,'tp'=4] {'fsdp'}, use_global_device_ids=true, to_apply=%region_32.33.clone | all-reduce | flops 2048 | bytes 16384
  856.7 19.6 %all-reduce.6 = (f32[64]{0:T(128)}, f32[64]{0:T(128)}, f32[4]{0:T(128)S(1)}, f32[]{:T(128)}) all-reduce(f32[64]{0:T(128)S(1)} %get-tuple-element.30, f32[64]{0:T(128)S(1)} %get-tuple-element.31, f32[4]{0:T(128)S(1)} %pad_maximum_fusion.9, f32[]{:T(128)} %fusion.75), channel_id=1, replica_groups=mesh['fsdp'=4,'ctx'=2,'tp'=4] {'fsdp','ctx'}, use_global_device_ids=true, to_apply=%region_39.40 | all-reduce | flops 133 | bytes 1064 | tf_op jit(solution)/shard_map/psum | solution.py:230
  886.4 68.8 %all-reduce.25.cloned.1.call-done = (f32[256,256]{1,0:T(8,128)}, f32[256,128]{1,0:T(8,128)}, f32[256,128]{1,0:T(8,128)}, f32[256,256]{1,0:T(8,128)}, f32[256,115...) async-done(((f32[256,256]{1,0:T(8,128)}, f32[256,128]{1,0:T(8,128)}, f32[256,128]{1,0:T(8,128)}, f32[256,256]{1,0:T(8,128)}, f32[256,1152]{1,0:T(8,128)}, ...) | async-done | bytes 4325392 | tf_op jit(solution)/shard_map/psum | solution.py:266
  (239 shorter events, 170.4 us)
Async XLA Ops:
  8.0 159.4 %all-reduce.17.cloned.1.call-start = ((), (), s32[]{:S(2)}) async-start(), calls=%async_computation.9 | async-start | bytes 4194304 | tf_op jit(solution)/shard_map/psum | solution.py:145
  10.6 55.5 %copy-start.48 = (f32[64]{0:T(128)}, f32[64]{0:T(128)S(1)}, u32[]{:S(2)}) copy-start(f32[64]{0:T(128)S(1)} %convert_element_type.138) | copy-start | bytes 772
  13.3 89.3 %copy-start.38 = (f32[512]{0:T(512)}, f32[512]{0:T(512)S(1)}, u32[]{:S(2)}) copy-start(f32[512]{0:T(512)S(1)} %fusion.73) | copy-start | bytes 6148
  26.6 76.0 %copy-start.32 = (f32[4,1,256]{2,1,0:T(1,128)}, f32[4,1,256]{2,1,0:T(1,128)S(1)}, u32[]{:S(2)}) copy-start(f32[4,1,256]{2,1,0:T(1,128)S(1)} %convert_element_type.169) | copy-start | bytes 12292
  40.7 23.9 %copy-start.3 = (bf16[1,512,1024]{2,1,0:T(8,128)(2,1)S(1)}, bf16[1,512,1024]{2,1,0:T(8,128)(2,1)}, u32[]{:S(2)}) copy-start(bf16[1,512,1024]{2,1,0:T(8,128)(2,1)} %param.15) | copy-start | bytes 3145732
  71.9 32.7 %copy-start.19 = (bf16[1024,128]{0,1:T(8,128)(2,1)}, bf16[1024,128]{0,1:T(8,128)(2,1)S(1)}, u32[]{:S(2)}) copy-start(bf16[1024,128]{0,1:T(8,128)(2,1)S(1)} %all_gather.37) | copy-start | bytes 786436
  116.7 55.0 %all-gather.8.cloned.1.call-start = ((), (), s32[]{:S(2)}) async-start(), calls=%async_computation.11 | async-start | bytes 2949120 | tf_op jit(solution)/shard_map/all_gather | solution.py:86
  117.3 100.9 %all-gather.6.cloned.1.call-start = ((), (), s32[]{:S(2)}) async-start(), calls=%async_computation.10 | async-start | bytes 2949120 | tf_op jit(solution)/shard_map/all_gather | solution.py:85
  117.9 150.9 %all-gather.10.cloned.1.call-start = ((), (), s32[]{:S(2)}) async-start(), calls=%async_computation.12 | async-start | bytes 2949120 | tf_op jit(solution)/shard_map/all_gather | solution.py:87
  118.5 212.3 %all-reduce.21.cloned.1.call-start = ((), (), s32[]{:S(2)}) async-start(), calls=%async_computation.14 | async-start | bytes 4194304 | tf_op jit(solution)/shard_map/psum | solution.py:166
  281.1 88.8 %all-reduce.19.cloned.1.call-start = ((), (), s32[]{:S(2)}) async-start(), calls=%async_computation.13 | async-start | bytes 2097152 | tf_op jit(solution)/shard_map/psum | solution.py:154
  285.7 116.7 %reduce-scatter.12.cloned.1.call-start = ((), (), s32[]{:S(2)}) async-start(), calls=%async_computation.16 | async-start | bytes 786432 | tf_op jit(solution)/shard_map/reduce_scatter | solution.py:197
  387.4 31.7 %reduce-scatter.10.cloned.1.call-start = ((), (), s32[]{:S(2)}) async-start(), calls=%async_computation.15 | async-start | bytes 786432 | tf_op jit(solution)/shard_map/reduce_scatter | solution.py:194
  396.7 56.8 %reduce-scatter.18.cloned.1.call-start = ((), (), s32[]{:S(2)}) async-start(), calls=%async_computation.20 | async-start | bytes 655360 | tf_op jit(solution)/shard_map/reduce_scatter | solution.py:248
  404.9 65.9 %reduce-scatter.20.cloned.1.call-start = ((), (), s32[]{:S(2)}) async-start(), calls=%async_computation.21 | async-start | bytes 1310720 | tf_op jit(solution)/shard_map/reduce_scatter | solution.py:249
  407.3 86.0 %reduce-scatter.16.cloned.1.call-start = ((), (), s32[]{:S(2)}) async-start(), calls=%async_computation.19 | async-start | bytes 655360 | tf_op jit(solution)/shard_map/reduce_scatter | solution.py:247
  426.4 94.8 %reduce-scatter.14.cloned.1.call-start = ((), (), s32[]{:S(2)}) async-start(), calls=%async_computation.18 | async-start | bytes 1310720 | tf_op jit(solution)/shard_map/reduce_scatter | solution.py:246
  432.7 174.6 %reduce-scatter.26.cloned.1.call-start = ((), (), s32[]{:S(2)}) async-start(), calls=%async_computation.24 | async-start | bytes 5898240 | tf_op jit(solution)/shard_map/reduce_scatter | solution.py:252
  438.0 257.6 %reduce-scatter.24.cloned.1.call-start = ((), (), s32[]{:S(2)}) async-start(), calls=%async_computation.23 | async-start | bytes 5898240 | tf_op jit(solution)/shard_map/reduce_scatter | solution.py:251
  443.7 340.0 %reduce-scatter.22.cloned.1.call-start = ((), (), s32[]{:S(2)}) async-start(), calls=%async_computation.22 | async-start | bytes 5898240 | tf_op jit(solution)/shard_map/reduce_scatter | solution.py:250
  449.2 389.5 %all-reduce.23.cloned.1.call-start = ((), (), s32[]{:S(2)}) async-start(), calls=%async_computation.17 | async-start | bytes 4194304 | tf_op jit(solution)/shard_map/psum | solution.py:218
  453.4 501.8 %all-reduce.25.cloned.1.call-start = ((), (), s32[]{:S(2)}) async-start(), calls=%async_computation.25 | async-start | bytes 8650752 | tf_op jit(solution)/shard_map/psum | solution.py:266
  783.7 58.3 %copy-start.44 = (f32[1024]{0:T(1024)S(1)}, f32[1024]{0:T(1024)}, u32[]{:S(2)}) copy-start(f32[1024]{0:T(1024)} %get-tuple-element.14) | copy-start | bytes 12292
  783.7 99.3 %copy-start.41 = (f32[512]{0:T(512)S(1)}, f32[512]{0:T(512)}, u32[]{:S(2)}) copy-start(f32[512]{0:T(512)} %copy-done.40) | copy-start | bytes 6148
  (51 other events, 222.8 us)
Sparse Core Ops, SparseCore 0:
  116.8 50.5 all-reduce.16
  281.2 49.5 all-reduce.20
  333.8 36.1 all-reduce.18
  387.5 14.9 reduce-scatter.11
  404.5 14.5 reduce-scatter.9
  421.3 21.6 reduce-scatter.17
  445.4 25.3 reduce-scatter.19
  473.1 20.2 reduce-scatter.15
  495.7 25.4 reduce-scatter.13
  523.4 83.8 reduce-scatter.25
  609.8 85.7 reduce-scatter.23
  697.9 85.7 reduce-scatter.21
  786.7 51.8 all-reduce.22
  841.6 113.5 all-reduce.24
Sparse Core Ops, SparseCore 1:
  118.8 49.1 all-gather.7
  169.5 48.6 all-gather.5
  219.7 49.0 all-gather.9
where the time goes:
time: 975 us; the launch traced here: 974 us
  waiting for transfers between devices  666 us (68%)
  blocking collectives  136 us (14%)
  matrix products  84.6 us (9%)
  other arithmetic  44.4 us (5%)
  local copies, waits for them, and re-layouts  22.6 us (2%)
  between operations  18.2 us (2%)
    reduce_scatter x1, waiting for transfers between devices, shards(): lax.psum_scatter(up_grad, 'fsdp', scatter_dimension=0, tiled=True)  88.2 us
    reduce_scatter x1, waiting for transfers between devices, shards(): lax.psum_scatter(gate_grad, 'fsdp', scatter_dimension=0, tiled=True)  88.1 us
    reduce_scatter x1, waiting for transfers between devices, shards(): lax.psum_scatter(down_grad, 'fsdp', scatter_dimension=1, tiled=True)  86.2 us
    psum x1, waiting for transfers between devices, shards(): lax.psum((query_share, key_share, value_share, output_share, gate_share,...  68.8 us
    all_gather x1, waiting for transfers between devices, shards(): lax.all_gather(down_weight, 'fsdp', axis=1, tiled=True)  45.7 us
    psum x1, waiting for transfers between devices, shards(): lax.psum((first_part, query_gain_part, key_gain_part), 'tp')  45.7 us
    psum x1, waiting for transfers between devices, shards(): normed_two_grad = lax.psum(second_part, 'tp')  44.9 us
    all_gather x1, waiting for transfers between devices, shards(): lax.all_gather(gate_weight, 'fsdp', axis=0, tiled=True)  41.6 us
  transfers between devices with their start and end apart: 17, of which 15 were waited for; matrix products, arithmetic and copies ran while one was open for 8% of the time, Pallas kernels for 0%

commit v1 on v0

v1 whole, which is shorter than its diff:
```python
import jax
import jax.numpy as jnp
from jax import lax
from jax.sharding import Mesh, PartitionSpec as P

HD = 64
epsilon = 1e-05
rope_base = 1000000.0
F32 = jnp.float32
BF16 = jnp.bfloat16
PLANE = ("ctx", "y", "core")


def product(left, right):
    return jnp.dot(left, right, preferred_element_type=F32)


def rows_product(left, right):
    return lax.dot_general(left, right, (((0,), (0,)), ((), ())), preferred_element_type=F32)


def cols_product(left, right):
    return lax.dot_general(left, right, (((1,), (1,)), ((), ())), preferred_element_type=F32)


def swap(value, axis):
    return lax.ppermute(value, axis, [(0, 1), (1, 0)])


def halve(value, index, axis):
    size = value.shape[axis] // 2
    return lax.dynamic_slice_in_dim(value, index * size, size, axis)


def in_order(mine, other, index, axis):
    first = jnp.where(index == 0, mine, other)
    second = jnp.where(index == 0, other, mine)
    return jnp.concatenate([first, second], axis)


def sum_scatter(parts):
    width = parts.shape[-1] // 2
    total = parts[0].astype(F32) + swap(parts[1], "core").astype(F32)
    low = total.astype(BF16)
    from_x = swap(low[1, :, :, :width], "ctx").astype(F32)
    from_y = swap(low[:, 1, :, width:], "y").astype(F32)
    left = total[0, :, :, :width] + from_x
    right = total[:, 0, :, width:] + from_y
    left = left[0] + swap(left[1].astype(BF16), "y").astype(F32)
    right = right[0] + swap(right[1].astype(BF16), "ctx").astype(F32)
    return jnp.concatenate([left, right], -1)


def gather_plane(block):
    width = block.shape[-1] // 2
    left, right = block[:, :width], block[:, width:]
    left = jnp.stack([left, swap(left, "ctx")])
    right = jnp.stack([right, swap(right, "y")])
    left = jnp.stack([left, swap(left, "y")], 1)
    right = jnp.stack([right, swap(right, "ctx")], 0)
    here = jnp.concatenate([left, right], -1)
    return jnp.stack([here, swap(here, "core")])


def sum_all(value):
    for axis in ("core", "y", "ctx"):
        value = value + swap(value, axis)
    size = lax.axis_size("fsdp")
    step = 1
    while step < size:
        value = value + lax.ppermute(value, "fsdp", [(i, i ^ step) for i in range(size)])
        step *= 2
    return value


def rotate(values, cosine, sine):
    half = values.shape[-1] // 2
    first = values[..., :half]
    second = values[..., half:]
    return jnp.concatenate([first * cosine - second * sine, second * cosine + first * sine], axis=-1)


def normalize(values, gain):
    inverse = lax.rsqrt(jnp.mean(values * values, axis=-1, keepdims=True) + epsilon)
    return values * inverse * gain


def shards(
    hidden_in,
    lengths,
    positions,
    query_weight,
    key_weight,
    value_weight,
    output_weight,
    gate_weight,
    up_weight,
    down_weight,
    attention_gain,
    feedforward_gain,
    query_gain,
    key_gain,
    cotangent,
):
    ctx, why, core = lax.axis_index("ctx"), lax.axis_index("y"), lax.axis_index("core")
    local, width = hidden_in.shape[1:]
    block = local // 4
    every = 2 * local
    length = lengths[0]

    attention_scale = attention_gain.astype(F32)[:, None]
    feedforward_scale = feedforward_gain.astype(F32)[:, None]
    qkv_own = jnp.concatenate(
        [halve(query_weight, ctx, 1), halve(key_weight, ctx, 1), halve(value_weight, ctx, 1)], 1
    )
    heads = query_weight.shape[1] // 2 // HD
    groups = key_weight.shape[1] // 2 // HD
    group = heads // groups
    wide = qkv_own.shape[1]
    qkv_own = (qkv_own.astype(F32) * attention_scale).astype(BF16)
    attn_own = jnp.concatenate([qkv_own, halve(output_weight, ctx, 0).T], 1)
    hidden = gate_weight.shape[1] // 2
    gu_own = jnp.concatenate([halve(gate_weight, ctx, 1), halve(up_weight, ctx, 1)], 1)
    gu_own = (gu_own.astype(F32) * feedforward_scale).astype(BF16)
    ff_own = jnp.concatenate([gu_own, halve(down_weight, ctx, 0).T], 1)
    attn_full = lax.all_gather(attn_own, "fsdp", axis=0, tiled=True)
    ff_own, attn_full = lax.optimization_barrier((ff_own, attn_full))
    ff_full = lax.all_gather(ff_own, "fsdp", axis=0, tiled=True)
    qkv_w, out_w = attn_full[:, :wide], attn_full[:, wide:]
    gate_w, up_w, down_w = ff_full[:, :hidden], ff_full[:, hidden : 2 * hidden], ff_full[:, 2 * hidden :]

    def relative(array):
        pieces = [
            lax.dynamic_slice_in_dim(array, (2 * (why ^ yy) + (core ^ kk)) * block, block)
            for kk in range(2)
            for yy in range(2)
        ]
        return jnp.concatenate(pieces)

    def both_halves(own):
        near, far = own[:local // 2], own[local // 2 :]
        other = swap(near, "ctx")
        return jnp.concatenate([near, other, far, swap(other, "core")])

    inputs = relative(hidden_in[0]).astype(F32)
    inverse = lax.rsqrt(jnp.mean(inputs * inputs, axis=-1, keepdims=True) + epsilon)
    unit = both_halves((inputs * inverse).astype(BF16))
    inputs, inverse = inputs[:block], inverse[:block]

    def slots_of(xx):
        steps = jnp.arange(block, dtype=jnp.int32)
        return [
            ((ctx ^ xx) * 4 + 2 * (why ^ yy) + (core ^ kk)) * block + steps for kk in range(2) for yy in range(2)
        ]

    near_slots, far_slots = slots_of(0), slots_of(1)
    slots = jnp.concatenate(near_slots[:2] + far_slots[:2] + near_slots[2:] + far_slots[2:])
    places = relative(positions[0])
    other_places = swap(places, "ctx")
    places = jnp.concatenate(
        [places[: local // 2], other_places[: local // 2], places[local // 2 :], other_places[local // 2 :]]
    )
    freqs = rope_base ** (-2.0 * jnp.arange(HD // 2, dtype=F32) / HD)
    angles = places.astype(F32)[:, None] * freqs[None, :]
    cosine, sine = jnp.cos(angles)[:, None, :], jnp.sin(angles)[:, None, :]
    allowed = (slots[None, :] <= slots[:, None]) & (slots[None, :] < length)
    valid = (slots[:block] < length).astype(F32)[:, None]
    upstream_rel = relative(cotangent[0])
    upstream = upstream_rel[:block].astype(F32) * valid
    branch_low = both_halves(upstream_rel)
    branch_low = jnp.where((slots < length)[:, None], branch_low, jnp.zeros_like(branch_low))

    qkv_raw = product(unit, qkv_w)
    scale = HD ** (-0.5)

    def shape_heads(query_lin, key_lin, query_scale, key_scale):
        query_rot = rotate(normalize(query_lin.reshape(every, heads, HD), query_scale), cosine, sine)
        key_rot = rotate(normalize(key_lin.reshape(every, groups, HD), key_scale), cosine, sine)
        return (query_rot, key_rot)

    (query_rot, key_rot), heads_pull = jax.vjp(
        shape_heads,
        qkv_raw[:, : heads * HD],
        qkv_raw[:, heads * HD : (heads + groups) * HD],
        query_gain.astype(F32),
        key_gain.astype(F32),
    )
    query_low = query_rot.astype(BF16).reshape(every, groups, group, HD)
    key_low = key_rot.astype(BF16)
    value_low = qkv_raw[:, (heads + groups) * HD :].astype(BF16).reshape(every, groups, HD)
    scores = jnp.einsum("qkgd,skd->kgqs", query_low, key_low, preferred_element_type=F32) * scale
    probs = jax.nn.softmax(jnp.where(allowed, scores, -1e30), axis=-1)
    probs_low = probs.astype(BF16)
    mixed = jnp.einsum("kgqs,skd->qkgd", probs_low, value_low, preferred_element_type=F32)
    mixed_low = mixed.reshape(every, heads * HD).astype(BF16)

    def split(array):
        return array.astype(BF16).reshape(2, 2, 2, block, width)

    attention_branch = sum_scatter(split(cols_product(mixed_low, out_w)))
    middle = inputs + attention_branch
    inverse_two = lax.rsqrt(jnp.mean(middle * middle, axis=-1, keepdims=True) + epsilon)
    unit_two_own = middle * inverse_two
    unit_two = gather_plane(unit_two_own.astype(BF16)).reshape(every, width)

    gate = product(unit_two, gate_w)
    upper = product(unit_two, up_w)
    sigmoid = 1.0 / (1.0 + jnp.exp(-gate))
    silu = gate * sigmoid
    activated = (silu * upper).astype(BF16)
    activated_grad = product(branch_low, down_w)
    gate_low = (activated_grad * upper * (sigmoid * (1.0 + gate * (1.0 - sigmoid)))).astype(BF16)
    upper_low = (activated_grad * silu).astype(BF16)
    second = sum_scatter(split(cols_product(gate_low, gate_w) + cols_product(upper_low, up_w)))
    ff_grad = jnp.concatenate(
        [
            rows_product(unit_two, gate_low).astype(BF16),
            rows_product(unit_two, upper_low).astype(BF16),
            rows_product(branch_low, activated).astype(BF16),
        ],
        1,
    )
    ff_share = lax.psum_scatter(ff_grad, "fsdp", scatter_dimension=0, tiled=True)
    middle_grad = upstream + inverse_two * (
        second - unit_two_own * jnp.mean(second * unit_two_own, axis=-1, keepdims=True)
    )
    feedforward_gain_part = jnp.sum(second * unit_two_own, axis=0)
    attention_low = gather_plane(middle_grad.astype(BF16)).reshape(every, width)
    feedforward_branch = sum_scatter(split(cols_product(activated, down_w)))
    output = ((middle + feedforward_branch) * valid).astype(BF16)
    block_rows = lax.all_gather(output, ("y", "core"), axis=0, tiled=True)

    output_grad = rows_product(attention_low, mixed_low)
    mixed_grad = product(attention_low, out_w).astype(BF16).reshape(every, groups, group, HD)
    value_grad = jnp.einsum("kgqs,qkgd->skd", probs_low, mixed_grad, preferred_element_type=F32)
    probs_grad = jnp.einsum("qkgd,skd->kgqs", mixed_grad, value_low, preferred_element_type=F32)
    score_grad = (probs * (probs_grad - jnp.sum(probs * probs_grad, axis=-1, keepdims=True))).astype(BF16)
    query_rot_grad = jnp.einsum("kgqs,skd->qkgd", score_grad, key_low, preferred_element_type=F32) * scale
    key_rot_grad = jnp.einsum("kgqs,qkgd->skd", score_grad, query_low, preferred_element_type=F32) * scale
    query_back, key_back, query_gain_part, key_gain_part = heads_pull(
        (query_rot_grad.reshape(every, heads, HD), key_rot_grad)
    )
    qkv_grad = jnp.concatenate([query_back, key_back, value_grad.reshape(every, groups * HD)], 1).astype(BF16)
    first = sum_scatter(split(cols_product(qkv_grad, qkv_w)))
    attn_grad = jnp.concatenate([rows_product(unit, qkv_grad), output_grad], 1).astype(BF16)
    attn_share = lax.psum_scatter(attn_grad, "fsdp", scatter_dimension=0, tiled=True)
    unit_own = inputs * inverse
    input_grad = middle_grad + inverse * (first - unit_own * jnp.mean(first * unit_own, axis=-1, keepdims=True))
    attention_gain_part = jnp.sum(first * unit_own, axis=0)
    input_rows = lax.all_gather(input_grad.astype(BF16), ("y", "core"), axis=0, tiled=True).astype(F32)

    squares = jnp.stack(
        [jnp.sum(item * item * valid) for item in (inputs, attention_branch, middle, feedforward_branch)]
    )
    small = jnp.concatenate(
        [
            attention_gain_part,
            feedforward_gain_part,
            query_gain_part,
            key_gain_part,
            squares,
            jnp.sum(valid)[None],
            jnp.zeros((123,), F32),
        ]
    )
    small = sum_all(small.reshape(-1, 128)).reshape(-1)
    own_gain = attention_gain.shape[0]
    shard = lax.axis_index("fsdp") * own_gain
    attention_share = lax.dynamic_slice_in_dim(small, shard, own_gain) / attention_scale[:, 0]
    feedforward_share = lax.dynamic_slice_in_dim(small, width + shard, own_gain) / feedforward_scale[:, 0]
    rest = small[2 * width :]
    query_gain_total, key_gain_total = rest[:HD], rest[HD : 2 * HD]
    stats = jnp.sqrt(rest[2 * HD : 2 * HD + 4] / (rest[2 * HD + 4] * width))

    attn_other = swap(attn_share, "ctx")
    ff_other = swap(ff_share, "ctx")

    def whole(mine, other, start, size, axis, gain):
        mine = mine[:, start : start + size].astype(F32)
        other = other[:, start : start + size].astype(F32)
        if gain is not None:
            mine, other = mine * gain, other * gain
        if axis == 0:
            mine, other = mine.T, other.T
        return in_order(mine, other, ctx, axis)

    query_cols, key_cols = heads * HD, groups * HD
    return (
        block_rows[None],
        input_rows[None],
        whole(attn_share, attn_other, 0, query_cols, 1, attention_scale),
        whole(attn_share, attn_other, query_cols, key_cols, 1, attention_scale),
        whole(attn_share, attn_other, query_cols + key_cols, key_cols, 1, attention_scale),
        whole(attn_share, attn_other, wide, query_cols, 0, None),
        whole(ff_share, ff_other, 0, hidden, 1, feedforward_scale),
        whole(ff_share, ff_other, hidden, hidden, 1, feedforward_scale),
        whole(ff_share, ff_other, 2 * hidden, hidden, 0, None),
        attention_share,
        feedforward_share,
        query_gain_total,
        key_gain_total,
        stats,
    )


def solution(mesh):
    fsdp, ctx, tp = (mesh.shape[axis] for axis in ("fsdp", "ctx", "tp"))
    assert ctx == 2 and tp == 4
    plane = Mesh(mesh.devices.reshape(fsdp, 2, 2, 2), ("fsdp", "ctx", "y", "core"))
    tp = ("y", "core")
    in_specs = (
        P("fsdp", "ctx", None),
        P("fsdp"),
        P("fsdp", "ctx"),
        P("fsdp", tp),
        P("fsdp", tp),
        P("fsdp", tp),
        P(tp, "fsdp"),
        P("fsdp", tp),
        P("fsdp", tp),
        P(tp, "fsdp"),
        P("fsdp"),
        P("fsdp"),
        P(),
        P(),
        P("fsdp", "ctx", None),
    )
    out_specs = (
        P("fsdp", "ctx", None),
        P("fsdp", "ctx", None),
        P("fsdp", tp),
        P("fsdp", tp),
        P("fsdp", tp),
        P(tp, "fsdp"),
        P("fsdp", tp),
        P("fsdp", tp),
        P(tp, "fsdp"),
        P("fsdp"),
        P("fsdp"),
        P(),
        P(),
        P(),
    )
    return jax.shard_map(shards, mesh=plane, in_specs=in_specs, out_specs=out_specs, check_vma=False)
```

time: 975 us -> 353 us (0.36)
  waiting for transfers between devices: 666 us -> 150 us
  blocking collectives: 136 us -> 20.6 us
  starting transfers between devices: 1.19 us -> 42.5 us
  matrix products: 84.6 us -> 52.4 us
    reduce_scatter x9 -> x2, waiting for transfers between devices: 344 us -> 28.3 us  [the longest x1 28.3 us: shards(): lax.psum_scatter(ff_grad, 'fsdp', scatter_dimension=0, tiled=True)]
    psum x5 -> x0, waiting for transfers between devices: 234 us -> none  [the longest x1 68.8 us: shards(): lax.psum((query_share, key_share, value_share, output_share, gate_share,...]
    ppermute x0 -> x42, waiting for transfers between devices: none -> 85 us  [the longest x40 78 us: swap(): return lax.ppermute(value, axis, [(0, 1), (1, 0)])]
    all_gather x8 -> x1, blocking collectives: 92.6 us -> 20.6 us  [shards(): attn_full = lax.all_gather(attn_own, 'fsdp', axis=0, tiled=True)]
    all_gather x3, waiting for transfers between devices: 87.3 us -> 37.1 us  [the longest x1 22.8 us: shards(): ff_full = lax.all_gather(ff_own, 'fsdp', axis=0, tiled=True)]
    ppermute x0 -> x42, starting transfers between devices: none -> 41.8 us  [the longest x40 41 us: swap(): return lax.ppermute(value, axis, [(0, 1), (1, 0)])]
    psum x3 -> x0, blocking collectives: 31.9 us -> none  [the longest x1 19.6 us: shards(): lax.psum((squares, jnp.sum(valid), query_gain_sum, key_gain_sum), ('fsdp'...]
    dot_general x7 -> x5, matrix products: 24.5 us -> 8.08 us  [rows_product(): lax.dot_general(left, right, (((0,), (0,)), ((), ())), preferred_element_...]
  transfers between devices with their start and end apart: 17 -> 47, of which waited for: 15 -> 35; matrix products, arithmetic and copies ran while one was open for 8% -> 21% of each run, Pallas kernels for 0% -> 0%
where the time goes in v1:
time: 353 us; the launch traced here: 349 us
  waiting for transfers between devices  150 us (42%)
  matrix products  52.4 us (15%)
  starting transfers between devices  42.5 us (12%)
  other arithmetic  37.6 us (11%)
  local copies, waits for them, and re-layouts  28.1 us (8%)
  blocking collectives  20.6 us (6%)
  between operations  17.3 us (5%)
    ppermute x40, waiting for transfers between devices, swap(): return lax.ppermute(value, axis, [(0, 1), (1, 0)])  78 us
    ppermute x40, starting transfers between devices, swap(): return lax.ppermute(value, axis, [(0, 1), (1, 0)])  41 us
    reduce_scatter x1, waiting for transfers between devices, shards(): lax.psum_scatter(ff_grad, 'fsdp', scatter_dimension=0, tiled=True)  28.3 us
    all_gather x1, waiting for transfers between devices, shards(): ff_full = lax.all_gather(ff_own, 'fsdp', axis=0, tiled=True)  22.8 us
    all_gather x1, blocking collectives, shards(): attn_full = lax.all_gather(attn_own, 'fsdp', axis=0, tiled=True)  20.6 us
    unnamed x186, local copies, waits for them, and re-layouts  15.3 us
    all_gather x1, waiting for transfers between devices, shards(): lax.all_gather(input_grad.astype(BF16), ('y', 'core'), axis=0, tiled=True)  14.3 us
    dot_general x1, matrix products, shards(): jnp.einsum('qkgd,skd->kgqs', mixed_grad, value_low, preferred_element_typ...  14.2 us
  transfers between devices with their start and end apart: 47, of which 35 were waited for; matrix products, arithmetic and copies ran while one was open for 21% of the time, Pallas kernels for 0%

profile of v1, /device:TPU:0, one launch (start us, length us, event | category | flops | bytes accessed | tf_op | source)
XLA Modules:
  0.0 348.9 jit_solution(1623804461639181437)
XLA Ops:
  9.4 3.0 collective-permute-start.2
  16.8 20.6 %all_gather.12 = bf16[1024,384]{1,0:T(8,128)(2,1)} all-gather(bf16[256,384]{1,0:T(8,128)(2,1)S(1)} %pad_maximum_fusion.26), channel_id=1, replica_groups=mesh['fsdp'=4,'ctx'=2,'y'=2,'core'=2] {'fsdp'}, dimensions={0}, use_global_device_ids=true | all-gather | bytes 983040 | tf_op jit(solution)/shard_map/all_gather | solution.py:126
  53.7 2.8 fusion.14
  68.3 5.1 %collective-permute-done.4 = bf16[2,128,512]{2,1,0:T(8,128)(2,1)S(1)} collective-permute-done((bf16[2,128,512]{2,1,0:T(8,128)(2,1)S(1)}, bf16[2,128,512]{2,1,0:T(8,128)(2,1)S(1)}, u32[]{:S(2)}, u32[]{:S(2)}) %collective-permute-start.4) | collective-permute-done | bytes 262176 | tf_op jit(solution)/shard_map/ppermute | solution.py:27
  91.1 4.6 %collective-permute-done.11 = bf16[2,128,512]{2,1,0:T(8,128)(2,1)S(1)} collective-permute-done((bf16[2,128,512]{2,1,0:T(8,128)(2,1)S(1)}, bf16[2,128,512]{2,1,0:T(8,128)(2,1)S(1)}, u32[]{:S(2)}, u32[]{:S(2)}) %collective-permute-start.11) | collective-permute-done | bytes 262176 | tf_op jit(solution)/shard_map/ppermute | solution.py:27
  96.0 8.7 %collective-permute-done.18 = bf16[256,1024]{1,0:T(8,128)(2,1)S(1)} collective-permute-done((bf16[256,1024]{1,0:T(8,128)(2,1)S(1)}, bf16[256,1024]{1,0:T(8,128)(2,1)S(1)}, u32[]{:S(2)}, u32[]{:S(2)}) %collective-permute-start.18) | collective-permute-done | bytes 524320 | tf_op jit(solution)/shard_map/ppermute | solution.py:27
  109.5 22.8 %all-gather.4.cloned.1.call-done = bf16[1024,1728]{1,0:T(8,128)(2,1)} async-done(((bf16[256,1728]{1,0:T(8,128)(2,1)}), bf16[1024,1728]{1,0:T(8,128)(2,1)}) %all-gather.4.cloned.1.call-update) | async-done | bytes 3538960 | tf_op jit(solution)/shard_map/all_gather | solution.py:128
  132.3 4.2 %fusion.26 = f32[1024,576]{0,1:T(8,128)S(1)} fusion(bf16[1024,1024]{1,0:T(8,128)(2,1)} %bitcast.353, bf16[1024,1728]{1,0:T(8,128)(2,1)} %all-gather.4.cloned.1.call-done), kind=kOutput, calls=%fused_computation.62 | convolution fusion | flops 1207959552 | bytes 5767168 | tf_op jit(solution)/shard_map/dot_general | solution.py:15
  138.1 3.0 multiply_convert_fusion
  153.9 4.4 %collective-permute-done.14 = bf16[2,128,512]{2,1,0:T(8,128)(2,1)S(1)} collective-permute-done((bf16[2,128,512]{2,1,0:T(8,128)(2,1)S(1)}, bf16[2,128,512]{2,1,0:T(8,128)(2,1)S(1)}, u32[]{:S(2)}, u32[]{:S(2)}) %collective-permute-start.14) | collective-permute-done | bytes 262176 | tf_op jit(solution)/shard_map/ppermute | solution.py:27
  168.0 2.8 collective-permute-done.24
  190.2 2.9 collective-permute-done.29
  195.9 14.2 %fusion = (f32[2,1024]{1,0:T(2,128)S(1)}, f32[1024,1024,2]{1,0,2:T(8,128)S(1)}) fusion(f32[2,1024]{1,0:T(2,128)S(1)} %copy-done.42, f32[2,1024]{1,0:T(2,128)S(1)} %copy-done.40, f32[1024,1024,2]{1,0,2:T(8,128)} %copy-done.2, pred[1024,1024]{0,1:T(8,128)(4,1)S(1)} %compare_and_fusion, bf16[1024,2,64]{0,2,1:T(8,128)(2,1)S(1)} %bitcast.366, ...), kind=kOutput, calls=%fused_computation.3 | convolution fusion | flops 281016320 | bytes 18243584 | tf_op jit(solution)/shard_map/qkgd,skd->kgqs/dot_general | solution.py:236
  210.1 2.8 fusion.6
  217.4 2.9 fusion.35
  240.5 5.6 %collective-permute-done.31 = bf16[2,128,512]{2,1,0:T(8,128)(2,1)S(1)} collective-permute-done((bf16[2,128,512]{2,1,0:T(8,128)(2,1)S(1)}, bf16[2,128,512]{2,1,0:T(8,128)(2,1)S(1)}, u32[]{:S(2)}, u32[]{:S(2)}) %collective-permute-start.31) | collective-permute-done | bytes 262176 | tf_op jit(solution)/shard_map/ppermute | solution.py:27
  254.1 3.3 concatenate.155
  262.8 3.1 collective-permute-done.39
  266.0 3.9 %collective-permute-done.40 = f32[18,128]{1,0:T(8,128)S(1)} collective-permute-done((f32[18,128]{1,0:T(8,128)S(1)}, f32[18,128]{1,0:T(8,128)S(1)}, u32[]{:S(2)}, u32[]{:S(2)}) %collective-permute-start.40) | collective-permute-done | bytes 9248 | tf_op jit(solution)/shard_map/ppermute | solution.py:71
  271.7 3.1 collective-permute-done.41
  278.6 4.9 %collective-permute-done.35 = bf16[256,384]{0,1:T(8,128)(2,1)S(1)} collective-permute-done((bf16[256,384]{0,1:T(8,128)(2,1)}, bf16[256,384]{0,1:T(8,128)(2,1)S(1)}, u32[]{:S(2)}, u32[]{:S(2)}) %collective-permute-start.35) | collective-permute-done | bytes 196640 | tf_op jit(solution)/shard_map/ppermute | solution.py:27
  285.1 28.3 %reduce-scatter.5.cloned.1.call-done = bf16[256,1728]{0,1:T(8,128)(2,1)} async-done(((bf16[1024,1728]{0,1:T(8,128)(2,1)}), bf16[256,1728]{0,1:T(8,128)(2,1)}) %reduce-scatter.5.cloned.1.call-update) | async-done | bytes 884752 | tf_op jit(solution)/shard_map/reduce_scatter | solution.py:223
  318.1 14.3 %all-gather.8.cloned.1.call-done = bf16[512,1024]{1,0:T(8,128)(2,1)} async-done(((bf16[128,1024]{1,0:T(8,128)(2,1)}), bf16[512,1024]{1,0:T(8,128)(2,1)}) %all-gather.8.cloned.1.call-update) | async-done | bytes 1048592 | tf_op jit(solution)/shard_map/all_gather | solution.py:250
  332.4 2.8 bitcast_convert_fusion
  (427 shorter events, 157.5 us)
Async XLA Ops:
  7.2 125.1 %all-gather.4.cloned.1.call-start = ((), (), s32[]{:S(2)}) async-start(), calls=%async_computation.2 | async-start | bytes 4587520 | tf_op jit(solution)/shard_map/all_gather | solution.py:128
  9.4 32.6 %collective-permute-start.2 = (s32[512]{0:T(512)S(1)}, s32[512]{0:T(512)S(1)}, u32[]{:S(2)}, u32[]{:S(2)}) collective-permute-start(s32[512]{0:T(512)S(1)} %pad_add_fusion.2), channel_id=1, source_target_pairs={{0,4},{4,0},{1,5},{5,1},{2,6},{6,2},{3,7},{7,3},{8,12},{12,8},{9,1... | collective-permute-start | bytes 6152 | tf_op jit(solution)/shard_map/ppermute | solution.py:27
  15.3 26.7 %collective-permute-start = (bf16[256,1024]{1,0:T(8,128)(2,1)}, bf16[256,1024]{1,0:T(8,128)(2,1)}, u32[]{:S(2)}, u32[]{:S(2)}) collective-permute-start(bf16[256,1024]{1,0:T(8,128)(2,1)} %get-tuple-element.88), channel_id=1, source_target_pairs={{0,4},{4,0},{1,5},{5,1},{2,6},{6,2},{3,7},{7,3},{8,12},{12,8},{9,1... | collective-permute-start | bytes 1572872 | tf_op jit(solution)/shard_map/ppermute | solution.py:27
  60.1 202.8 %all-gather.6.cloned.1.call-start = ((), (), s32[]{:S(2)}) async-start(), calls=%async_computation.3 | async-start | bytes 1310720 | tf_op jit(solution)/shard_map/all_gather | solution.py:231
  65.0 8.4 %collective-permute-start.4 = (bf16[2,128,512]{2,1,0:T(8,128)(2,1)S(1)}, bf16[2,128,512]{2,1,0:T(8,128)(2,1)S(1)}, u32[]{:S(2)}, u32[]{:S(2)}) collective-permute-start(bf16[2,128,512]{2,1,0:T(8,128)(2,1)S(1)} %slice_bitcast_fusion.23), channel_id=1, source_target_pairs={{0,4},{4,0},{1,5},{5,1},{2,6},{6,2},{3,7},{7,3},{8,12},{12,8},{9,1... | collective-permute-start | bytes 786440 | tf_op jit(solution)/shard_map/ppermute | solution.py:27
  66.5 8.1 %collective-permute-start.6 = (bf16[2,128,512]{2,1,0:T(8,128)(2,1)S(1)}, bf16[2,128,512]{2,1,0:T(8,128)(2,1)S(1)}, u32[]{:S(2)}, u32[]{:S(2)}) collective-permute-start(bf16[2,128,512]{2,1,0:T(8,128)(2,1)S(1)} %slice_bitcast_fusion.21), channel_id=1, source_target_pairs={{0,2},{2,0},{1,3},{3,1},{4,6},{6,4},{5,7},{7,5},{8,10},{10,8},{9,1... | collective-permute-start | bytes 786440 | tf_op jit(solution)/shard_map/ppermute | solution.py:27
  86.4 9.3 %collective-permute-start.11 = (bf16[2,128,512]{2,1,0:T(8,128)(2,1)S(1)}, bf16[2,128,512]{2,1,0:T(8,128)(2,1)S(1)}, u32[]{:S(2)}, u32[]{:S(2)}) collective-permute-start(bf16[2,128,512]{2,1,0:T(8,128)(2,1)S(1)} %get-tuple-element.129), channel_id=1, source_target_pairs={{0,4},{4,0},{1,5},{5,1},{2,6},{6,2},{3,7},{7,3},{8,12},{12,8},{9,1... | collective-permute-start | bytes 786440 | tf_op jit(solution)/shard_map/ppermute | solution.py:27
  89.3 6.4 %collective-permute-start.9 = (bf16[2,128,512]{2,1,0:T(8,128)(2,1)S(1)}, bf16[2,128,512]{2,1,0:T(8,128)(2,1)S(1)}, u32[]{:S(2)}, u32[]{:S(2)}) collective-permute-start(bf16[2,128,512]{2,1,0:T(8,128)(2,1)S(1)} %get-tuple-element.123), channel_id=1, source_target_pairs={{0,2},{2,0},{1,3},{3,1},{4,6},{6,4},{5,7},{7,5},{8,10},{10,8},{9,1... | collective-permute-start | bytes 786440 | tf_op jit(solution)/shard_map/ppermute | solution.py:27
  89.7 15.0 %collective-permute-start.18 = (bf16[256,1024]{1,0:T(8,128)(2,1)S(1)}, bf16[256,1024]{1,0:T(8,128)(2,1)S(1)}, u32[]{:S(2)}, u32[]{:S(2)}) collective-permute-start(bf16[256,1024]{1,0:T(8,128)(2,1)S(1)} %pad_maximum_fusion.11), channel_id=1, source_target_pairs={{0,4},{4,0},{1,5},{5,1},{2,6},{6,2},{3,7},{7,3},{8,12},{12,8},{9,1... | collective-permute-start | bytes 1572872 | tf_op jit(solution)/shard_map/ppermute | solution.py:27
  95.9 10.7 %collective-permute-start.12 = (bf16[2,2,128,1024]{3,2,1,0:T(8,128)(2,1)S(1)}, bf16[2,2,128,1024]{3,2,1,0:T(8,128)(2,1)S(1)}, u32[]{:S(2)}, u32[]{:S(2)}) collective-permute-start(bf16[2,2,128,1024]{3,2,1,0:T(8,128)(2,1)S(1)} %get-tuple-element.86), channel_id=1, source_target_pairs={{0,1},{1,0},{2,3},{3,2},{4,5},{5,4},{6,7},{7,6},{8,9},{9,8},{10,11... | collective-permute-start | bytes 3145736 | tf_op jit(solution)/shard_map/ppermute | solution.py:27
  149.1 9.2 %collective-permute-start.14 = (bf16[2,128,512]{2,1,0:T(8,128)(2,1)S(1)}, bf16[2,128,512]{2,1,0:T(8,128)(2,1)S(1)}, u32[]{:S(2)}, u32[]{:S(2)}) collective-permute-start(bf16[2,128,512]{2,1,0:T(8,128)(2,1)S(1)} %slice_bitcast_fusion.19), channel_id=1, source_target_pairs={{0,4},{4,0},{1,5},{5,1},{2,6},{6,2},{3,7},{7,3},{8,12},{12,8},{9,1... | collective-permute-start | bytes 786440 | tf_op jit(solution)/shard_map/ppermute | solution.py:27
  150.7 9.3 %collective-permute-start.16 = (bf16[2,128,512]{2,1,0:T(8,128)(2,1)S(1)}, bf16[2,128,512]{2,1,0:T(8,128)(2,1)S(1)}, u32[]{:S(2)}, u32[]{:S(2)}) collective-permute-start(bf16[2,128,512]{2,1,0:T(8,128)(2,1)S(1)} %slice_bitcast_fusion.17), channel_id=1, source_target_pairs={{0,2},{2,0},{1,3},{3,1},{4,6},{6,4},{5,7},{7,5},{8,10},{10,8},{9,1... | collective-permute-start | bytes 786440 | tf_op jit(solution)/shard_map/ppermute | solution.py:27
  152.7 11.3 %collective-permute-start.21 = (bf16[2,128,512]{2,1,0:T(8,128)(2,1)S(1)}, bf16[2,128,512]{2,1,0:T(8,128)(2,1)S(1)}, u32[]{:S(2)}, u32[]{:S(2)}) collective-permute-start(bf16[2,128,512]{2,1,0:T(8,128)(2,1)S(1)} %slice_bitcast_fusion.15), channel_id=1, source_target_pairs={{0,4},{4,0},{1,5},{5,1},{2,6},{6,2},{3,7},{7,3},{8,12},{12,8},{9,1... | collective-permute-start | bytes 786440 | tf_op jit(solution)/shard_map/ppermute | solution.py:27
  153.3 12.2 %collective-permute-start.23 = (bf16[2,128,512]{2,1,0:T(8,128)(2,1)S(1)}, bf16[2,128,512]{2,1,0:T(8,128)(2,1)S(1)}, u32[]{:S(2)}, u32[]{:S(2)}) collective-permute-start(bf16[2,128,512]{2,1,0:T(8,128)(2,1)S(1)} %slice_bitcast_fusion.13), channel_id=1, source_target_pairs={{0,2},{2,0},{1,3},{3,1},{4,6},{6,4},{5,7},{7,5},{8,10},{10,8},{9,1... | collective-permute-start | bytes 786440 | tf_op jit(solution)/shard_map/ppermute | solution.py:27
  160.2 12.1 %collective-permute-start.17 = (bf16[128,512]{1,0:T(8,128)(2,1)S(1)}, bf16[128,512]{1,0:T(8,128)(2,1)S(1)}, u32[]{:S(2)}, u32[]{:S(2)}) collective-permute-start(bf16[128,512]{1,0:T(8,128)(2,1)S(1)} %fusion.91), channel_id=1, source_target_pairs={{0,4},{4,0},{1,5},{5,1},{2,6},{6,2},{3,7},{7,3},{8,12},{12,8},{9,1... | collective-permute-start | bytes 393224 | tf_op jit(solution)/shard_map/ppermute | solution.py:27
  160.8 11.6 %collective-permute-start.15 = (bf16[128,512]{1,0:T(8,128)(2,1)S(1)}, bf16[128,512]{1,0:T(8,128)(2,1)S(1)}, u32[]{:S(2)}, u32[]{:S(2)}) collective-permute-start(bf16[128,512]{1,0:T(8,128)(2,1)S(1)} %fusion.90), channel_id=1, source_target_pairs={{0,2},{2,0},{1,3},{3,1},{4,6},{6,4},{5,7},{7,5},{8,10},{10,8},{9,1... | collective-permute-start | bytes 393224 | tf_op jit(solution)/shard_map/ppermute | solution.py:27
  179.7 6.7 %collective-permute-start.28 = (bf16[2,128,512]{2,1,0:T(8,128)(2,1)S(1)}, bf16[2,128,512]{2,1,0:T(8,128)(2,1)S(1)}, u32[]{:S(2)}, u32[]{:S(2)}) collective-permute-start(bf16[2,128,512]{2,1,0:T(8,128)(2,1)S(1)} %get-tuple-element.121), channel_id=1, source_target_pairs={{0,4},{4,0},{1,5},{5,1},{2,6},{6,2},{3,7},{7,3},{8,12},{12,8},{9,1... | collective-permute-start | bytes 786440 | tf_op jit(solution)/shard_map/ppermute | solution.py:27
  182.0 6.4 %collective-permute-start.26 = (bf16[2,128,512]{2,1,0:T(8,128)(2,1)S(1)}, bf16[2,128,512]{2,1,0:T(8,128)(2,1)S(1)}, u32[]{:S(2)}, u32[]{:S(2)}) collective-permute-start(bf16[2,128,512]{2,1,0:T(8,128)(2,1)S(1)} %get-tuple-element.115), channel_id=1, source_target_pairs={{0,2},{2,0},{1,3},{3,1},{4,6},{6,4},{5,7},{7,5},{8,10},{10,8},{9,1... | collective-permute-start | bytes 786440 | tf_op jit(solution)/shard_map/ppermute | solution.py:27
  190.1 87.1 %reduce-scatter.3.cloned.1.call-start = ((), (), s32[]{:S(2)}) async-start(), calls=%async_computation.5 | async-start | bytes 983040 | tf_op jit(solution)/shard_map/reduce_scatter | solution.py:246
  223.8 89.6 %reduce-scatter.5.cloned.1.call-start = ((), (), s32[]{:S(2)}) async-start(), calls=%async_computation.6 | async-start | bytes 4423680 | tf_op jit(solution)/shard_map/reduce_scatter | solution.py:223
  232.5 99.8 %all-gather.8.cloned.1.call-start = ((), (), s32[]{:S(2)}) async-start(), calls=%async_computation.4 | async-start | bytes 1310720 | tf_op jit(solution)/shard_map/all_gather | solution.py:250
  237.7 8.4 %collective-permute-start.31 = (bf16[2,128,512]{2,1,0:T(8,128)(2,1)S(1)}, bf16[2,128,512]{2,1,0:T(8,128)(2,1)S(1)}, u32[]{:S(2)}, u32[]{:S(2)}) collective-permute-start(bf16[2,128,512]{2,1,0:T(8,128)(2,1)S(1)} %slice_bitcast_fusion.11), channel_id=1, source_target_pairs={{0,4},{4,0},{1,5},{5,1},{2,6},{6,2},{3,7},{7,3},{8,12},{12,8},{9,1... | collective-permute-start | bytes 786440 | tf_op jit(solution)/shard_map/ppermute | solution.py:27
  238.3 8.1 %collective-permute-start.33 = (bf16[2,128,512]{2,1,0:T(8,128)(2,1)S(1)}, bf16[2,128,512]{2,1,0:T(8,128)(2,1)S(1)}, u32[]{:S(2)}, u32[]{:S(2)}) collective-permute-start(bf16[2,128,512]{2,1,0:T(8,128)(2,1)S(1)} %slice_bitcast_fusion.9), channel_id=1, source_target_pairs={{0,2},{2,0},{1,3},{3,1},{4,6},{6,4},{5,7},{7,5},{8,10},{10,8},{9,1... | collective-permute-start | bytes 786440 | tf_op jit(solution)/shard_map/ppermute | solution.py:27
  313.3 21.8 %collective-permute-start.36 = (bf16[256,1728]{0,1:T(8,128)(2,1)}, bf16[256,1728]{0,1:T(8,128)(2,1)}, u32[]{:S(2)}, u32[]{:S(2)}) collective-permute-start(bf16[256,1728]{0,1:T(8,128)(2,1)} %reduce-scatter.5.cloned.1.call-done), channel_id=1, source_target_pairs={{0,4},{4,0},{1,5},{5,1},{2,6},{6,2},{3,7},{7,3},{8,12},{12,8},{9,1... | collective-permute-start | bytes 2654216 | tf_op jit(solution)/shard_map/ppermute | solution.py:27
  (109 other events, 723.6 us)
Sparse Core Ops, SparseCore 0:
  60.2 72.0 all-gather.3
  190.2 14.7 all-gather.5
  223.9 21.0 reduce-scatter.2
  247.2 66.0 reduce-scatter.4
  315.3 16.9 all-gather.7

commit v2 on v1

v2 whole, which is shorter than its diff:
```python
import jax
import jax.numpy as jnp
from jax import lax
from jax.experimental import pallas as pl
from jax.experimental.pallas import tpu as pltpu
from jax.sharding import Mesh, PartitionSpec as P

HD = 64
epsilon = 1e-05
rope_base = 1000000.0
F32 = jnp.float32
BF16 = jnp.bfloat16
PLANE = ("ctx", "y", "core")


def swap(value, axis):
    return lax.ppermute(value, axis, [(0, 1), (1, 0)])


def halve(value, index, axis):
    size = value.shape[axis] // 2
    return lax.dynamic_slice_in_dim(value, index * size, size, axis)


def in_order(mine, other, index, axis):
    first = jnp.where(index == 0, mine, other)
    second = jnp.where(index == 0, other, mine)
    return jnp.concatenate([first, second], axis)


def sum_scatter(near, far):
    block, width = near.shape[0] // 4, near.shape[1] // 2
    total = near.astype(F32) + swap(far, "core").astype(F32)
    total = total.reshape(2, 2, block, -1)
    low = total.astype(BF16)
    from_x = swap(low[1, :, :, :width], "ctx").astype(F32)
    from_y = swap(low[:, 1, :, width:], "y").astype(F32)
    left = total[0, :, :, :width] + from_x
    right = total[:, 0, :, width:] + from_y
    left = left[0] + swap(left[1].astype(BF16), "y").astype(F32)
    right = right[0] + swap(right[1].astype(BF16), "ctx").astype(F32)
    return jnp.concatenate([left, right], -1)


def gather_plane(block):
    width = block.shape[-1] // 2
    left, right = block[:, :width], block[:, width:]
    left = jnp.stack([left, swap(left, "ctx")])
    right = jnp.stack([right, swap(right, "y")])
    left = jnp.stack([left, swap(left, "y")], 1)
    right = jnp.stack([right, swap(right, "ctx")], 0)
    near = jnp.concatenate([left, right], -1).reshape(-1, 2 * width)
    return near, swap(near, "core")


def gather_shards(own):
    size = lax.axis_size("fsdp")
    parts = [own]
    for step in range(1, size):
        parts.append(lax.ppermute(own, "fsdp", [(i, i ^ step) for i in range(size)]))
    return parts


def region(flag, work, *args):
    shapes = jax.eval_shape(work, *args)
    return lax.cond(flag, work, lambda *_: jax.tree.map(lambda x: jnp.zeros(x.shape, x.dtype), shapes), *args)


def gather_rows(block, why, core):
    pair = jnp.stack([block, swap(block, "y")])
    four = jnp.concatenate([pair, swap(pair, "core")])
    pieces = [lax.dynamic_slice_in_dim(four, 2 * (core ^ (i % 2)) + (why ^ (i // 2)), 1)[0] for i in range(4)]
    return jnp.concatenate(pieces)


def sum_all(value):
    for axis in ("core", "y", "ctx"):
        value = value + swap(value, axis)
    size = lax.axis_size("fsdp")
    step = 1
    while step < size:
        value = value + lax.ppermute(value, "fsdp", [(i, i ^ step) for i in range(size)])
        step *= 2
    return value


def lanes(shape):
    return lax.broadcasted_iota(jnp.int32, shape, len(shape) - 1)


def nt(left, right):
    return lax.dot_general(left, right, (((1,), (1,)), ((), ())), preferred_element_type=F32)


def tn(left, right):
    return lax.dot_general(left, right, (((0,), (0,)), ((), ())), preferred_element_type=F32)


def nn(left, right):
    return lax.dot_general(left, right, (((1,), (0,)), ((), ())), preferred_element_type=F32)


def half_sums(values, low):
    first = jnp.sum(jnp.where(low, values, 0.0), axis=-1, keepdims=True)
    second = jnp.sum(jnp.where(low, 0.0, values), axis=-1, keepdims=True)
    return first, second


def turned(values):
    return jnp.where(lanes(values.shape) % HD < HD // 2, pltpu.roll(values, 96, 1), pltpu.roll(values, 32, 1))


def rows_of(own, kk, xx, yy, block):
    return pl.multiple_of((own ^ (xx * 4 + yy * 2 + kk)) * block, block)


def attention_forward(
    index, h0, h1, h2, h3, cosine, sine, query_gain, key_gain, *rest
):
    *parts, w, gains, part_low, part_high, unit, query, key, value, raw, mixed, mixed_rel, inverse = rest
    own, length = index[0], index[1]
    if len(parts) > 2:
        rows = w.shape[0] // len(parts)
        for at, part in enumerate(parts):
            to = pl.multiple_of((index[2] ^ at) * rows, rows)
            w[pl.ds(to, rows), :] = part[:rows, :]
            gains[:, pl.ds(to, rows)] = part[rows : rows + 16, :rows].astype(F32)[:8]
    else:
        w[...] = parts[0][...]
        gains[...] = parts[1][...]
    gain = gains[0:1, :]
    pair = h0.shape[0]
    block = pair // 2
    low = lanes((pair, 2 * HD)) < HD
    for at, h in enumerate((h0, h1, h2, h3)):
        kk, xx = divmod(at, 2)
        here = slice(at * pair, (at + 1) * pair)
        x = h[...].astype(F32)
        r = lax.rsqrt(jnp.mean(x * x, axis=-1, keepdims=True) + epsilon)
        u = (x * r * gain).astype(BF16)
        unit[here, :] = u
        lin = nn(u, w[:, : 4 * HD])
        raw[here, :] = lin
        q, kv = lin[:, : 2 * HD], lin[:, 2 * HD :]
        one, two = half_sums(q * q, low)
        r = jnp.where(low, lax.rsqrt(one / HD + epsilon), lax.rsqrt(two / HD + epsilon))
        y = q * r * query_gain[...]
        c, s = cosine[here, :], sine[here, :]
        q = (y * c + turned(y) * s).astype(BF16).astype(F32) * HD**-0.5
        one, _ = half_sums(kv * kv, low)
        y = kv * lax.rsqrt(one / HD + epsilon) * key_gain[...]
        kv = jnp.where(low, y * c + turned(y) * s, kv)
        other = pltpu.roll(kv, HD, 1)
        k, v = jnp.where(low, kv, other), jnp.where(low, other, kv)
        for yy in range(2):
            to = rows_of(own, kk, xx, yy, block)
            some = slice(yy * block, (yy + 1) * block)
            query[pl.ds(to, block), :] = q[some].astype(BF16)
            key[pl.ds(to, block), :] = k[some].astype(BF16)
            value[pl.ds(to, block), :] = v[some].astype(BF16)
    for at in range(4):
        here = slice(at * pair, (at + 1) * pair)
        n = (at + 1) * pair
        q = query[here, :]
        q = jnp.concatenate([jnp.where(low, q, jnp.zeros_like(q)), jnp.where(low, jnp.zeros_like(q), q)])
        e = masked_exp(nt(q, key[:n, :]), at, pair, length)
        total = 1.0 / jnp.sum(e, axis=-1, keepdims=True)
        o = nn((e * total).astype(BF16), value[:n, :])
        mixed[here, :] = jnp.where(low, o[:pair], o[pair:])
        inverse[here, :] = jnp.where(low, total[:pair], total[pair:])
    for at in range(4):
        kk, xx = divmod(at, 2)
        pieces = [mixed[pl.ds(rows_of(own, kk, xx, yy, block), block), :] for yy in range(2)]
        m = jnp.concatenate(pieces).astype(BF16)
        mixed_rel[at * pair : (at + 1) * pair, :] = m
        part = nt(m, w[:, 4 * HD :]).astype(BF16)
        to = part_high if kk else part_low
        to[xx * pair : (xx + 1) * pair, :] = part


def masked_exp(scores, at, pair, length):
    n = scores.shape[1]
    columns = lax.broadcasted_iota(jnp.int32, scores.shape, 1)
    rows = lax.broadcasted_iota(jnp.int32, scores.shape, 0) % pair + at * pair
    return jnp.where((columns <= rows) & (columns < length), jnp.exp(scores), 0.0)


def attention_backward(
    index, a_low, a_high, w, query, key, value, raw, mixed, inverse, cosine, sine, query_gain, key_gain,
    first_low, first_high, back, gains, down, dq, dk, dv,
):
    own, length = index[0], index[1]
    pair = a_low.shape[0] // 2
    block = pair // 2
    low = lanes((pair, 2 * HD)) < HD
    for at in range(4):
        kk, xx = divmod(at, 2)
        a = a_high if kk else a_low
        m = nn(a[xx * pair : (xx + 1) * pair, :], w[:, 4 * HD :]).astype(BF16)
        for yy in range(2):
            down[pl.ds(rows_of(own, kk, xx, yy, block), block), :] = m[yy * block : (yy + 1) * block]
    dk[...] = jnp.zeros_like(dk)
    dv[...] = jnp.zeros_like(dv)
    for at in range(4):
        here = slice(at * pair, (at + 1) * pair)
        n = (at + 1) * pair
        q, m = query[here, :], down[here, :]
        zero = jnp.zeros_like(q)
        q = jnp.concatenate([jnp.where(low, q, zero), jnp.where(low, zero, q)])
        one, two = half_sums(m.astype(F32) * mixed[here, :], low)
        drop = jnp.concatenate([one, two])
        m = jnp.concatenate([jnp.where(low, m, zero), jnp.where(low, zero, m)])
        total = jnp.concatenate([inverse[here, 0:1], inverse[here, HD : HD + 1]])
        p = masked_exp(nt(q, key[:n, :]), at, pair, length) * total
        g = (p * (nt(m, value[:n, :]) - drop)).astype(BF16)
        dv[:n, :] += tn(p.astype(BF16), m)
        dk[:n, :] += tn(g, q)
        o = nn(g, key[:n, :])
        dq[here, :] = jnp.where(low, o[:pair], o[pair:]) * HD**-0.5
    query_sum = jnp.zeros((1, 2 * HD), F32)
    key_sum = jnp.zeros((1, 2 * HD), F32)
    for at in range(4):
        kk, xx = divmod(at, 2)
        here = slice(at * pair, (at + 1) * pair)
        spots = [pl.ds(rows_of(own, kk, xx, yy, block), block) for yy in range(2)]
        c, s = cosine[here, :], sine[here, :]
        x, kv = raw[here, : 2 * HD], raw[here, 2 * HD :]
        one, two = half_sums(x * x, low)
        r = jnp.where(low, lax.rsqrt(one / HD + epsilon), lax.rsqrt(two / HD + epsilon))
        z = x * r
        y = jnp.concatenate([dq[spot, :] for spot in spots])
        y = y * c - turned(y) * s
        query_sum += jnp.sum(y * z, axis=0, keepdims=True)
        y = y * query_gain[...]
        one, two = half_sums(y * z, low)
        x = r * (y - z * jnp.where(low, one / HD, two / HD))
        one, _ = half_sums(kv * kv, low)
        r = lax.rsqrt(one / HD + epsilon)
        z = kv * r
        y = jnp.concatenate([dk[spot, :] for spot in spots])
        y = y + pltpu.roll(y, HD, 1)
        y = y * c - turned(y) * s
        key_sum += jnp.sum(y * z, axis=0, keepdims=True)
        y = y * key_gain[...]
        one, _ = half_sums(y * z, low)
        v = jnp.concatenate([dv[spot, :] for spot in spots])
        kv = jnp.where(low, r * (y - z * (one / HD)), v + pltpu.roll(v, HD, 1))
        lin = jnp.concatenate([x, kv], axis=1).astype(BF16)
        back[here, :] = lin
        part = nt(lin, w[:, : 4 * HD]).astype(BF16)
        to = first_high if kk else first_low
        to[xx * pair : (xx + 1) * pair, :] = part
    gains[0:1, :] = query_sum
    gains[1:2, :] = key_sum


def feed_forward(
    index, x_low, x_high, b0, b1, b2, b3, f, second_low, second_high, gate_up, activated, branch, unit
):
    own, length = index[0], index[1]
    pair = b0.shape[0]
    block, four = pair // 2, 2 * pair
    main = gate_up.shape[1] // 2 // 128 * 128
    both = 2 * main
    wide = both + 128
    low = lanes((four, 128)) < HD
    rows = lax.broadcasted_iota(jnp.int32, (pair, 1), 0)
    for kk, (x, bs, to) in enumerate(((x_low, (b0, b1), second_low), (x_high, (b2, b3), second_high))):
        here = slice(kk * four, (kk + 1) * four)
        x = x[...]
        unit[here, :] = x
        for xx, b in enumerate(bs):
            starts = jnp.where(rows < block, own ^ (xx * 4 + kk), own ^ (xx * 4 + 2 + kk)) * block
            b = b[...]
            b = jnp.where(starts + rows % block < length, b, jnp.zeros_like(b))
            branch[kk * four + xx * pair : kk * four + (xx + 1) * pair, :] = b
        gu = nn(x, f[:, :wide])
        back = nn(branch[here, :], f[:, wide:])
        tail = gu[:, both:]
        gate = jnp.concatenate([gu[:, :main], tail], 1)
        upper = jnp.concatenate([gu[:, main:both], pltpu.roll(tail, HD, 1)], 1)
        sigmoid = 1.0 / (1.0 + jnp.exp(-gate))
        silu = gate * sigmoid
        act = silu * upper
        gate_back = back * upper * (sigmoid + silu * (1.0 - sigmoid))
        upper_back = back * silu
        activated[here, :main] = act[:, :main].astype(BF16)
        activated[here, main:] = jnp.where(low, act[:, main:], 0.0).astype(BF16)
        mix = jnp.where(low, gate_back[:, main:], pltpu.roll(upper_back[:, main:], HD, 1))
        gu = jnp.concatenate([gate_back[:, :main], upper_back[:, :main], mix], 1).astype(BF16)
        gate_up[here, :] = gu
        to[...] = nt(gu, f[:, :wide]).astype(BF16)


def pack_attention(index, query, key, value, output, gains, out):
    rows = query.shape[0]
    wide = query.shape[1] // 2
    for half in range(2):

        @pl.when(index[3] == half)
        def _():
            out[:rows, :wide] = query[:, half * wide : (half + 1) * wide]
            low = lanes((rows, 2 * HD)) < HD
            k, v = key[...].astype(F32), value[...].astype(F32)
            if half:
                kv = jnp.where(low, pltpu.roll(k, HD, 1), v)
            else:
                kv = jnp.where(low, k, pltpu.roll(v, HD, 1))
            out[:rows, wide : wide + 2 * HD] = kv.astype(BF16)
            out[:rows, wide + 2 * HD :] = output[half * wide : (half + 1) * wide, :].astype(F32).T.astype(BF16)

    out[rows:, :rows] = gains[...]


def unpack_attention(index, mine, other, query, key, value, output):
    wide = query.shape[1] // 2
    low = lanes((mine.shape[0], 2 * HD)) < HD
    for half in range(2):

        @pl.when(index[3] == half)
        def _():
            first, second = (other, mine) if half else (mine, other)
            for at, part in enumerate((first, second)):
                query[:, at * wide : (at + 1) * wide] = part[:, :wide].astype(F32)
                output[at * wide : (at + 1) * wide, :] = part[:, wide + 2 * HD :].astype(F32).T
            one = first[:, wide : wide + 2 * HD].astype(F32)
            two = second[:, wide : wide + 2 * HD].astype(F32)
            key[...] = jnp.where(low, one, pltpu.roll(two, HD, 1))
            value[...] = jnp.where(low, pltpu.roll(one, HD, 1), two)


def unpack_feed_forward(index, mine, other, gate, upper, down):
    rows, hidden = mine.shape[0], gate.shape[1] // 2
    main = hidden // 128 * 128
    both, wide = 2 * main, 2 * hidden
    low = lanes((rows, 128)) < HD
    for half in range(2):

        @pl.when(index[3] == half)
        def _():
            first, second = (other, mine) if half else (mine, other)
            for at, to in enumerate((gate, upper)):
                to[:, :main] = first[:, at * main : (at + 1) * main].astype(F32)
                one = first[:, both : both + 128].astype(F32)
                two = second[:, both : both + 128].astype(F32)
                if at:
                    one = pltpu.roll(one, HD, 1)
                else:
                    two = pltpu.roll(two, HD, 1)
                end = second[:, at * main : (at + 1) * main].astype(F32)
                end = pltpu.roll(jnp.concatenate([end, jnp.zeros((rows, 128), F32)], 1), HD, 1)
                to[:, main : main + 128] = jnp.where(low, one, end[:, :128])
                to[:, main + 128 : 2 * main] = end[:, 128:main]
                to[:, 2 * main :] = jnp.where(low, end[:, main:], two)
            for at, part in enumerate((first, second)):
                turned = part[:, wide:].astype(F32).T
                down[at * hidden : (at + 1) * hidden, :] = turned[:hidden]


def call(kernel, outs, args, scratch=()):
    vmem = pl.BlockSpec(memory_space=pltpu.VMEM)
    return pl.pallas_call(
        kernel,
        out_shape=[jax.ShapeDtypeStruct(shape, kind) for shape, kind in outs],
        in_specs=[pl.BlockSpec(memory_space=pltpu.SMEM) if arg.dtype == jnp.int32 else vmem for arg in args],
        out_specs=[vmem] * len(outs),
        scratch_shapes=[pltpu.VMEM(shape, kind) for shape, kind in scratch],
        compiler_params=pltpu.CompilerParams(vmem_limit_bytes=48 * 2**20),
        cost_estimate=pl.CostEstimate(flops=1000, bytes_accessed=1000, transcendentals=0),
    )(*args)


def down_product(activated, f, part_low, part_high):
    wide = f.shape[1] - activated.shape[1]
    half = part_low.shape[0]
    part_low[...] = nt(activated[:half, :], f[:, wide:]).astype(BF16)
    part_high[...] = nt(activated[half:, :], f[:, wide:]).astype(BF16)


def feed_forward_weights(unit, branch, gate_up, activated, out):
    wide = gate_up.shape[1]
    step = out.shape[0] // 2
    for row in range(0, out.shape[0], step):
        here = slice(row, row + step)
        out[here, :wide] = tn(unit[:, here], gate_up[...]).astype(BF16)
        out[here, wide:] = tn(branch[:, here], activated[...]).astype(BF16)


def attention_weights(unit, back, a_low, a_high, mixed_rel, w, gains, out, gain_out):
    wide = back.shape[1]
    half = a_low.shape[0]
    step = 256
    for row in range(0, out.shape[0], step):
        here = slice(row, row + step)
        grad = tn(unit[:, here], back[...])
        out[here, :wide] = grad.astype(BF16)
        grad = jnp.sum(grad * w[here, :wide].astype(F32), axis=1, keepdims=True)
        gain_out[:, here] = jnp.broadcast_to(grad, (step, 128)).T[:8] / gains[0:1, here]
        o = tn(a_low[:, here], mixed_rel[:half, :]) + tn(a_high[:, here], mixed_rel[half:, :])
        out[here, wide:] = o.astype(BF16)


def shards(
    hidden_in,
    lengths,
    positions,
    query_weight,
    key_weight,
    value_weight,
    output_weight,
    gate_weight,
    up_weight,
    down_weight,
    attention_gain,
    feedforward_gain,
    query_gain,
    key_gain,
    cotangent,
):
    ctx, why, core = lax.axis_index("ctx"), lax.axis_index("y"), lax.axis_index("core")
    local, width = hidden_in.shape[1:]
    block = local // 4
    every = 2 * local
    length = lengths[0]

    heads = query_weight.shape[1] // 2 // HD
    groups = key_weight.shape[1] // 2 // HD
    group = heads // groups
    wide = (heads + 2 * groups) * HD
    rows = query_weight.shape[0]
    gains = jnp.pad(jnp.stack([attention_gain, feedforward_gain]), ((0, 14), (0, 0)))
    own = ctx * 4 + why * 2 + core
    shard = lax.axis_index("fsdp")
    index = jnp.stack([own, length, shard, ctx]).astype(jnp.int32)
    (attn_parts,) = call(
        pack_attention,
        [((rows + 16, wide + heads * HD), BF16)],
        (index, query_weight, key_weight, value_weight, output_weight, gains),
    )
    size = lax.axis_size("fsdp")
    if size > 4:
        attn_parts = lax.all_gather(attn_parts, "fsdp")
        gains = attn_parts[:, rows : rows + 8, :rows].astype(F32).transpose(1, 0, 2).reshape(8, -1)
        attn_parts = [attn_parts[:, :rows].reshape(-1, wide + heads * HD), gains]
    else:
        attn_parts = gather_shards(attn_parts)
    hidden = gate_weight.shape[1] // 2
    main = hidden // 128 * 128
    assert hidden - main == HD and 2 * heads * HD == 256 and groups == 1
    gate_own, up_own = halve(gate_weight, ctx, 1), halve(up_weight, ctx, 1)
    gu_own = jnp.concatenate([gate_own[:, :main], up_own[:, :main], gate_own[:, main:], up_own[:, main:]], 1)
    down_own = jnp.concatenate([halve(down_weight, ctx, 0).T, jnp.zeros((rows, HD), BF16)], 1)

    def relative(array, kk):
        pieces = [
            lax.dynamic_slice_in_dim(array, (2 * (why ^ yy) + (core ^ kk)) * block, block) for yy in range(2)
        ]
        return jnp.concatenate(pieces)

    def both_halves(array):
        near = relative(array, 0)
        other = swap(near, "ctx")
        return near, other, relative(array, 1), swap(other, "core")

    flag = length > 0

    def prepare(hidden_in, positions):
        hidden_rel = both_halves(hidden_in[0])
        places = jnp.stack([relative(positions[0], kk) for kk in range(2)])
        places = jnp.stack([places, swap(places, "ctx")], 1).reshape(-1)
        freqs = rope_base ** (-2.0 * jnp.arange(HD // 2, dtype=F32) / HD)
        angles = places.astype(F32)[:, None] * jnp.tile(freqs, 4)[None, :]
        cosine = jnp.cos(angles)
        sine = jnp.sin(angles) * jnp.where(jnp.arange(2 * HD) % HD < HD // 2, -1.0, 1.0)[None, :]
        return hidden_rel, cosine, sine

    hidden_rel, cosine, sine = region(flag, prepare, hidden_in, positions)
    attn_parts, hidden_rel = lax.optimization_barrier((attn_parts, hidden_rel))
    cotangent_rel, _ = lax.optimization_barrier((relative(cotangent[0], 0), hidden_rel[1]))
    cotangent_x = swap(cotangent_rel, "ctx")
    ff_own, _ = lax.optimization_barrier((jnp.concatenate([gu_own, down_own], 1), hidden_rel[1]))
    ff_full = lax.all_gather(ff_own, "fsdp", axis=0, tiled=True)
    inputs = hidden_rel[0][:block].astype(F32)
    inverse = lax.rsqrt(jnp.mean(inputs * inputs, axis=-1, keepdims=True) + epsilon)

    valid = (own * block + jnp.arange(block, dtype=jnp.int32) < length).astype(F32)[:, None]
    upstream = cotangent_rel[:block].astype(F32) * valid

    query_row = jnp.tile(query_gain.astype(F32), 2)[None]
    key_row = jnp.concatenate([key_gain.astype(F32), jnp.ones((HD,), F32)])[None]
    lane = 2 * HD
    attn_full, gains, near, far, unit, query, key, value, raw, mixed, mixed_rel, total = call(
        attention_forward,
        [((width, wide + 2 * HD), BF16), ((8, width), F32)]
        + [((every // 2, width), BF16)] * 2
        + [((every, width), BF16)]
        + [((every, lane), BF16)] * 3
        + [((every, 2 * lane), F32), ((every, lane), F32), ((every, lane), BF16), ((every, lane), F32)],
        (index, *hidden_rel, cosine, sine, query_row, key_row, *attn_parts),
    )
    attention_scale, feedforward_scale = gains[0:1], gains[1:2]
    kept = (attn_full, query, key, value, raw, mixed, total, cosine, sine, query_row, key_row)
    near, cotangent_x = lax.optimization_barrier((near, cotangent_x))

    def middle_of(near, far, inputs, feedforward_scale, cotangent_x, cotangent_in):
        attention_branch = sum_scatter(near, far)
        middle = inputs + attention_branch
        inverse_two = lax.rsqrt(jnp.mean(middle * middle, axis=-1, keepdims=True) + epsilon)
        unit_two_own = middle * inverse_two
        unit_near, unit_far = gather_plane((unit_two_own * feedforward_scale).astype(BF16))
        cotangent_far = relative(cotangent_in[0], 1), swap(cotangent_x, "core")
        return attention_branch, middle, inverse_two, unit_near, unit_far, cotangent_far

    attention_branch, middle, inverse_two, unit_near, unit_far, cotangent_far = region(
        flag, middle_of, near, far, inputs, feedforward_scale, cotangent_x, cotangent
    )
    unit_two_own = middle * inverse_two

    tail = main + 2 * HD
    near, far, gate_up, activated, branch_low, unit_two = call(
        feed_forward,
        [((every // 2, width), BF16)] * 2
        + [((every, 2 * hidden), BF16), ((every, tail), BF16), ((every, width), BF16), ((every, width), BF16)],
        (index, unit_near, unit_far, cotangent_rel, cotangent_x, *cotangent_far, ff_full),
    )
    (ff_grad,) = call(
        feed_forward_weights, [((width, 2 * hidden + tail), BF16)], (unit_two, branch_low, gate_up, activated)
    )
    ff_grad, near = lax.optimization_barrier((ff_grad, near))
    ff_share = lax.psum_scatter(ff_grad, "fsdp", scatter_dimension=0, tiled=True)

    def turn(near, far, activated, ff_full, unit_two_own, inverse_two, upstream, middle, kept, unit, mixed_rel):
        second = sum_scatter(near, far)
        feedforward_gain_part = jnp.sum(second * unit_two_own, axis=0)
        second = second * feedforward_scale
        middle_grad = upstream + inverse_two * (
            second - unit_two_own * jnp.mean(second * unit_two_own, axis=-1, keepdims=True)
        )
        attention_near, attention_far = gather_plane(middle_grad.astype(BF16))
        near, far = call(down_product, [((every // 2, width), BF16)] * 2, (activated, ff_full))
        feedforward_branch = sum_scatter(near, far)
        output = ((middle + feedforward_branch) * valid).astype(BF16)
        block_rows = gather_rows(output, why, core)
        near, far, back, gain_sums = call(
            attention_backward,
            [((every // 2, width), BF16)] * 2 + [((every, 2 * lane), BF16), ((8, lane), F32)],
            (index, attention_near, attention_far, *kept),
            [((every, lane), BF16)] + [((every, lane), F32)] * 3,
        )
        attn_grad, attention_gain_part = call(
            attention_weights,
            [((width, 3 * lane), BF16), ((8, width), F32)],
            (unit, back, attention_near, attention_far, mixed_rel, kept[0], gains),
        )
        feedforward_gain_part = jnp.stack([feedforward_gain_part, attention_gain_part[0]])
        return near, far, attn_grad, gain_sums, block_rows, feedforward_branch, middle_grad, feedforward_gain_part

    near, far, attn_grad, gain_sums, block_rows, feedforward_branch, middle_grad, gain_parts = region(
        flag,
        turn,
        near,
        far,
        activated,
        ff_full,
        unit_two_own,
        inverse_two,
        upstream,
        middle,
        kept,
        unit,
        mixed_rel,
    )
    attn_share = lax.psum_scatter(attn_grad, "fsdp", scatter_dimension=0, tiled=True)
    ff_share, near = lax.optimization_barrier((ff_share, near))
    ff_other = swap(ff_share, "ctx")

    def sums(near, far, inputs, gain_parts, gain_sums, branches):
        squares = jnp.stack([jnp.sum(item * item * valid) for item in (inputs, *branches)])
        small = jnp.concatenate(
            [
                gain_parts.reshape(-1),
                gain_sums[0, :HD] + gain_sums[0, HD:],
                gain_sums[1, :HD],
                squares,
                jnp.sum(valid)[None],
                jnp.zeros((123,), F32),
            ]
        )
        return sum_scatter(near, far), sum_all(small.reshape(-1, 128)).reshape(-1)

    first, small = region(
        flag, sums, near, far, inputs, gain_parts, gain_sums, (attention_branch, middle, feedforward_branch)
    )
    first, attn_share, ff_other = lax.optimization_barrier((first, attn_share, ff_other))
    attn_other = swap(attn_share, "ctx")

    def finish(first, middle_grad, inputs, inverse, attention_scale, index, ff_share, ff_other):
        unit_own = inputs * inverse
        first = first * attention_scale
        input_grad = middle_grad + inverse * (
            first - unit_own * jnp.mean(first * unit_own, axis=-1, keepdims=True)
        )
        ff_grads = call(
            unpack_feed_forward,
            [((rows, 2 * hidden), F32)] * 2 + [((2 * hidden, rows), F32)],
            (index, ff_share, ff_other),
        )
        return gather_rows(input_grad.astype(BF16), why, core).astype(F32), ff_grads

    input_rows, ff_grads = region(
        flag, finish, first, middle_grad, inputs, inverse, attention_scale, index, ff_share, ff_other
    )
    attn_other, input_rows = lax.optimization_barrier((attn_other, input_rows))
    attn_grads = call(
        unpack_attention,
        [((rows, 2 * heads * HD), F32)] + [((rows, 2 * groups * HD), F32)] * 2 + [((2 * heads * HD, rows), F32)],
        (index, attn_share, attn_other),
    )
    own_gain = attention_gain.shape[0]
    shard = shard * own_gain
    feedforward_share = lax.dynamic_slice_in_dim(small, shard, own_gain)
    attention_share = lax.dynamic_slice_in_dim(small, width + shard, own_gain)
    rest = small[2 * width :]
    query_gain_total, key_gain_total = rest[:HD], rest[HD : 2 * HD]
    stats = jnp.sqrt(rest[2 * HD : 2 * HD + 4] / (rest[2 * HD + 4] * width))

    return (
        block_rows[None],
        input_rows[None],
        *attn_grads,
        *ff_grads,
        attention_share,
        feedforward_share,
        query_gain_total,
        key_gain_total,
        stats,
    )


def solution(mesh):
    fsdp, ctx, tp = (mesh.shape[axis] for axis in ("fsdp", "ctx", "tp"))
    assert ctx == 2 and tp == 4
    plane = Mesh(mesh.devices.reshape(fsdp, 2, 2, 2), ("fsdp", "ctx", "y", "core"))
    tp = ("y", "core")
    in_specs = (
        P("fsdp", "ctx", None),
        P("fsdp"),
        P("fsdp", "ctx"),
        P("fsdp", tp),
        P("fsdp", tp),
        P("fsdp", tp),
        P(tp, "fsdp"),
        P("fsdp", tp),
        P("fsdp", tp),
        P(tp, "fsdp"),
        P("fsdp"),
        P("fsdp"),
        P(),
        P(),
        P("fsdp", "ctx", None),
    )
    out_specs = (
        P("fsdp", "ctx", None),
        P("fsdp", "ctx", None),
        P("fsdp", tp),
        P("fsdp", tp),
        P("fsdp", tp),
        P(tp, "fsdp"),
        P("fsdp", tp),
        P("fsdp", tp),
        P(tp, "fsdp"),
        P("fsdp"),
        P("fsdp"),
        P(),
        P(),
        P(),
    )
    return jax.shard_map(shards, mesh=plane, in_specs=in_specs, out_specs=out_specs, check_vma=False)
```

time: 353 us -> 286 us (0.81)
  matrix products: 52.4 us -> 0 us
  Pallas kernels: 0 us -> 51.7 us
  waiting for transfers between devices: 150 us -> 115 us
  blocking collectives: 20.6 us -> 0 us
  other arithmetic: 37.6 us -> 20.6 us
  loops' own time: 0 us -> 11.4 us
  local copies, waits for them, and re-layouts: 28.1 us -> 21.7 us
  starting transfers between devices: 42.5 us -> 47.7 us
    dot_general x21 -> x0, matrix products: 52.4 us -> none  [the longest x1 14.2 us: shards(): jnp.einsum('qkgd,skd->kgqs', mixed_grad, value_low, preferred_element_typ...]
    pallas_call x0 -> x9, Pallas kernels: none -> 51.7 us  [call(): pl.pallas_call(kernel, out_shape=[jax.ShapeDtypeStruct(shape, kind) for s...]
    reduce_scatter x1, waiting for transfers between devices: 28.3 us -> 0.02 us  [shards(): lax.psum_scatter(ff_grad, 'fsdp', scatter_dimension=0, tiled=True)]
    all_gather x1 -> x0, blocking collectives: 20.6 us -> none  [shards(): attn_full = lax.all_gather(attn_own, 'fsdp', axis=0, tiled=True)]
    all_gather x2 -> x0, waiting for transfers between devices: 14.3 us -> none  [the longest x1 14.3 us: shards(): lax.all_gather(input_grad.astype(BF16), ('y', 'core'), axis=0, tiled=True)]
    unnamed x186 -> x29, local copies, waits for them, and re-layouts: 15.3 us -> 3.74 us
    another operation x0 -> x5, loops' own time: none -> 11.4 us  [region(): lax.cond(flag, work, lambda *_: jax.tree.map(lambda x: jnp.zeros(x.shape,...]
    ppermute x40 -> x44, waiting for transfers between devices: 78 us -> 87.9 us  [swap(): return lax.ppermute(value, axis, [(0, 1), (1, 0)])]
  transfers between devices with their start and end apart: 47 -> 52, of which waited for: 35 -> 33; matrix products, arithmetic and copies ran while one was open for 21% -> 12% of each run, Pallas kernels for 0% -> 10%
where the time goes in v2:
time: 286 us; the launch traced here: 283 us
  waiting for transfers between devices  115 us (40%)
  Pallas kernels  51.7 us (18%)
  starting transfers between devices  47.7 us (17%)
  local copies, waits for them, and re-layouts  21.7 us (8%)
  other arithmetic  20.6 us (7%)
  between operations  15.5 us (5%)
  loops' own time  11.4 us (4%)
    ppermute x44, waiting for transfers between devices, swap(): return lax.ppermute(value, axis, [(0, 1), (1, 0)])  87.9 us
    pallas_call x9, Pallas kernels, call(): pl.pallas_call(kernel, out_shape=[jax.ShapeDtypeStruct(shape, kind) for s...  51.7 us
    ppermute x44, starting transfers between devices, swap(): return lax.ppermute(value, axis, [(0, 1), (1, 0)])  40.9 us
    all_gather x1, waiting for transfers between devices, shards(): ff_full = lax.all_gather(ff_own, 'fsdp', axis=0, tiled=True)  19.2 us
    another operation x5, loops' own time, region(): lax.cond(flag, work, lambda *_: jax.tree.map(lambda x: jnp.zeros(x.shape,...  11.4 us
    ppermute x2, waiting for transfers between devices, sum_all(): lax.ppermute(value, 'fsdp', [(i, i ^ step) for i in range(size)])  7.32 us
    ppermute x3, starting transfers between devices, gather_shards(): lax.ppermute(own, 'fsdp', [(i, i ^ step) for i in range(size)])  5.76 us
  transfers between devices with their start and end apart: 52, of which 33 were waited for; matrix products, arithmetic and copies ran while one was open for 12% of the time, Pallas kernels for 10%

profile of v2, /device:TPU:0, one launch (start us, length us, event | category | flops | bytes accessed | tf_op | source)
XLA Modules:
  0.0 283.1 jit_solution(2532350707941234642)
XLA Ops:
  13.5 5.1 %collective-permute-start.45 = (bf16[272,384]{1,0:T(8,128)(2,1)S(1)}, bf16[272,384]{1,0:T(8,128)(2,1)S(1)}, u32[]{:S(2)}, u32[]{:S(2)}) collective-permute-start(bf16[272,384]{1,0:T(8,128)(2,1)S(1)} %shard_map.256.rest_0_), channel_id=1, source_target_pairs={{0,24},{8,16},{16,8},{24,0},{1,25},{9,17},{17,9},{25,1},{2,26},{10... | collective-permute-start | bytes 626696 | tf_op jit(solution)/shard_map/ppermute | solution.py:60
  19.5 17.9 %conditional.5 = (bf16[256,1024]{1,0:T(8,128)(2,1)}, bf16[256,1024]{1,0:T(8,128)(2,1)}, bf16[256,1024]{1,0:T(8,128)(2,1)S(1)}, bf16[256,1024]{1,0:T(8,128)(2,1)}...) conditional(s32[]{:T(128)} %convert_element_type.170, () %tuple.68, (s32[]{:T(128)}, s32[]{:T(128)}, ...), branch_computations={%region_0.1_spmd, %region_1.2_spmd} | conditional | flops 2363448 | bytes 9500412 | solution.py:66
  23.8 11.3 %collective-permute-done = bf16[256,1024]{1,0:T(8,128)(2,1)} collective-permute-done((bf16[256,1024]{1,0:T(8,128)(2,1)}, bf16[256,1024]{1,0:T(8,128)(2,1)}, u32[]{:S(2)}, u32[]{:S(2)}) %collective-permute-start) | collective-permute-done | bytes 524320 | tf_op jit(solution)/shard_map/cond/branch_1_fun/ppermute | solution.py:17
  45.4 8.2 %shard_map.257 = (bf16[1024,384]{1,0:T(8,128)(2,1)}, f32[8,1024]{1,0:T(8,128)S(1)}, bf16[512,1024]{1,0:T(8,128)(2,1)S(1)}, bf16[512,1024]{1,0:T(8,128)(2,1)S(1)}...) custom-call(s32[4]{0:T(128)S(1)} %pad_add_fusion.3.index, ...), custom_call_target="tpu_custom_call" | custom-call | flops 1000 | bytes 1000 | tf_op jit(solution)/shard_map/pallas_call | solution.py:362
  54.6 3.5 %collective-permute-done.46.b1 = bf16[256,1024]{1,0:T(8,128)(2,1)} collective-permute-done((bf16[256,1024]{1,0:T(8,128)(2,1)S(1)}, bf16[256,1024]{1,0:T(8,128)(2,1)}, u32[]{:S(2)}, u32[]{:S(2)}) %collective-permute-start.46) | collective-permute-done | bytes 524320 | tf_op jit(solution)/shard_map/ppermute | solution.py:17
  58.1 38.6 %conditional.6 = (f32[128,1024]{1,0:T(8,128)S(1)}, f32[128,1024]{1,0:T(8,128)S(1)}, f32[128,1]{0,1:T(1,128)S(1)}, bf16[512,1024]{1,0:T(8,128)(2,1)}, bf16[512,10...) conditional(s32[]{:T(128)} %convert_element_type.170, () %tuple.72, ...), branch_computations={%region_2.3_spmd, %region_3.5_spmd} | conditional | flops 8781966 | bytes 40115408 | solution.py:66
  64.6 5.3 %collective-permute-done.6 = bf16[2,128,512]{2,1,0:T(8,128)(2,1)S(1)} collective-permute-done((bf16[2,128,512]{2,1,0:T(8,128)(2,1)S(1)}, bf16[2,128,512]{2,1,0:T(8,128)(2,1)S(1)}, u32[]{:S(2)}, u32[]{:S(2)}) %collective-permute-start.6) | collective-permute-done | bytes 262176 | tf_op jit(solution)/shard_map/cond/branch_1_fun/ppermute | solution.py:17
  85.7 3.9 %collective-permute-done.13 = bf16[2,128,512]{2,1,0:T(8,128)(2,1)S(1)} collective-permute-done((bf16[2,128,512]{2,1,0:T(8,128)(2,1)S(1)}, bf16[2,128,512]{2,1,0:T(8,128)(2,1)S(1)}, u32[]{:S(2)}, u32[]{:S(2)}) %collective-permute-start.13) | collective-permute-done | bytes 262176 | tf_op jit(solution)/shard_map/cond/branch_1_fun/ppermute | solution.py:17
  96.8 19.2 %all-gather.2.cloned.1.call-done.f = bf16[1024,1792]{1,0:T(8,128)(2,1)} async-done(((bf16[256,1792]{1,0:T(8,128)(2,1)}), bf16[1024,1792]{1,0:T(8,128)(2,1)}) %all-gather.2.cloned.1.call-update) | async-done | bytes 3670032 | tf_op jit(solution)/shard_map/all_gather | solution.py:482
  116.0 12.7 %shard_map.258 = (bf16[512,1024]{1,0:T(8,128)(2,1)}, bf16[512,1024]{1,0:T(8,128)(2,1)}, bf16[1024,1152]{1,0:T(8,128)(2,1)}, bf16[1024,640]{1,0:T(8,128)(2,1)S(1)...) custom-call(s32[4]{0:T(128)S(1)} %pad_add_fusion.3.index, bf16[512,1024]{1,0:T(8,128)(2,1)} %get-tuple-element.307.x_low, ...), custom_call_target="tpu_custom_call" | custom-call | flops 1000 | bytes 1000 | tf_op jit(solution)/shard_map/pallas_call | solution.py:362
  128.7 8.1 %shard_map.259 = bf16[1024,1792]{1,0:T(8,128)(2,1)} custom-call(bf16[1024,1024]{1,0:T(8,128)(2,1)S(1)} %get-tuple-element.312.unit, bf16[1024,1024]{1,0:T(8,128)(2,1)S(1)} %get-tuple-element.313.branch, bf16[1024,1152]{1,0:T(8,128)(2,1)} %get-tuple-element.314.gate_up, bf16[1024,640]{1,0:T(8,128)(2,1)S(1)} %get-tuple-element.315.activated), custom_call_target="tpu_custom_call" | custom-call | flops 1000 | bytes 1000 | tf_op jit(solution)/shard_map/pallas_call | solution.py:362
  136.9 77.1 %conditional.7 = (bf16[512,1024]{1,0:T(8,128)(2,1)}, bf16[512,1024]{1,0:T(8,128)(2,1)}, bf16[1024,384]{1,0:T(8,128)(2,1)}, f32[8,128]{1,0:T(8,128)S(1)}, f32[128...) conditional(s32[]{:T(128)} %convert_element_type.170, () %tuple.67, ...), branch_computations={%region_5.6_spmd, %region_6.9_spmd} | conditional | flops 17305548 | bytes 94678800 | solution.py:66
  147.3 4.0 %branch_1_fun.6 = (bf16[512,1024]{1,0:T(8,128)(2,1)S(1)}, bf16[512,1024]{1,0:T(8,128)(2,1)S(1)}) custom-call(bf16[1024,640]{1,0:T(8,128)(2,1)S(1)} %get-tuple-element.174.activated, bf16[1024,1792]{1,0:T(8,128)(2,1)} %get-tuple-element.175.f), custom_call_target="tpu_custom_call" | custom-call | flops 1000 | bytes 1000 | tf_op jit(solution)/shard_map/cond/branch_1_fun/pallas_call | solution.py:362
  157.7 3.8 %collective-permute-done.17 = bf16[2,128,512]{2,1,0:T(8,128)(2,1)S(1)} collective-permute-done((bf16[2,128,512]{2,1,0:T(8,128)(2,1)S(1)}, bf16[2,128,512]{2,1,0:T(8,128)(2,1)S(1)}, u32[]{:S(2)}, u32[]{:S(2)}) %collective-permute-start.17) | collective-permute-done | bytes 262176 | tf_op jit(solution)/shard_map/cond/branch_1_fun/ppermute | solution.py:17
  187.3 2.9 %collective-permute-done.22 = bf16[2,128,512]{2,1,0:T(8,128)(2,1)S(1)} collective-permute-done((bf16[2,128,512]{2,1,0:T(8,128)(2,1)S(1)}, bf16[2,128,512]{2,1,0:T(8,128)(2,1)S(1)}, u32[]{:S(2)}, u32[]{:S(2)}) %collective-permute-start.22) | collective-permute-done | bytes 262176 | tf_op jit(solution)/shard_map/cond/branch_1_fun/ppermute | solution.py:17
  200.7 10.5 %branch_1_fun.4 = (bf16[512,1024]{1,0:T(8,128)(2,1)}, bf16[512,1024]{1,0:T(8,128)(2,1)}, bf16[1024,256]{1,0:T(8,128)(2,1)S(1)}, f32[8,128]{1,0:T(8,128)S(1)}) custom-call(s32[4]{0:T(128)S(1)} %get-tuple-element.147.index, bf16[512,1024]{1,0:T(8,128)(2,1)S(1)} %bitcast.224, bf16[512,1024]{1,0:T(8,128)(2,1)S(1)} %collective-permute-done.25.a_high, ...), custom_call_target="tpu_custom_call" | custom-call | flops 1000 | bytes 1000 | tf_op jit(solution)/shard_map/cond/branch_1_fun/pallas_call | solution.py:362
  215.6 42.2 %conditional.8 = (f32[128,1024]{1,0:T(8,128)S(1)}, f32[2304]{0:T(1024)S(1)}) conditional(s32[]{:T(128)} %convert_element_type.170, () %tuple.78, (bf16[512,1024]{1,0:T(8,128)(2,1)}, bf16[512,1024]{1,0:T(8,128)(2,1)}, f32[2,1024]{1,0:T(2,128)S(1)}, f32[8,128]{1,0:T(8,128)S(1)}, f32[128,1024]{1,0:T(8,128)S(1)}, /*index=5*/f32[128,1]{0,1:T(1,128)S(1)}, ...), branch_computations={%region_10.11_spmd, %region_11.17_spmd} | conditional | flops 4077243 | bytes 20554920 | solution.py:66
  218.3 3.3 %concatenate.53 = f32[2304]{0:T(1024)S(1)} concatenate(f32[2048]{0:T(1024)S(1)} %bitcast.261, f32[64]{0:T(128)S(1)} %get-tuple-element.390, f32[64]{0:T(128)S(1)} %get-tuple-element.389, f32[1]{0:T(128)} %bitcast.87, f32[1]{0:T(128)} %bitcast.88, f32[1]{0:T(128)} %bitcast.89, f32[1]{0:T(128)} %bitcast.90, f32[1]{0:T(128)} %bitcast.91, f32[123]{0:T(128)S(1)} %broadcast.178), dimensions={0} | concatenate | bytes 18432 | tf_op jit(solution)/shard_map/cond/branch_1_fun/concatenate | solution.py:579
  228.8 13.7 %collective-permute-done.40 = f32[18,128]{1,0:T(8,128)S(1)} collective-permute-done((f32[18,128]{1,0:T(8,128)S(1)}, f32[18,128]{1,0:T(8,128)S(1)}, u32[]{:S(2)}, u32[]{:S(2)}) %collective-permute-start.40) | collective-permute-done | bytes 9248 | tf_op jit(solution)/shard_map/cond/branch_1_fun/ppermute | solution.py:17
  242.5 3.7 %collective-permute-done.41 = f32[18,128]{1,0:T(8,128)S(1)} collective-permute-done((f32[18,128]{1,0:T(8,128)S(1)}, f32[18,128]{1,0:T(8,128)S(1)}, u32[]{:S(2)}, u32[]{:S(2)}) %collective-permute-start.41) | collective-permute-done | bytes 9248 | tf_op jit(solution)/shard_map/cond/branch_1_fun/ppermute | solution.py:82
  247.2 3.6 %collective-permute-done.42 = f32[18,128]{1,0:T(8,128)S(1)} collective-permute-done((f32[18,128]{1,0:T(8,128)S(1)}, f32[18,128]{1,0:T(8,128)S(1)}, u32[]{:S(2)}, u32[]{:S(2)}) %collective-permute-start.42) | collective-permute-done | bytes 9248 | tf_op jit(solution)/shard_map/cond/branch_1_fun/ppermute | solution.py:82
  261.3 13.4 %conditional.9 = (f32[512,1024]{1,0:T(8,128)}, f32[256,1152]{1,0:T(8,128)}, f32[256,1152]{1,0:T(8,128)}, f32[1152,256]{1,0:T(8,128)}) conditional(s32[]{:T(128)} %convert_element_type.170, () %tuple.82, (f32[128,1024]{1,0:T(8,128)S(1)}, f32[8,1024]{1,0:T(8,128)S(1)}, f32[128,1024]{1,0:T(8,128)S(1)}, f32[128,1024]{1,0:T(8,128)}, s32[]{:T(128)}, ...), branch_computations={%region_18.19_spmd, %region_19.22_spmd} | conditional | flops 7210108 | bytes 14964560 | solution.py:66
  263.5 5.8 %collective-permute-done.3 = bf16[128,1024]{1,0:T(8,128)(2,1)S(1)} collective-permute-done((bf16[128,1024]{1,0:T(8,128)(2,1)S(1)}, bf16[128,1024]{1,0:T(8,128)(2,1)S(1)}, u32[]{:S(2)}, u32[]{:S(2)}) %collective-permute-start.3) | collective-permute-done | bytes 262176 | tf_op jit(solution)/shard_map/cond/branch_1_fun/ppermute | solution.py:17
  269.4 3.5 %branch_1_fun.7 = (f32[256,1152]{1,0:T(8,128)}, f32[256,1152]{1,0:T(8,128)}, f32[1152,256]{1,0:T(8,128)}) custom-call(s32[4]{0:T(128)S(1)} %get-tuple-element.196.index, bf16[256,1792]{1,0:T(8,128)(2,1)S(1)} %get-tuple-element.197.mine, bf16[256,1792]{1,0:T(8,128)(2,1)} %get-tuple-element.198.other), custom_call_target="tpu_custom_call" | custom-call | flops 1000 | bytes 1000 | tf_op jit(solution)/shard_map/cond/branch_1_fun/pallas_call | solution.py:362
  (271 shorter events, 124.2 us)
Async XLA Ops:
  7.2 108.8 %all-gather.2.cloned.1.call-start = ((), (), s32[]{:S(2)}) async-start(), calls=%async_computation.2 | async-start | bytes 4587520 | tf_op jit(solution)/shard_map/all_gather | solution.py:482
  13.5 29.0 %collective-permute-start.45 = (bf16[272,384]{1,0:T(8,128)(2,1)S(1)}, bf16[272,384]{1,0:T(8,128)(2,1)S(1)}, u32[]{:S(2)}, u32[]{:S(2)}) collective-permute-start(bf16[272,384]{1,0:T(8,128)(2,1)S(1)} %shard_map.256.rest_0_), channel_id=1, source_target_pairs={{0,24},{8,16},{16,8},{24,0},{1,25},{9,17},{17,9},{25,1},{2,26},{10... | collective-permute-start | bytes 626696 | tf_op jit(solution)/shard_map/ppermute | solution.py:60
  18.7 23.9 %collective-permute-start.44 = (bf16[272,384]{1,0:T(8,128)(2,1)S(1)}, bf16[272,384]{1,0:T(8,128)(2,1)S(1)}, u32[]{:S(2)}, u32[]{:S(2)}) collective-permute-start(bf16[272,384]{1,0:T(8,128)(2,1)S(1)} %shard_map.256.rest_0_), channel_id=1, source_target_pairs={{0,16},{8,24},{16,0},{24,8},{1,17},{9,25},{17,1},{25,9},{2,18},{10... | collective-permute-start | bytes 626696 | tf_op jit(solution)/shard_map/ppermute | solution.py:60
  18.7 23.9 %collective-permute-start.43 = (bf16[272,384]{1,0:T(8,128)(2,1)S(1)}, bf16[272,384]{1,0:T(8,128)(2,1)S(1)}, u32[]{:S(2)}, u32[]{:S(2)}) collective-permute-start(bf16[272,384]{1,0:T(8,128)(2,1)S(1)} %shard_map.256.rest_0_), channel_id=1, source_target_pairs={{0,8},{8,0},{16,24},{24,16},{1,9},{9,1},{17,25},{25,17},{2,10},{10... | collective-permute-start | bytes 626696 | tf_op jit(solution)/shard_map/ppermute | solution.py:60
  21.7 13.4 %collective-permute-start = (bf16[256,1024]{1,0:T(8,128)(2,1)}, bf16[256,1024]{1,0:T(8,128)(2,1)}, u32[]{:S(2)}, u32[]{:S(2)}) collective-permute-start(bf16[256,1024]{1,0:T(8,128)(2,1)} %pad_maximum_fusion), channel_id=1, source_target_pairs={{0,4},{4,0},{1,5},{5,1},{2,6},{6,2},{3,7},{7,3},{8,12},{12,8},{9,1... | collective-permute-start | bytes 1572872 | tf_op jit(solution)/shard_map/cond/branch_1_fun/ppermute | solution.py:17
  23.4 11.9 %collective-permute-start.2 = (s32[2,256]{1,0:T(2,128)S(1)}, s32[2,256]{1,0:T(2,128)S(1)}, u32[]{:S(2)}, u32[]{:S(2)}) collective-permute-start(s32[2,256]{1,0:T(2,128)S(1)} %get-tuple-element.380), channel_id=1, source_target_pairs={{0,4},{4,0},{1,5},{5,1},{2,6},{6,2},{3,7},{7,3},{8,12},{12,8},{9,1... | collective-permute-start | bytes 6152 | tf_op jit(solution)/shard_map/cond/branch_1_fun/ppermute | solution.py:17
  42.6 171.4 %reduce-scatter.3.cloned.1.call-start = ((), (), s32[]{:S(2)}) async-start(), calls=%async_computation.3 | async-start | bytes 4587520 | tf_op jit(solution)/shard_map/reduce_scatter | solution.py:530
  43.7 14.4 %collective-permute-start.46 = (bf16[256,1024]{1,0:T(8,128)(2,1)S(1)}, bf16[256,1024]{1,0:T(8,128)(2,1)}, u32[]{:S(2)}, u32[]{:S(2)}) collective-permute-start(bf16[256,1024]{1,0:T(8,128)(2,1)S(1)} %pad_maximum_fusion.16.b0), channel_id=1, source_target_pairs={{0,4},{4,0},{1,5},{5,1},{2,6},{6,2},{3,7},{7,3},{8,12},{12,8},{9,1... | collective-permute-start | bytes 1572872 | tf_op jit(solution)/shard_map/ppermute | solution.py:17
  61.5 8.4 %collective-permute-start.6 = (bf16[2,128,512]{2,1,0:T(8,128)(2,1)S(1)}, bf16[2,128,512]{2,1,0:T(8,128)(2,1)S(1)}, u32[]{:S(2)}, u32[]{:S(2)}) collective-permute-start(bf16[2,128,512]{2,1,0:T(8,128)(2,1)S(1)} %slice_bitcast_fusion.5), channel_id=1, source_target_pairs={{0,4},{4,0},{1,5},{5,1},{2,6},{6,2},{3,7},{7,3},{8,12},{12,8},{9,1... | collective-permute-start | bytes 786440 | tf_op jit(solution)/shard_map/cond/branch_1_fun/ppermute | solution.py:17
  63.1 8.1 %collective-permute-start.8 = (bf16[2,128,512]{2,1,0:T(8,128)(2,1)S(1)}, bf16[2,128,512]{2,1,0:T(8,128)(2,1)S(1)}, u32[]{:S(2)}, u32[]{:S(2)}) collective-permute-start(bf16[2,128,512]{2,1,0:T(8,128)(2,1)S(1)} %slice_bitcast_fusion.3), channel_id=1, source_target_pairs={{0,2},{2,0},{1,3},{3,1},{4,6},{6,4},{5,7},{7,5},{8,10},{10,8},{9,1... | collective-permute-start | bytes 786440 | tf_op jit(solution)/shard_map/cond/branch_1_fun/ppermute | solution.py:17
  136.8 123.5 %reduce-scatter.5.cloned.1.call-start = ((), (), s32[]{:S(2)}) async-start(), calls=%async_computation.4 | async-start | bytes 983040 | tf_op jit(solution)/shard_map/reduce_scatter | solution.py:573
  152.3 9.2 %collective-permute-start.17 = (bf16[2,128,512]{2,1,0:T(8,128)(2,1)S(1)}, bf16[2,128,512]{2,1,0:T(8,128)(2,1)S(1)}, u32[]{:S(2)}, u32[]{:S(2)}) collective-permute-start(bf16[2,128,512]{2,1,0:T(8,128)(2,1)S(1)} %slice_bitcast_fusion.19), channel_id=1, source_target_pairs={{0,4},{4,0},{1,5},{5,1},{2,6},{6,2},{3,7},{7,3},{8,12},{12,8},{9,1... | collective-permute-start | bytes 786440 | tf_op jit(solution)/shard_map/cond/branch_1_fun/ppermute | solution.py:17
  153.9 9.3 %collective-permute-start.19 = (bf16[2,128,512]{2,1,0:T(8,128)(2,1)S(1)}, bf16[2,128,512]{2,1,0:T(8,128)(2,1)S(1)}, u32[]{:S(2)}, u32[]{:S(2)}) collective-permute-start(bf16[2,128,512]{2,1,0:T(8,128)(2,1)S(1)} %slice_bitcast_fusion.17), channel_id=1, source_target_pairs={{0,2},{2,0},{1,3},{3,1},{4,6},{6,4},{5,7},{7,5},{8,10},{10,8},{9,1... | collective-permute-start | bytes 786440 | tf_op jit(solution)/shard_map/cond/branch_1_fun/ppermute | solution.py:17
  155.9 11.3 %collective-permute-start.27 = (bf16[2,128,512]{2,1,0:T(8,128)(2,1)S(1)}, bf16[2,128,512]{2,1,0:T(8,128)(2,1)S(1)}, u32[]{:S(2)}, u32[]{:S(2)}) collective-permute-start(bf16[2,128,512]{2,1,0:T(8,128)(2,1)S(1)} %slice_bitcast_fusion.15), channel_id=1, source_target_pairs={{0,4},{4,0},{1,5},{5,1},{2,6},{6,2},{3,7},{7,3},{8,12},{12,8},{9,1... | collective-permute-start | bytes 786440 | tf_op jit(solution)/shard_map/cond/branch_1_fun/ppermute | solution.py:17
  156.5 12.3 %collective-permute-start.29 = (bf16[2,128,512]{2,1,0:T(8,128)(2,1)S(1)}, bf16[2,128,512]{2,1,0:T(8,128)(2,1)S(1)}, u32[]{:S(2)}, u32[]{:S(2)}) collective-permute-start(bf16[2,128,512]{2,1,0:T(8,128)(2,1)S(1)} %slice_bitcast_fusion.13), channel_id=1, source_target_pairs={{0,2},{2,0},{1,3},{3,1},{4,6},{6,4},{5,7},{7,5},{8,10},{10,8},{9,1... | collective-permute-start | bytes 786440 | tf_op jit(solution)/shard_map/cond/branch_1_fun/ppermute | solution.py:17
  163.4 7.8 %collective-permute-start.20 = (bf16[128,512]{1,0:T(8,128)(2,1)S(1)}, bf16[128,512]{1,0:T(8,128)(2,1)S(1)}, u32[]{:S(2)}, u32[]{:S(2)}) collective-permute-start(bf16[128,512]{1,0:T(8,128)(2,1)S(1)} %fusion.25), channel_id=1, source_target_pairs={{0,4},{4,0},{1,5},{5,1},{2,6},{6,2},{3,7},{7,3},{8,12},{12,8},{9,1... | collective-permute-start | bytes 393224 | tf_op jit(solution)/shard_map/cond/branch_1_fun/ppermute | solution.py:17
  184.4 8.6 %collective-permute-start.31 = (bf16[128,1024]{1,0:T(8,128)(2,1)S(1)}, bf16[128,1024]{1,0:T(8,128)(2,1)S(1)}, u32[]{:S(2)}, u32[]{:S(2)}) collective-permute-start(bf16[128,1024]{1,0:T(8,128)(2,1)S(1)} %get-tuple-element.369), channel_id=1, source_target_pairs={{0,2},{2,0},{1,3},{3,1},{4,6},{6,4},{5,7},{7,5},{8,10},{10,8},{9,1... | collective-permute-start | bytes 786440 | tf_op jit(solution)/shard_map/cond/branch_1_fun/ppermute | solution.py:17
  190.3 9.0 %collective-permute-start.25 = (bf16[512,1024]{1,0:T(8,128)(2,1)S(1)}, bf16[512,1024]{1,0:T(8,128)(2,1)S(1)}, u32[]{:S(2)}, u32[]{:S(2)}) collective-permute-start(bf16[512,1024]{1,0:T(8,128)(2,1)S(1)} %bitcast.223), channel_id=1, source_target_pairs={{0,1},{1,0},{2,3},{3,2},{4,5},{5,4},{6,7},{7,6},{8,9},{9,8},{10,11... | collective-permute-start | bytes 3145736 | tf_op jit(solution)/shard_map/cond/branch_1_fun/ppermute | solution.py:17
  214.0 46.2 %collective-permute-start.47 = (bf16[256,1792]{1,0:T(8,128)(2,1)}, bf16[256,1792]{1,0:T(8,128)(2,1)}, u32[]{:S(2)}, u32[]{:S(2)}) collective-permute-start(bf16[256,1792]{1,0:T(8,128)(2,1)} %reduce-scatter.3.cloned.1.call-done), channel_id=1, source_target_pairs={{0,4},{4,0},{1,5},{5,1},{2,6},{6,2},{3,7},{7,3},{8,12},{12,8},{9,1... | collective-permute-start | bytes 2752520 | tf_op jit(solution)/shard_map/ppermute | solution.py:17
  215.6 8.0 %collective-permute-start.33 = (bf16[512,1024]{1,0:T(8,128)(2,1)}, bf16[512,1024]{1,0:T(8,128)(2,1)S(1)}, u32[]{:S(2)}, u32[]{:S(2)}) collective-permute-start(bf16[512,1024]{1,0:T(8,128)(2,1)} %get-tuple-element.182), channel_id=1, source_target_pairs={{0,1},{1,0},{2,3},{3,2},{4,5},{5,4},{6,7},{7,6},{8,9},{9,8},{10,11... | collective-permute-start | bytes 3145736 | tf_op jit(solution)/shard_map/cond/branch_1_fun/ppermute | solution.py:17
  225.3 25.5 %collective-permute-start.34 = (bf16[2,128,512]{2,1,0:T(8,128)(2,1)S(1)}, bf16[2,128,512]{2,1,0:T(8,128)(2,1)S(1)}, u32[]{:S(2)}, u32[]{:S(2)}) collective-permute-start(bf16[2,128,512]{2,1,0:T(8,128)(2,1)S(1)} %slice_bitcast_fusion.27), channel_id=1, source_target_pairs={{0,4},{4,0},{1,5},{5,1},{2,6},{6,2},{3,7},{7,3},{8,12},{12,8},{9,1... | collective-permute-start | bytes 786440 | tf_op jit(solution)/shard_map/cond/branch_1_fun/ppermute | solution.py:17
  225.9 24.9 %collective-permute-start.36 = (bf16[2,128,512]{2,1,0:T(8,128)(2,1)S(1)}, bf16[2,128,512]{2,1,0:T(8,128)(2,1)S(1)}, u32[]{:S(2)}, u32[]{:S(2)}) collective-permute-start(bf16[2,128,512]{2,1,0:T(8,128)(2,1)S(1)} %slice_bitcast_fusion.25), channel_id=1, source_target_pairs={{0,2},{2,0},{1,3},{3,1},{4,6},{6,4},{5,7},{7,5},{8,10},{10,8},{9,1... | collective-permute-start | bytes 786440 | tf_op jit(solution)/shard_map/cond/branch_1_fun/ppermute | solution.py:17
  227.3 15.2 %collective-permute-start.40 = (f32[18,128]{1,0:T(8,128)S(1)}, f32[18,128]{1,0:T(8,128)S(1)}, u32[]{:S(2)}, u32[]{:S(2)}) collective-permute-start(f32[18,128]{1,0:T(8,128)S(1)} %fusion.42), channel_id=1, source_target_pairs={{0,4},{4,0},{1,5},{5,1},{2,6},{6,2},{3,7},{7,3},{8,12},{12,8},{9,1... | collective-permute-start | bytes 27656 | tf_op jit(solution)/shard_map/cond/branch_1_fun/ppermute | solution.py:17
  260.2 14.5 %collective-permute-start.48 = (bf16[256,384]{1,0:T(8,128)(2,1)}, bf16[256,384]{1,0:T(8,128)(2,1)S(1)}, u32[]{:S(2)}, u32[]{:S(2)}) collective-permute-start(bf16[256,384]{1,0:T(8,128)(2,1)} %reduce-scatter.5.cloned.1.call-done.mine), channel_id=1, source_target_pairs={{0,4},{4,0},{1,5},{5,1},{2,6},{6,2},{3,7},{7,3},{8,12},{12,8},{9,1... | collective-permute-start | bytes 589832 | tf_op jit(solution)/shard_map/ppermute | solution.py:17
  (58 other events, 343.0 us)
Sparse Core Ops, SparseCore 0:
  42.7 73.2 all-gather.1
  136.9 66.9 reduce-scatter.2
  214.1 20.9 reduce-scatter.4

commit v3 on v2

--- a/solution.py
+++ b/solution.py
@@ -42,46 +42,67 @@
     return jnp.concatenate([left, right], -1)
 
 
-def gather_plane(block):
+def hop(value, axis, step=1):
+    size = lax.axis_size(axis)
+    return lax.ppermute(value, axis, [(i, i ^ step) for i in range(size)])
+
+
+def last_sums(near, far, small):
+    block, width = near.shape[0] // 4, near.shape[1] // 2
+    far, more = together(swap(far, "core"), hop(small, "core"))
+    total = (near.astype(F32) + far.astype(F32)).reshape(2, 2, block, -1)
+    small = small + more
+    low = total.astype(BF16)
+    from_x = swap(low[1, :, :, :width], "ctx")
+    from_y = swap(low[:, 1, :, width:], "y")
+    from_x, from_y, more = together(from_x, from_y, hop(small, "ctx"))
+    left = total[0, :, :, :width] + from_x.astype(F32)
+    right = total[:, 0, :, width:] + from_y.astype(F32)
+    small = small + more
+    from_y = swap(left[1].astype(BF16), "y")
+    from_x = swap(right[1].astype(BF16), "ctx")
+    from_x, from_y, more = together(from_x, from_y, hop(small, "y"))
+    return jnp.concatenate([left[0] + from_y.astype(F32), right[0] + from_x.astype(F32)], -1), small + more
+
+
+def gather_plane(block, beside=None):
     width = block.shape[-1] // 2
     left, right = block[:, :width], block[:, width:]
-    left = jnp.stack([left, swap(left, "ctx")])
-    right = jnp.stack([right, swap(right, "y")])
+    left_x, right_y = swap(left, "ctx"), swap(right, "y")
+    if beside is not None:
+        beside, left_x, right_y = together(swap(beside, "core"), left_x, right_y)
+    left = jnp.stack([left, left_x])
+    right = jnp.stack([right, right_y])
     left = jnp.stack([left, swap(left, "y")], 1)
     right = jnp.stack([right, swap(right, "ctx")], 0)
     near = jnp.concatenate([left, right], -1).reshape(-1, 2 * width)
-    return near, swap(near, "core")
-
-
-def gather_shards(own):
+    return near, swap(near, "core"), beside
+
+
+def near_shards():
+    return lax.axis_size("fsdp") <= 4
+
+
+def direct(pieces):
     size = lax.axis_size("fsdp")
-    parts = [own]
-    for step in range(1, size):
-        parts.append(lax.ppermute(own, "fsdp", [(i, i ^ step) for i in range(size)]))
-    return parts
+    return [
+        piece if step == 0 else lax.ppermute(piece, "fsdp", [(i, i ^ step) for i in range(size)])
+        for step, piece in enumerate(pieces)
+    ]
+
+
+def onward(value):
+    size = lax.axis_size("fsdp")
+    return lax.ppermute(value, "fsdp", [(i, (i + 1) % size) for i in range(size)])
+
+
+def together(*values):
+    return lax.optimization_barrier(values)
 
 
 def region(flag, work, *args):
     shapes = jax.eval_shape(work, *args)
     return lax.cond(flag, work, lambda *_: jax.tree.map(lambda x: jnp.zeros(x.shape, x.dtype), shapes), *args)
-
-
-def gather_rows(block, why, core):
-    pair = jnp.stack([block, swap(block, "y")])
-    four = jnp.concatenate([pair, swap(pair, "core")])
-    pieces = [lax.dynamic_slice_in_dim(four, 2 * (core ^ (i % 2)) + (why ^ (i // 2)), 1)[0] for i in range(4)]
-    return jnp.concatenate(pieces)
-
-
-def sum_all(value):
-    for axis in ("core", "y", "ctx"):
-        value = value + swap(value, axis)
-    size = lax.axis_size("fsdp")
-    step = 1
-    while step < size:
-        value = value + lax.ppermute(value, "fsdp", [(i, i ^ step) for i in range(size)])
-        step *= 2
-    return value
 
 
 def lanes(shape):
@@ -254,45 +275,139 @@
     gains[1:2, :] = key_sum
 
 
-def feed_forward(
-    index, x_low, x_high, b0, b1, b2, b3, f, second_low, second_high, gate_up, activated, branch, unit
-):
+def activated_gradient(index, b0, b1, b2, b3, *rest):
+    *parts, down_w, back = rest
     own, length = index[0], index[1]
+    count, rows = len(parts), parts[0].shape[0]
+    for at, part in enumerate(parts):
+        to = pl.multiple_of((index[2] + count - at) % count * rows, rows)
+        down_w[pl.ds(to, rows), :] = part[...]
+    pair = b0.shape[0]
+    block = pair // 2
+    row = lax.broadcasted_iota(jnp.int32, (pair, 1), 0)
+    for at, b in enumerate((b0, b1, b2, b3)):
+        kk, xx = divmod(at, 2)
+        ok = (own ^ (kk + 4 * xx + jnp.where(row >= block, 2, 0))) * block + row % block < length
+        back[at * pair : (at + 1) * pair, :] = jnp.where(ok, nn(b[...], down_w[...]), 0.0)
+
+
+def feed_forward(index, x_low, x_high, b0, b1, b2, b3, back_all, gu_w, second_low, second_high, grad, activated, gate_up):
+    own, length = index[0], index[1]
+    width = x_low.shape[1]
     pair = b0.shape[0]
     block, four = pair // 2, 2 * pair
     main = gate_up.shape[1] // 2 // 128 * 128
     both = 2 * main
     wide = both + 128
     low = lanes((four, 128)) < HD
-    rows = lax.broadcasted_iota(jnp.int32, (pair, 1), 0)
-    for kk, (x, bs, to) in enumerate(((x_low, (b0, b1), second_low), (x_high, (b2, b3), second_high))):
+    row = lax.broadcasted_iota(jnp.int32, (four, 1), 0)
+    bs = (b0, b1, b2, b3)
+    for kk, (x, to) in enumerate(((x_low, second_low), (x_high, second_high))):
         here = slice(kk * four, (kk + 1) * four)
-        x = x[...]
-        unit[here, :] = x
-        for xx, b in enumerate(bs):
-            starts = jnp.where(rows < block, own ^ (xx * 4 + kk), own ^ (xx * 4 + 2 + kk)) * block
-            b = b[...]
-            b = jnp.where(starts + rows % block < length, b, jnp.zeros_like(b))
-            branch[kk * four + xx * pair : kk * four + (xx + 1) * pair, :] = b
-        gu = nn(x, f[:, :wide])
-        back = nn(branch[here, :], f[:, wide:])
+        start = own ^ (kk + jnp.where(row >= pair, 4, 0) + jnp.where(row % pair >= block, 2, 0))
+        ok = start * block + row % block < length
+        gu = nn(x[...], gu_w[...])
+        back = back_all[here, :]
         tail = gu[:, both:]
         gate = jnp.concatenate([gu[:, :main], tail], 1)
         upper = jnp.concatenate([gu[:, main:both], pltpu.roll(tail, HD, 1)], 1)
         sigmoid = 1.0 / (1.0 + jnp.exp(-gate))
         silu = gate * sigmoid
-        act = silu * upper
+        act = jnp.where(ok, silu * upper, 0.0)
         gate_back = back * upper * (sigmoid + silu * (1.0 - sigmoid))
         upper_back = back * silu
         activated[here, :main] = act[:, :main].astype(BF16)
         activated[here, main:] = jnp.where(low, act[:, main:], 0.0).astype(BF16)
         mix = jnp.where(low, gate_back[:, main:], pltpu.roll(upper_back[:, main:], HD, 1))
-        gu = jnp.concatenate([gate_back[:, :main], upper_back[:, :main], mix], 1).astype(BF16)
-        gate_up[here, :] = gu
-        to[...] = nt(gu, f[:, :wide]).astype(BF16)
-
-
-def pack_attention(index, query, key, value, output, gains, out):
+        gate_up[here, :main] = gate_back[:, :main].astype(BF16)
+        gate_up[here, main:both] = upper_back[:, :main].astype(BF16)
+        gate_up[here, both:] = mix.astype(BF16)
+        to[...] = nt(gate_up[here, :], gu_w[...]).astype(BF16)
+    step = width // 2
+    for row in range(0, width, step):
+        here = slice(row, row + step)
+        out = tn(x_low[:, here], gate_up[:four, :]) + tn(x_high[:, here], gate_up[four:, :])
+        grad[here, :wide] = out.astype(BF16)
+        out = tn(b0[:, here], activated[:pair, :])
+        for piece in range(1, 4):
+            out += tn(bs[piece][:, here], activated[piece * pair : (piece + 1) * pair, :])
+        grad[here, wide:] = out.astype(BF16)
+
+
+def down_product(index, activated, down_w, branch_low, branch_high):
+    four = branch_low.shape[0]
+    branch_low[...] = nt(activated[:four, :], down_w[...]).astype(BF16)
+    branch_high[...] = nt(activated[four:, :], down_w[...]).astype(BF16)
+
+
+def small_sums(index, inputs, middle, branch, second, inverse, gain, attention_sums, head_sums, out):
+    own, length = index[0], index[1]
+    block, width = inputs.shape
+    row = lax.broadcasted_iota(jnp.int32, (block, 1), 0)
+    valid = (own * block + row < length).astype(F32)
+    x, m = inputs[...], middle[...]
+    feedforward_sums = jnp.sum(second[...] * (m * inverse[...]), axis=0, keepdims=True)
+    for at in range(width // 128):
+        here = slice(at * 128, (at + 1) * 128)
+        out[at : at + 1, :] = feedforward_sums[:, here]
+        out[width // 128 + at : width // 128 + at + 1, :] = attention_sums[0:1, here]
+    lane = lanes((1, 128))
+    q = head_sums[0:1, :] + pltpu.roll(head_sums[0:1, :], HD, 1)
+    out[16:17, :] = jnp.where(lane < HD, q, pltpu.roll(head_sums[1:2, :], HD, 1))
+    line = jnp.where(lane == 4, jnp.sum(valid), 0.0)
+    for at, item in enumerate((x, m - x, m, branch[...])):
+        line = jnp.where(lane == at, jnp.sum(item * item * valid), line)
+    out[17:18, :] = line
+    out[18:, :] = jnp.zeros((out.shape[0] - 18, 128), F32)
+
+
+def attention_weights(index, unit, back, a_low, a_high, mixed_rel, w, gains, out, gain_out):
+    wide = back.shape[1]
+    half = a_low.shape[0]
+    step = 256
+    for row in range(0, out.shape[0], step):
+        here = slice(row, row + step)
+        grad = tn(unit[:, here], back[...])
+        out[here, :wide] = grad.astype(BF16)
+        grad = jnp.sum(grad * w[here, :wide].astype(F32), axis=1, keepdims=True)
+        gain_out[:, here] = jnp.broadcast_to(grad, (step, 128)).T[:8] / gains[0:1, here]
+        o = tn(a_low[:, here], mixed_rel[:half, :]) + tn(a_high[:, here], mixed_rel[half:, :])
+        out[here, wide:] = o.astype(BF16)
+
+
+def fetch(sources, targets, sems):
+    copies = [pltpu.make_async_copy(one, two, sems.at[at]) for at, (one, two) in enumerate(zip(sources, targets))]
+    for copy in copies:
+        copy.start()
+    return copies
+
+
+def halves(own, source, targets, sems, base):
+    block = targets[0].shape[0] // 2
+    copies = []
+    for kk, target in enumerate(targets):
+        for yy in range(2):
+            start = pl.multiple_of(((own ^ (2 * yy + kk)) & 3) * block, block)
+            to = target.at[pl.ds(yy * block, block)]
+            copies.append(pltpu.make_async_copy(source.at[0, pl.ds(start, block)], to, sems.at[base + len(copies)]))
+    for copy in copies:
+        copy.start()
+    return copies
+
+
+def prelude(
+    index, query_from, key_from, value_from, output_from, one_from, two_from, hidden,
+    out, hidden_near, hidden_far,
+    query, key, value, output, one_gain, two_gain, sems,
+):
+    copies = fetch(
+        (query_from, key_from, value_from, output_from, one_from, two_from),
+        (query, key, value, output, one_gain, two_gain),
+        sems,
+    )
+    late = halves(index[0], hidden, (hidden_near, hidden_far), sems, len(copies))
+    for copy in copies:
+        copy.wait()
     rows = query.shape[0]
     wide = query.shape[1] // 2
     for half in range(2):
@@ -309,7 +424,42 @@
             out[:rows, wide : wide + 2 * HD] = kv.astype(BF16)
             out[:rows, wide + 2 * HD :] = output[half * wide : (half + 1) * wide, :].astype(F32).T.astype(BF16)
 
-    out[rows:, :rows] = gains[...]
+    one, two = one_gain[...].astype(F32)[None], two_gain[...].astype(F32)[None]
+    first = lax.broadcasted_iota(jnp.int32, (16, rows), 0) == 0
+    out[rows:, :rows] = jnp.where(first, one, two).astype(BF16)
+    out[rows:, rows:] = jnp.zeros((16, out.shape[1] - rows), BF16)
+    for copy in late:
+        copy.wait()
+
+
+def pack_feed_forward(index, *rest):
+    cotangent, out, down_out, cotangent_near, cotangent_far, gate, upper, down, sems = rest[3:]
+    copies = fetch(rest[:3], (gate, upper, down), sems)
+    late = halves(index[0], cotangent, (cotangent_near, cotangent_far), sems, len(copies))
+    for copy in copies:
+        copy.wait()
+    rows, hidden = gate.shape[0], gate.shape[1] // 2
+    main = hidden // 128 * 128
+    both, wide = 2 * main, 2 * hidden
+    low = lanes((rows, 128)) < HD
+    for half in range(2):
+
+        @pl.when(index[3] == half)
+        def _():
+            tails = []
+            for at, part in enumerate((gate, upper)):
+                if half:
+                    part = pltpu.roll(part[:, main:].astype(F32), main + HD, 1)
+                else:
+                    part = part[:, : main + 128].astype(F32)
+                out[:, at * main : (at + 1) * main] = part[:, :main].astype(BF16)
+                tails.append(part[:, main:])
+            out[:, both:wide] = jnp.where(low, tails[0], pltpu.roll(tails[1], HD, 1)).astype(BF16)
+            turned = down[half * hidden : (half + 1) * hidden, :].astype(F32)
+            turned = jnp.concatenate([turned, jnp.zeros((HD, rows), F32)]).T
+            down_out[...] = turned.astype(BF16)
+    for copy in late:
+        copy.wait()
 
 
 def unpack_attention(index, mine, other, query, key, value, output):
@@ -357,47 +507,37 @@
                 down[at * hidden : (at + 1) * hidden, :] = turned[:hidden]
 
 
-def call(kernel, outs, args, scratch=()):
-    vmem = pl.BlockSpec(memory_space=pltpu.VMEM)
+def unpack_rows(index, near, far, rows):
+    block = near.shape[1]
+    for kk, part in enumerate((near, far)):
+        for yy in range(2):
+            to = pl.multiple_of(((index[0] ^ (2 * yy + kk)) & 3) * block, block)
+            rows[pl.ds(to, block), :] = part[yy].astype(rows.dtype)
+
+
+def call(kernel, outs, args, scratch=(), limit=48, fetched=0, cost=0):
+    vmem, hbm = pl.BlockSpec(memory_space=pltpu.VMEM), pl.BlockSpec(memory_space=pl.ANY)
+    kinds = [
+        pl.BlockSpec(memory_space=pltpu.SMEM)
+        if arg.dtype == jnp.int32
+        else hbm
+        if fetched
+        else vmem
+        for arg in args
+    ]
+    scratch = [pltpu.VMEM(shape, kind) for shape, kind in scratch]
+    if fetched:
+        scratch += [pltpu.VMEM(arg.shape, arg.dtype) for arg in args[1 : 1 + fetched]]
+        scratch += [pltpu.SemaphoreType.DMA((fetched + 4,))]
     return pl.pallas_call(
         kernel,
         out_shape=[jax.ShapeDtypeStruct(shape, kind) for shape, kind in outs],
-        in_specs=[pl.BlockSpec(memory_space=pltpu.SMEM) if arg.dtype == jnp.int32 else vmem for arg in args],
+        in_specs=kinds,
         out_specs=[vmem] * len(outs),
-        scratch_shapes=[pltpu.VMEM(shape, kind) for shape, kind in scratch],
-        compiler_params=pltpu.CompilerParams(vmem_limit_bytes=48 * 2**20),
-        cost_estimate=pl.CostEstimate(flops=1000, bytes_accessed=1000, transcendentals=0),
+        scratch_shapes=scratch,
+        compiler_params=pltpu.CompilerParams(vmem_limit_bytes=limit * 2**20),
+        cost_estimate=pl.CostEstimate(flops=1000 + cost * 10**9, bytes_accessed=1000, transcendentals=0),
     )(*args)
-
-
-def down_product(activated, f, part_low, part_high):
-    wide = f.shape[1] - activated.shape[1]
-    half = part_low.shape[0]
-    part_low[...] = nt(activated[:half, :], f[:, wide:]).astype(BF16)
-    part_high[...] = nt(activated[half:, :], f[:, wide:]).astype(BF16)
-
-
-def feed_forward_weights(unit, branch, gate_up, activated, out):
-    wide = gate_up.shape[1]
-    step = out.shape[0] // 2
-    for row in range(0, out.shape[0], step):
-        here = slice(row, row + step)
-        out[here, :wide] = tn(unit[:, here], gate_up[...]).astype(BF16)
-        out[here, wide:] = tn(branch[:, here], activated[...]).astype(BF16)
-
-
-def attention_weights(unit, back, a_low, a_high, mixed_rel, w, gains, out, gain_out):
-    wide = back.shape[1]
-    half = a_low.shape[0]
-    step = 256
-    for row in range(0, out.shape[0], step):
-        here = slice(row, row + step)
-        grad = tn(unit[:, here], back[...])
-        out[here, :wide] = grad.astype(BF16)
-        grad = jnp.sum(grad * w[here, :wide].astype(F32), axis=1, keepdims=True)
-        gain_out[:, here] = jnp.broadcast_to(grad, (step, 128)).T[:8] / gains[0:1, here]
-        o = tn(a_low[:, here], mixed_rel[:half, :]) + tn(a_high[:, here], mixed_rel[half:, :])
-        out[here, wide:] = o.astype(BF16)
 
 
 def shards(
@@ -425,214 +565,242 @@
 
     heads = query_weight.shape[1] // 2 // HD
     groups = key_weight.shape[1] // 2 // HD
-    group = heads // groups
+    lane = 2 * HD
     wide = (heads + 2 * groups) * HD
     rows = query_weight.shape[0]
-    gains = jnp.pad(jnp.stack([attention_gain, feedforward_gain]), ((0, 14), (0, 0)))
+    hidden = gate_weight.shape[1] // 2
+    main = hidden // 128 * 128
+    assert hidden - main == HD and heads * HD == lane and groups == 1
+    pack = 2 * hidden + main + lane
     own = ctx * 4 + why * 2 + core
     shard = lax.axis_index("fsdp")
+    size = lax.axis_size("fsdp")
     index = jnp.stack([own, length, shard, ctx]).astype(jnp.int32)
-    (attn_parts,) = call(
-        pack_attention,
-        [((rows + 16, wide + heads * HD), BF16)],
-        (index, query_weight, key_weight, value_weight, output_weight, gains),
-    )
-    size = lax.axis_size("fsdp")
-    if size > 4:
-        attn_parts = lax.all_gather(attn_parts, "fsdp")
+    flag = length > 0
+
+    attn_own, hidden_near, hidden_far = call(
+        prelude,
+        [((rows + 16, wide + lane), BF16)] + [((local // 2, width), BF16)] * 2,
+        (
+            index,
+            query_weight,
+            key_weight,
+            value_weight,
+            output_weight,
+            attention_gain,
+            feedforward_gain,
+            hidden_in,
+        ),
+        limit=60,
+        fetched=6,
+    )
+    hidden_other = swap(hidden_near, "ctx")
+    if near_shards():
+        attn_parts = direct([attn_own] * size)
+    else:
+        attn_parts = lax.all_gather(attn_own, "fsdp")
         gains = attn_parts[:, rows : rows + 8, :rows].astype(F32).transpose(1, 0, 2).reshape(8, -1)
-        attn_parts = [attn_parts[:, :rows].reshape(-1, wide + heads * HD), gains]
-    else:
-        attn_parts = gather_shards(attn_parts)
-    hidden = gate_weight.shape[1] // 2
-    main = hidden // 128 * 128
-    assert hidden - main == HD and 2 * heads * HD == 256 and groups == 1
-    gate_own, up_own = halve(gate_weight, ctx, 1), halve(up_weight, ctx, 1)
-    gu_own = jnp.concatenate([gate_own[:, :main], up_own[:, :main], gate_own[:, main:], up_own[:, main:]], 1)
-    down_own = jnp.concatenate([halve(down_weight, ctx, 0).T, jnp.zeros((rows, HD), BF16)], 1)
-
-    def relative(array, kk):
+        attn_parts = [attn_parts[:, :rows].reshape(-1, wide + lane), gains]
+
+    def prepare(positions, gate_weight, up_weight, down_weight, cotangent):
+        gu_own, down_own, *cotangent_rel = call(
+            pack_feed_forward,
+            [((rows, 2 * hidden), BF16), ((rows, main + lane), BF16)] + [((local // 2, width), BF16)] * 2,
+            (index, gate_weight, up_weight, down_weight, cotangent),
+            limit=60,
+            fetched=3,
+        )
         pieces = [
-            lax.dynamic_slice_in_dim(array, (2 * (why ^ yy) + (core ^ kk)) * block, block) for yy in range(2)
+            lax.dynamic_slice_in_dim(positions[0], (2 * (why ^ yy) + (core ^ kk)) * block, block)
+            for kk in range(2)
+            for yy in range(2)
         ]
-        return jnp.concatenate(pieces)
-
-    def both_halves(array):
-        near = relative(array, 0)
-        other = swap(near, "ctx")
-        return near, other, relative(array, 1), swap(other, "core")
-
-    flag = length > 0
-
-    def prepare(hidden_in, positions):
-        hidden_rel = both_halves(hidden_in[0])
-        places = jnp.stack([relative(positions[0], kk) for kk in range(2)])
+        places = jnp.concatenate(pieces).reshape(2, -1)
         places = jnp.stack([places, swap(places, "ctx")], 1).reshape(-1)
         freqs = rope_base ** (-2.0 * jnp.arange(HD // 2, dtype=F32) / HD)
         angles = places.astype(F32)[:, None] * jnp.tile(freqs, 4)[None, :]
         cosine = jnp.cos(angles)
-        sine = jnp.sin(angles) * jnp.where(jnp.arange(2 * HD) % HD < HD // 2, -1.0, 1.0)[None, :]
-        return hidden_rel, cosine, sine
-
-    hidden_rel, cosine, sine = region(flag, prepare, hidden_in, positions)
-    attn_parts, hidden_rel = lax.optimization_barrier((attn_parts, hidden_rel))
-    cotangent_rel, _ = lax.optimization_barrier((relative(cotangent[0], 0), hidden_rel[1]))
-    cotangent_x = swap(cotangent_rel, "ctx")
-    ff_own, _ = lax.optimization_barrier((jnp.concatenate([gu_own, down_own], 1), hidden_rel[1]))
-    ff_full = lax.all_gather(ff_own, "fsdp", axis=0, tiled=True)
-    inputs = hidden_rel[0][:block].astype(F32)
+        sine = jnp.sin(angles) * jnp.where(jnp.arange(lane) % HD < HD // 2, -1.0, 1.0)[None, :]
+        return gu_own, down_own, cosine, sine, *cotangent_rel
+
+    gu_own, down_own, cosine, sine, cotangent_near, cotangent_far = region(
+        flag, prepare, positions, gate_weight, up_weight, down_weight, cotangent
+    )
+    attn_parts, gu_own, hidden_other, cotangent_near = together(attn_parts, gu_own, hidden_other, cotangent_near)
+    gu_full = lax.all_gather(gu_own, "fsdp", axis=0, tiled=True)
+    down_parts = [down_own]
+    if near_shards():
+        down_parts.append(onward(down_own))
+    else:
+        down_parts = [lax.all_gather(down_own, "fsdp", axis=0, tiled=True)]
+    hidden_rel = (hidden_near, hidden_other, hidden_far, swap(hidden_other, "core"))
+    cotangent_other = swap(cotangent_near, "ctx")
+    inputs = hidden_near[:block].astype(F32)
     inverse = lax.rsqrt(jnp.mean(inputs * inputs, axis=-1, keepdims=True) + epsilon)
-
     valid = (own * block + jnp.arange(block, dtype=jnp.int32) < length).astype(F32)[:, None]
-    upstream = cotangent_rel[:block].astype(F32) * valid
-
     query_row = jnp.tile(query_gain.astype(F32), 2)[None]
     key_row = jnp.concatenate([key_gain.astype(F32), jnp.ones((HD,), F32)])[None]
-    lane = 2 * HD
-    attn_full, gains, near, far, unit, query, key, value, raw, mixed, mixed_rel, total = call(
-        attention_forward,
-        [((width, wide + 2 * HD), BF16), ((8, width), F32)]
-        + [((every // 2, width), BF16)] * 2
-        + [((every, width), BF16)]
-        + [((every, lane), BF16)] * 3
-        + [((every, 2 * lane), F32), ((every, lane), F32), ((every, lane), BF16), ((every, lane), F32)],
-        (index, *hidden_rel, cosine, sine, query_row, key_row, *attn_parts),
-    )
+
+    def attend(hidden_rel, cosine, sine, query_row, key_row, attn_parts):
+        attn_full, gains, near, far, unit, query, key, value, raw, mixed, mixed_rel, total = call(
+            attention_forward,
+            [((width, wide + lane), BF16), ((8, width), F32)]
+            + [((every // 2, width), BF16)] * 2
+            + [((every, width), BF16)]
+            + [((every, lane), BF16)] * 3
+            + [((every, 2 * lane), F32), ((every, lane), F32), ((every, lane), BF16), ((every, lane), F32)],
+            (index, *hidden_rel, cosine, sine, query_row, key_row, *attn_parts),
+            cost=8,
+        )
+        return near, far, gains, unit, mixed_rel, (attn_full, query, key, value, raw, mixed, total)
+
+    near, far, gains, unit, mixed_rel, kept = region(
+        flag, attend, hidden_rel, cosine, sine, query_row, key_row, attn_parts
+    )
+    kept = kept + (cosine, sine, query_row, key_row)
+    near, down_parts = together(near, down_parts)
+    if near_shards():
+        down_parts.append(onward(down_parts[1]))
+    middle = region(flag, lambda near, far, inputs: inputs + sum_scatter(near, far), near, far, inputs)
     attention_scale, feedforward_scale = gains[0:1], gains[1:2]
-    kept = (attn_full, query, key, value, raw, mixed, total, cosine, sine, query_row, key_row)
-    near, cotangent_x = lax.optimization_barrier((near, cotangent_x))
-
-    def middle_of(near, far, inputs, feedforward_scale, cotangent_x, cotangent_in):
-        attention_branch = sum_scatter(near, far)
-        middle = inputs + attention_branch
+    middle, cotangent_other, down_parts = together(middle, cotangent_other, down_parts)
+    if near_shards():
+        down_parts.append(onward(down_parts[2]))
+
+    def spread(middle, feedforward_scale, cotangent_other, cotangent_near):
         inverse_two = lax.rsqrt(jnp.mean(middle * middle, axis=-1, keepdims=True) + epsilon)
-        unit_two_own = middle * inverse_two
-        unit_near, unit_far = gather_plane((unit_two_own * feedforward_scale).astype(BF16))
-        cotangent_far = relative(cotangent_in[0], 1), swap(cotangent_x, "core")
-        return attention_branch, middle, inverse_two, unit_near, unit_far, cotangent_far
-
-    attention_branch, middle, inverse_two, unit_near, unit_far, cotangent_far = region(
-        flag, middle_of, near, far, inputs, feedforward_scale, cotangent_x, cotangent
-    )
+        *unit_two, cotangent_last = gather_plane(
+            (middle * inverse_two * feedforward_scale).astype(BF16), cotangent_other
+        )
+        return inverse_two, unit_two, cotangent_last, cotangent_near[:block].astype(F32) * valid
+
+    inverse_two, unit_two, cotangent_last, upstream = region(
+        flag, spread, middle, feedforward_scale, cotangent_other, cotangent_near
+    )
+    if near_shards():
+        unit_two, down_parts = together(unit_two, down_parts)
     unit_two_own = middle * inverse_two
 
-    tail = main + 2 * HD
-    near, far, gate_up, activated, branch_low, unit_two = call(
+    cotangent_rel = (cotangent_near, cotangent_other, cotangent_far, cotangent_last)
+    down_full, back = call(
+        activated_gradient,
+        [((width, main + lane), BF16), ((every, main + lane), F32)],
+        (index, *cotangent_rel, *down_parts),
+    )
+    gu_full, back = together(gu_full, back)
+    near, far, ff_grad, activated = call(
         feed_forward,
-        [((every // 2, width), BF16)] * 2
-        + [((every, 2 * hidden), BF16), ((every, tail), BF16), ((every, width), BF16), ((every, width), BF16)],
-        (index, unit_near, unit_far, cotangent_rel, cotangent_x, *cotangent_far, ff_full),
-    )
-    (ff_grad,) = call(
-        feed_forward_weights, [((width, 2 * hidden + tail), BF16)], (unit_two, branch_low, gate_up, activated)
-    )
-    ff_grad, near = lax.optimization_barrier((ff_grad, near))
+        [((every // 2, width), BF16)] * 2 + [((width, pack), BF16), ((every, main + lane), BF16)],
+        (index, *unit_two, *cotangent_rel, back, gu_full),
+        [((every, 2 * hidden), BF16)],
+    )
+    ff_grad, near = together(ff_grad, near)
     ff_share = lax.psum_scatter(ff_grad, "fsdp", scatter_dimension=0, tiled=True)
 
-    def turn(near, far, activated, ff_full, unit_two_own, inverse_two, upstream, middle, kept, unit, mixed_rel):
+    def turn(near, far, unit_two_own, inverse_two, upstream, feedforward_scale, activated, down_full, middle, rest):
+        kept, unit, mixed_rel, gains, inputs = rest
         second = sum_scatter(near, far)
-        feedforward_gain_part = jnp.sum(second * unit_two_own, axis=0)
-        second = second * feedforward_scale
+        c = second * feedforward_scale
         middle_grad = upstream + inverse_two * (
-            second - unit_two_own * jnp.mean(second * unit_two_own, axis=-1, keepdims=True)
+            c - unit_two_own * jnp.mean(c * unit_two_own, axis=-1, keepdims=True)
         )
-        attention_near, attention_far = gather_plane(middle_grad.astype(BF16))
-        near, far = call(down_product, [((every // 2, width), BF16)] * 2, (activated, ff_full))
-        feedforward_branch = sum_scatter(near, far)
+        *attention_grad, _ = gather_plane(middle_grad.astype(BF16))
+        branch_near, branch_far = call(
+            down_product, [((every // 2, width), BF16)] * 2, (index, activated, down_full)
+        )
+        feedforward_branch = sum_scatter(branch_near, branch_far)
         output = ((middle + feedforward_branch) * valid).astype(BF16)
-        block_rows = gather_rows(output, why, core)
-        near, far, back, gain_sums = call(
+        near, far, back, head_sums = call(
             attention_backward,
             [((every // 2, width), BF16)] * 2 + [((every, 2 * lane), BF16), ((8, lane), F32)],
-            (index, attention_near, attention_far, *kept),
+            (index, *attention_grad, *kept),
             [((every, lane), BF16)] + [((every, lane), F32)] * 3,
+            cost=12,
         )
-        attn_grad, attention_gain_part = call(
+        output_y = swap(output, "y")
+        attn_grad, attention_sums = call(
             attention_weights,
-            [((width, 3 * lane), BF16), ((8, width), F32)],
-            (unit, back, attention_near, attention_far, mixed_rel, kept[0], gains),
+            [((width, wide + lane), BF16), ((8, width), F32)],
+            (index, unit, back, *attention_grad, mixed_rel, kept[0], gains),
         )
-        feedforward_gain_part = jnp.stack([feedforward_gain_part, attention_gain_part[0]])
-        return near, far, attn_grad, gain_sums, block_rows, feedforward_branch, middle_grad, feedforward_gain_part
-
-    near, far, attn_grad, gain_sums, block_rows, feedforward_branch, middle_grad, gain_parts = region(
+        (small,) = call(
+            small_sums,
+            [((24, lane), F32)],
+            (index, inputs, middle, feedforward_branch, second, inverse_two, gains, attention_sums, head_sums),
+        )
+        near, output_y = together(near, output_y)
+        return near, far, attn_grad, small, jnp.stack([output, output_y]), middle_grad
+
+    near, far, attn_grad, small, output, middle_grad = region(
         flag,
         turn,
         near,
         far,
-        activated,
-        ff_full,
         unit_two_own,
         inverse_two,
         upstream,
+        feedforward_scale,
+        activated,
+        down_full,
         middle,
-        kept,
-        unit,
-        mixed_rel,
+        (kept, unit, mixed_rel, gains, inputs),
     )
     attn_share = lax.psum_scatter(attn_grad, "fsdp", scatter_dimension=0, tiled=True)
-    ff_share, near = lax.optimization_barrier((ff_share, near))
+    near, ff_share = together(near, ff_share)
+    output_core = swap(output, "core")
+    first, small = region(flag, last_sums, near, far, small)
+    first, ff_share, output_core = together(first, ff_share, output_core)
     ff_other = swap(ff_share, "ctx")
 
-    def sums(near, far, inputs, gain_parts, gain_sums, branches):
-        squares = jnp.stack([jnp.sum(item * item * valid) for item in (inputs, *branches)])
-        small = jnp.concatenate(
-            [
-                gain_parts.reshape(-1),
-                gain_sums[0, :HD] + gain_sums[0, HD:],
-                gain_sums[1, :HD],
-                squares,
-                jnp.sum(valid)[None],
-                jnp.zeros((123,), F32),
-            ]
-        )
-        return sum_scatter(near, far), sum_all(small.reshape(-1, 128)).reshape(-1)
-
-    first, small = region(
-        flag, sums, near, far, inputs, gain_parts, gain_sums, (attention_branch, middle, feedforward_branch)
-    )
-    first, attn_share, ff_other = lax.optimization_barrier((first, attn_share, ff_other))
+    def finish(first, middle_grad, inputs, inverse, attention_scale, small):
+        unit_own = inputs * inverse
+        c = first * attention_scale
+        input_grad = middle_grad + inverse * (c - unit_own * jnp.mean(c * unit_own, axis=-1, keepdims=True))
+        input_grad = input_grad.astype(BF16)
+        other, more = together(swap(input_grad, "y"), hop(small, "fsdp"))
+        return jnp.stack([input_grad, other]), small + more
+
+    pair, small = region(flag, finish, first, middle_grad, inputs, inverse, attention_scale, small)
+    pair, attn_share = together(pair, attn_share)
     attn_other = swap(attn_share, "ctx")
 
-    def finish(first, middle_grad, inputs, inverse, attention_scale, index, ff_share, ff_other):
-        unit_own = inputs * inverse
-        first = first * attention_scale
-        input_grad = middle_grad + inverse * (
-            first - unit_own * jnp.mean(first * unit_own, axis=-1, keepdims=True)
-        )
-        ff_grads = call(
-            unpack_feed_forward,
-            [((rows, 2 * hidden), F32)] * 2 + [((2 * hidden, rows), F32)],
-            (index, ff_share, ff_other),
-        )
-        return gather_rows(input_grad.astype(BF16), why, core).astype(F32), ff_grads
-
-    input_rows, ff_grads = region(
-        flag, finish, first, middle_grad, inputs, inverse, attention_scale, index, ff_share, ff_other
-    )
-    attn_other, input_rows = lax.optimization_barrier((attn_other, input_rows))
+    def unpack(index, pair, output, output_core, small, shard):
+        step = 2
+        while step < lax.axis_size("fsdp"):
+            small = small + hop(small, "fsdp", step)
+            step *= 2
+        pair_core, small = together(swap(pair, "core"), small)
+        (block_rows,) = call(unpack_rows, [((local, width), BF16)], (index, output, output_core))
+        (input_rows,) = call(unpack_rows, [((local, width), F32)], (index, pair, pair_core))
+        own_gain = attention_gain.shape[0]
+        flat = small[:16].reshape(2, -1)
+        shares = lax.dynamic_slice_in_dim(flat, shard * own_gain, own_gain, 1)
+        stats = jnp.sqrt(small[17, :4] / (small[17, 4] * width))
+        return input_rows, block_rows, shares, small[16, :HD], small[16, HD:], stats
+
+    input_rows, block_rows, shares, query_share, key_share, stats = region(
+        flag, unpack, index, pair, output, output_core, small, shard
+    )
+    ff_other, attn_other, input_rows = together(ff_other, attn_other, input_rows)
+    ff_grads = call(
+        unpack_feed_forward,
+        [((rows, 2 * hidden), F32)] * 2 + [((2 * hidden, rows), F32)],
+        (index, ff_share, ff_other),
+    )
     attn_grads = call(
         unpack_attention,
-        [((rows, 2 * heads * HD), F32)] + [((rows, 2 * groups * HD), F32)] * 2 + [((2 * heads * HD, rows), F32)],
+        [((rows, 2 * lane), F32)] + [((rows, lane), F32)] * 2 + [((2 * lane, rows), F32)],
         (index, attn_share, attn_other),
     )
-    own_gain = attention_gain.shape[0]
-    shard = shard * own_gain
-    feedforward_share = lax.dynamic_slice_in_dim(small, shard, own_gain)
-    attention_share = lax.dynamic_slice_in_dim(small, width + shard, own_gain)
-    rest = small[2 * width :]
-    query_gain_total, key_gain_total = rest[:HD], rest[HD : 2 * HD]
-    stats = jnp.sqrt(rest[2 * HD : 2 * HD + 4] / (rest[2 * HD + 4] * width))
-
     return (
         block_rows[None],
         input_rows[None],
         *attn_grads,
         *ff_grads,
-        attention_share,
-        feedforward_share,
-        query_gain_total,
-        key_gain_total,
+        shares[1],
+        shares[0],
+        query_share,
+        key_share,
         stats,
     )
 

time: 286 us -> 258 us (0.902)
  waiting for transfers between devices: 115 us -> 78.3 us
  Pallas kernels: 51.7 us -> 62.1 us
  local copies, waits for them, and re-layouts: 21.7 us -> 11.5 us
  starting transfers between devices: 47.7 us -> 51.6 us
    ppermute x44 -> x41, waiting for transfers between devices: 87.9 us -> 58.7 us  [swap(): return lax.ppermute(value, axis, [(0, 1), (1, 0)])]
    all_gather x1, waiting for transfers between devices: 19.2 us -> 0.02 us  [shards(): gu_full = lax.all_gather(gu_own, 'fsdp', axis=0, tiled=True)]
    ppermute x5 -> x11, waiting for transfers between devices: 7.33 us -> 19.5 us  [the longest x5 12.3 us: hop(): return lax.ppermute(value, axis, [(i, i ^ step) for i in range(size)])]
    pallas_call x9 -> x13, Pallas kernels: 51.7 us -> 62.1 us  [call(): pl.pallas_call(kernel, out_shape=[jax.ShapeDtypeStruct(shape, kind) for s...]
    ppermute x5 -> x11, starting transfers between devices: 6.72 us -> 13.5 us  [the longest x5 6.49 us: hop(): return lax.ppermute(value, axis, [(i, i ^ step) for i in range(size)])]
    concatenate x2 -> x0, local copies, waits for them, and re-layouts: 5.25 us -> none  [the longest x1 3.31 us: sums(): jnp.concatenate([gain_parts.reshape(-1), gain_sums[0, :HD] + gain_sums[0,...]
    add x4 -> x9, other arithmetic: 0.02 us -> 3.78 us  [the longest x1 1.9 us: shards(): inputs + sum_scatter(near, far)]
    dynamic_slice x6 -> x2, local copies, waits for them, and re-layouts: 4.08 us -> 0.74 us  [the longest x1 0.73 us: prepare(): lax.dynamic_slice_in_dim(positions[0], (2 * (why ^ yy) + (core ^ kk)) * b...]
  transfers between devices with their start and end apart: 52 -> 55, of which waited for: 33 -> 33; matrix products, arithmetic and copies ran while one was open for 12% -> 11% of each run, Pallas kernels for 10% -> 16%
where the time goes in v3:
time: 258 us; the launch traced here: 253 us
  waiting for transfers between devices  78.3 us (30%)
  Pallas kernels  62.1 us (24%)
  starting transfers between devices  51.6 us (20%)
  other arithmetic  23.3 us (9%)
  between operations  15 us (6%)
  loops' own time  11.6 us (4%)
  local copies, waits for them, and re-layouts  11.5 us (4%)
    pallas_call x13, Pallas kernels, call(): pl.pallas_call(kernel, out_shape=[jax.ShapeDtypeStruct(shape, kind) for s...  62.1 us
    ppermute x41, waiting for transfers between devices, swap(): return lax.ppermute(value, axis, [(0, 1), (1, 0)])  58.7 us
    ppermute x41, starting transfers between devices, swap(): return lax.ppermute(value, axis, [(0, 1), (1, 0)])  38 us
    ppermute x5, waiting for transfers between devices, hop(): return lax.ppermute(value, axis, [(i, i ^ step) for i in range(size)])  12.3 us
    another operation x8, loops' own time, region(): lax.cond(flag, work, lambda *_: jax.tree.map(lambda x: jnp.zeros(x.shape,...  11.6 us
    ppermute x3, waiting for transfers between devices, direct(): lax.ppermute(piece, 'fsdp', [(i, i ^ step) for i in range(size)])  7.13 us
    ppermute x5, starting transfers between devices, hop(): return lax.ppermute(value, axis, [(i, i ^ step) for i in range(size)])  6.49 us
    unnamed x54, local copies, waits for them, and re-layouts  5.29 us
  transfers between devices with their start and end apart: 55, of which 33 were waited for; matrix products, arithmetic and copies ran while one was open for 11% of the time, Pallas kernels for 16%

profile of v3, /device:TPU:0, one launch (start us, length us, event | category | flops | bytes accessed | tf_op | source)
XLA Modules:
  0.0 253.2 jit_solution(13139782747836737701)
XLA Ops:
  13.8 3.6 %collective-permute-start.42 = (bf16[272,384]{1,0:T(8,128)(2,1)S(1)}, bf16[272,384]{1,0:T(8,128)(2,1)S(1)}, u32[]{:S(2)}, u32[]{:S(2)}) collective-permute-start(bf16[272,384]{1,0:T(8,128)(2,1)S(1)} %get-tuple-element.387), channel_id=1, source_target_pairs={{0,24},{8,16},{16,8},{24,0},{1,25},{9,17},{17,9},{25,1},{2,26},{10... | collective-permute-start | bytes 626696 | tf_op jit(solution)/shard_map/ppermute | solution.py:89
  18.2 9.6 %conditional.8 = (bf16[256,1152]{1,0:T(8,128)(2,1)S(1)}, bf16[256,640]{1,0:T(8,128)(2,1)S(1)}, f32[1024,128]{1,0:T(8,128)S(1)}, f32[1024,128]{1,0:T(8,128)S(1)},...) conditional(s32[]{:T(128)} %convert_element_type.168, () %tuple.105, (s32[4]{0:T(128)S(1)}, ...), branch_computations={%region_0.0_spmd, %region_1.2_spmd} | conditional | flops 267808 | bytes 3014720 | solution.py:105
  19.4 3.1 %branch_1_fun.8 = (bf16[256,1152]{1,0:T(8,128)(2,1)S(1)}, bf16[256,640]{1,0:T(8,128)(2,1)S(1)}, bf16[256,1024]{1,0:T(8,128)(2,1)S(1)}, bf16[256,1024]{1,0:T(8,128)(2,1)}) custom-call(s32[4]{0:T(128)S(1)} %get-tuple-element.163.index, bf16[256,1152]{1,0:T(8,128)(2,1)} %get-tuple-element.477.rest_0_, bf16[256,1152]{1,0:T(8,128)(2,1)} %get-tuple-element.478.rest_1_, ...), custom_call_target="tpu_custom_call" | custom-call | flops 1000 | bytes 1000 | tf_op jit(solution)/shard_map/cond/branch_1_fun/pallas_call | solution.py:532
  22.6 3.3 %collective-permute-done = s32[2,256]{1,0:T(2,128)S(1)} collective-permute-done((s32[2,256]{1,0:T(2,128)S(1)}, s32[2,256]{1,0:T(2,128)S(1)}, u32[]{:S(2)}, u32[]{:S(2)}) %collective-permute-start) | collective-permute-done | bytes 2080 | tf_op jit(solution)/shard_map/cond/branch_1_fun/ppermute | solution.py:17
  27.9 7.1 %collective-permute-done.41 = bf16[272,384]{1,0:T(8,128)(2,1)} collective-permute-done((bf16[272,384]{1,0:T(8,128)(2,1)S(1)}, bf16[272,384]{1,0:T(8,128)(2,1)}, u32[]{:S(2)}, u32[]{:S(2)}) %collective-permute-start.41) | collective-permute-done | bytes 208928 | tf_op jit(solution)/shard_map/ppermute | solution.py:89
  37.4 11.0 %conditional.9 = (bf16[512,1024]{1,0:T(8,128)(2,1)S(1)}, bf16[512,1024]{1,0:T(8,128)(2,1)S(1)}, f32[8,1024]{1,0:T(8,128)}, bf16[1024,1024]{1,0:T(8,128)(2,1)}, b...) conditional(s32[]{:T(128)} %convert_element_type.168, ...), branch_computations={%region_2.3_spmd, %region_3.4_spmd} | conditional | flops 8000001024 | bytes 8167576 | solution.py:105
  38.6 9.0 %branch_1_fun.9 = (bf16[1024,384]{1,0:T(8,128)(2,1)}, f32[8,1024]{1,0:T(8,128)}, bf16[512,1024]{1,0:T(8,128)(2,1)S(1)}, bf16[512,1024]{1,0:T(8,128)(2,1)S(1)}, b...) custom-call(s32[4]{0:T(128)S(1)} %get-tuple-element.175.index, ...), custom_call_target="tpu_custom_call" | custom-call | flops 8000001024 | bytes 1000 | tf_op jit(solution)/shard_map/cond/branch_1_fun/pallas_call | solution.py:532
  50.4 20.6 %conditional.10 = (f32[128,1024]{1,0:T(8,128)}) conditional(s32[]{:T(128)} %convert_element_type.168, () %tuple.112, (bf16[512,1024]{1,0:T(8,128)(2,1)S(1)}, bf16[512,1024]{1,0:T(8,128)(2,1)S(1)}, f32[128,1024]{1,0:T(8,128)}) %tuple.114), branch_computations={%region_4.5_spmd, %region_5.6_spmd} | conditional | flops 2621440 | bytes 18612432 | solution.py:105
  55.6 6.3 %collective-permute-done.12 = bf16[2,128,512]{2,1,0:T(8,128)(2,1)S(1)} collective-permute-done((bf16[2,128,512]{2,1,0:T(8,128)(2,1)S(1)}, bf16[2,128,512]{2,1,0:T(8,128)(2,1)S(1)}, u32[]{:S(2)}, u32[]{:S(2)}) %collective-permute-start.12) | collective-permute-done | bytes 262176 | tf_op jit(solution)/shard_map/cond/branch_1_fun/ppermute | solution.py:17
  73.9 22.3 %conditional.11 = (f32[128,1]{0,1:T(1,128)S(1)}, bf16[512,1024]{1,0:T(8,128)(2,1)}, bf16[512,1024]{1,0:T(8,128)(2,1)}, bf16[256,1024]{1,0:T(8,128)(2,1)}, f32[128,1024]{1,0:T(8,128)S(1)}) conditional(s32[]{:T(128)} %convert_element_type.168, () %tuple.111, (f32[128,1024]{1,0:T(8,128)}, f32[1,1024]{1,0:T(1,128)S(1)}, bf16[256,1024]{1,0:T(8,128)(2,1)}, ...), branch_computations={%region_6.7_spmd, %region_7.9_spmd} | conditional | flops 5374080 | bytes 15998232 | solution.py:105
  86.2 5.5 %collective-permute-done.4 = bf16[2,128,512]{2,1,0:T(8,128)(2,1)S(1)} collective-permute-done((bf16[2,128,512]{2,1,0:T(8,128)(2,1)S(1)}, bf16[2,128,512]{2,1,0:T(8,128)(2,1)S(1)}, u32[]{:S(2)}, u32[]{:S(2)}) %collective-permute-start.4) | collective-permute-done | bytes 262176 | tf_op jit(solution)/shard_map/cond/branch_1_fun/ppermute | solution.py:17
  98.1 3.5 %shard_map.260 = (bf16[1024,640]{1,0:T(8,128)(2,1)}, f32[1024,640]{1,0:T(8,128)S(1)}) custom-call(s32[4]{0:T(128)S(1)} %pad_add_fusion.1.index, bf16[256,1024]{1,0:T(8,128)(2,1)} %copy-done.6, bf16[256,1024]{1,0:T(8,128)(2,1)} %collective-permute-done.46.b1, bf16[256,1024]{1,0:T(8,128)(2,1)} %get-tuple-element.410.b2, ...), custom_call_target="tpu_custom_call" | custom-call | flops 1000 | bytes 1000 | tf_op jit(solution)/shard_map/pallas_call | solution.py:532
  103.3 14.5 %shard_map.261 = (bf16[512,1024]{1,0:T(8,128)(2,1)}, bf16[512,1024]{1,0:T(8,128)(2,1)}, bf16[1024,1792]{1,0:T(8,128)(2,1)}, bf16[1024,640]{1,0:T(8,128)(2,1)}) custom-call(s32[4]{0:T(128)S(1)} %pad_add_fusion.1.index, bf16[512,1024]{1,0:T(8,128)(2,1)} %get-tuple-element.408.x_low, bf16[512,1024]{1,0:T(8,128)(2,1)} %get-tuple-element.409.x_high, ...), custom_call_target="tpu_custom_call" | custom-call | flops 1000 | bytes 1000 | tf_op jit(solution)/shard_map/pallas_call | solution.py:532
  119.6 76.2 %conditional.12 = (bf16[512,1024]{1,0:T(8,128)(2,1)}, bf16[512,1024]{1,0:T(8,128)(2,1)}, bf16[1024,384]{1,0:T(8,128)(2,1)}, f32[24,128]{1,0:T(8,128)S(1)}, bf16[...) conditional(s32[]{:T(128)} %convert_element_type.168, () %tuple.110, (f32[128,1]{0,1:T(1,128)S(1)}, ...), branch_computations={%region_9.10_spmd, %region_10.12_spmd} | conditional | flops 12011669504 | bytes 65815716 | solution.py:105
  129.8 3.1 %branch_1_fun.11 = (bf16[512,1024]{1,0:T(8,128)(2,1)S(1)}, bf16[512,1024]{1,0:T(8,128)(2,1)S(1)}) custom-call(s32[4]{0:T(128)S(1)} %get-tuple-element.211.index, bf16[1024,640]{1,0:T(8,128)(2,1)} %get-tuple-element.230.activated, bf16[1024,640]{1,0:T(8,128)(2,1)S(1)} %get-tuple-element.231.down_w), custom_call_target="tpu_custom_call" | custom-call | flops 1000 | bytes 1000 | tf_op jit(solution)/shard_map/cond/branch_1_fun/pallas_call | solution.py:532
  139.4 3.7 %collective-permute-done.25 = bf16[2,128,512]{2,1,0:T(8,128)(2,1)S(1)} collective-permute-done((bf16[2,128,512]{2,1,0:T(8,128)(2,1)S(1)}, bf16[2,128,512]{2,1,0:T(8,128)(2,1)S(1)}, u32[]{:S(2)}, u32[]{:S(2)}) %collective-permute-start.25) | collective-permute-done | bytes 262176 | tf_op jit(solution)/shard_map/cond/branch_1_fun/ppermute | solution.py:17
  168.8 3.1 %collective-permute-done.32 = bf16[2,128,512]{2,1,0:T(8,128)(2,1)S(1)} collective-permute-done((bf16[2,128,512]{2,1,0:T(8,128)(2,1)S(1)}, bf16[2,128,512]{2,1,0:T(8,128)(2,1)S(1)}, u32[]{:S(2)}, u32[]{:S(2)}) %collective-permute-start.32) | collective-permute-done | bytes 262176 | tf_op jit(solution)/shard_map/cond/branch_1_fun/ppermute | solution.py:17
  177.4 12.3 %branch_1_fun.10 = (bf16[512,1024]{1,0:T(8,128)(2,1)}, bf16[512,1024]{1,0:T(8,128)(2,1)}, bf16[1024,256]{1,0:T(8,128)(2,1)S(1)}, f32[8,128]{1,0:T(8,128)S(1)}) custom-call(s32[4]{0:T(128)S(1)} %get-tuple-element.211.index, bf16[512,1024]{1,0:T(8,128)(2,1)S(1)} %bitcast.175, bf16[512,1024]{1,0:T(8,128)(2,1)S(1)} %collective-permute-done.33.a_high, ...), custom_call_target="tpu_custom_call" | custom-call | flops 12000001024 | bytes 1000 | tf_op jit(solution)/shard_map/cond/branch_1_fun/pallas_call | solution.py:532
  190.6 3.3 %branch_1_fun.12 = (bf16[1024,384]{1,0:T(8,128)(2,1)}, f32[8,1024]{1,0:T(8,128)S(1)}) custom-call(s32[4]{0:T(128)S(1)} %get-tuple-element.211.index, bf16[1024,1024]{1,0:T(8,128)(2,1)S(1)} %copy-done.5, bf16[1024,256]{1,0:T(8,128)(2,1)S(1)} %get-tuple-element.238.back, bf16[512,1024]{1,0:T(8,128)(2,1)S(1)} %bitcast.176, ...), custom_call_target="tpu_custom_call" | custom-call | flops 1000 | bytes 1000 | tf_op jit(solution)/shard_map/cond/branch_1_fun/pallas_call | solution.py:532
  196.0 21.1 %conditional.13 = (f32[128,1024]{1,0:T(8,128)S(1)}, f32[24,128]{1,0:T(8,128)S(1)}) conditional(s32[]{:T(128)} %convert_element_type.168, () %tuple.109, (bf16[512,1024]{1,0:T(8,128)(2,1)}, bf16[512,1024]{1,0:T(8,128)(2,1)}, f32[24,128]{1,0:T(8,128)S(1)}) %tuple.122), branch_computations={%region_13.14_spmd, %region_14.15_spmd} | conditional | flops 2499584 | bytes 18346320 | solution.py:105
  204.0 5.9 %collective-permute-done.20 = f32[24,128]{1,0:T(8,128)S(1)} collective-permute-done((f32[24,128]{1,0:T(8,128)S(1)}, f32[24,128]{1,0:T(8,128)S(1)}, u32[]{:S(2)}, u32[]{:S(2)}) %collective-permute-start.20) | collective-permute-done | bytes 12320 | tf_op jit(solution)/shard_map/cond/branch_1_fun/ppermute | solution.py:47
  214.0 3.1 %collective-permute-done.23 = f32[24,128]{1,0:T(8,128)S(1)} collective-permute-done((f32[24,128]{1,0:T(8,128)S(1)}, f32[24,128]{1,0:T(8,128)S(1)}, u32[]{:S(2)}, u32[]{:S(2)}) %collective-permute-start.23) | collective-permute-done | bytes 12320 | tf_op jit(solution)/shard_map/cond/branch_1_fun/ppermute | solution.py:47
  218.8 10.3 %conditional.14 = (bf16[2,128,1024]{2,1,0:T(8,128)(2,1)S(1)}, f32[24,128]{1,0:T(8,128)S(1)}) conditional(s32[]{:T(128)} %convert_element_type.168, () %tuple.103, (f32[128,1024]{1,0:T(8,128)}, f32[1,1024]{1,0:T(1,128)S(1)}, f32[128,1024]{1,0:T(8,128)S(1)}, f32[128,1024]{1,0:T(8,128)}, f32[24,128]{1,0:T(8,128)S(1)}) %tuple.124), branch_computations={%region_15.16_spmd, %region_16.19_spmd} | conditional | flops 1969280 | bytes 5603936 | solution.py:105
  229.9 10.0 %conditional.15 = (f32[512,1024]{1,0:T(8,128)}, bf16[2,256]{1,0:T(2,128)(2,1)S(1)}, f32[64]{0:T(128)S(1)}, f32[64]{0:T(128)S(1)}, f32[4]{0:T(128)S(1)}, /*index=...) conditional(s32[]{:T(128)} %convert_element_type.168, ...), branch_computations={%region_20.21_spmd, %region_21.22_spmd} | conditional | flops 5082 | bytes 3151494 | solution.py:105
  (266 shorter events, 136.2 us)
Async XLA Ops:
  7.2 94.5 %all-gather.2.cloned.1.call-start = ((), (), s32[]{:S(2)}) async-start(), calls=%async_computation.2 | async-start | bytes 2949120 | tf_op jit(solution)/shard_map/all_gather | solution.py:630
  10.8 24.2 %collective-permute-start.43 = (bf16[256,1024]{1,0:T(8,128)(2,1)S(1)}, bf16[256,1024]{1,0:T(8,128)(2,1)}, u32[]{:S(2)}, u32[]{:S(2)}) collective-permute-start(bf16[256,1024]{1,0:T(8,128)(2,1)S(1)} %get-tuple-element.379), channel_id=1, source_target_pairs={{0,4},{4,0},{1,5},{5,1},{2,6},{6,2},{3,7},{7,3},{8,12},{12,8},{9,1... | collective-permute-start | bytes 1572872 | tf_op jit(solution)/shard_map/ppermute | solution.py:17
  13.8 14.0 %collective-permute-start.42 = (bf16[272,384]{1,0:T(8,128)(2,1)S(1)}, bf16[272,384]{1,0:T(8,128)(2,1)S(1)}, u32[]{:S(2)}, u32[]{:S(2)}) collective-permute-start(bf16[272,384]{1,0:T(8,128)(2,1)S(1)} %get-tuple-element.387), channel_id=1, source_target_pairs={{0,24},{8,16},{16,8},{24,0},{1,25},{9,17},{17,9},{25,1},{2,26},{10... | collective-permute-start | bytes 626696 | tf_op jit(solution)/shard_map/ppermute | solution.py:89
  17.4 17.6 %collective-permute-start.41 = (bf16[272,384]{1,0:T(8,128)(2,1)S(1)}, bf16[272,384]{1,0:T(8,128)(2,1)}, u32[]{:S(2)}, u32[]{:S(2)}) collective-permute-start(bf16[272,384]{1,0:T(8,128)(2,1)S(1)} %get-tuple-element.387), channel_id=1, source_target_pairs={{0,16},{8,24},{16,0},{24,8},{1,17},{9,25},{17,1},{25,9},{2,18},{10... | collective-permute-start | bytes 626696 | tf_op jit(solution)/shard_map/ppermute | solution.py:89
  17.4 17.6 %collective-permute-start.40 = (bf16[272,384]{1,0:T(8,128)(2,1)S(1)}, bf16[272,384]{1,0:T(8,128)(2,1)}, u32[]{:S(2)}, u32[]{:S(2)}) collective-permute-start(bf16[272,384]{1,0:T(8,128)(2,1)S(1)} %get-tuple-element.387), channel_id=1, source_target_pairs={{0,8},{8,0},{16,24},{24,16},{1,9},{9,1},{17,25},{25,17},{2,10},{10... | collective-permute-start | bytes 626696 | tf_op jit(solution)/shard_map/ppermute | solution.py:89
  35.0 161.0 %reduce-scatter.3.cloned.1.call-start = ((), (), s32[]{:S(2)}) async-start(), calls=%async_computation.3 | async-start | bytes 4587520 | tf_op jit(solution)/shard_map/reduce_scatter | solution.py:698
  35.2 13.3 %collective-permute-start.45 = (bf16[256,640]{1,0:T(8,128)(2,1)S(1)}, bf16[256,640]{1,0:T(8,128)(2,1)S(1)}, u32[]{:S(2)}, u32[]{:S(2)}) collective-permute-start(bf16[256,640]{1,0:T(8,128)(2,1)S(1)} %get-tuple-element.413.rest_0_), channel_id=1, source_target_pairs={{0,8},{8,16},{16,24},{24,0},{1,9},{9,17},{17,25},{25,1},{2,10},{10... | collective-permute-start | bytes 983048 | tf_op jit(solution)/shard_map/ppermute | solution.py:96
  35.2 35.7 %collective-permute-start.46 = (bf16[256,1024]{1,0:T(8,128)(2,1)S(1)}, bf16[256,1024]{1,0:T(8,128)(2,1)}, u32[]{:S(2)}, u32[]{:S(2)}) collective-permute-start(bf16[256,1024]{1,0:T(8,128)(2,1)S(1)} %get-tuple-element.396.b0), channel_id=1, source_target_pairs={{0,4},{4,0},{1,5},{5,1},{2,6},{6,2},{3,7},{7,3},{8,12},{12,8},{9,1... | collective-permute-start | bytes 1572872 | tf_op jit(solution)/shard_map/ppermute | solution.py:17
  48.5 22.4 %collective-permute-start.47 = (bf16[256,640]{1,0:T(8,128)(2,1)S(1)}, bf16[256,640]{1,0:T(8,128)(2,1)S(1)}, u32[]{:S(2)}, u32[]{:S(2)}) collective-permute-start(bf16[256,640]{1,0:T(8,128)(2,1)S(1)} %collective-permute-done.45.rest_1_), channel_id=1, source_target_pairs={{0,8},{8,16},{16,24},{24,0},{1,9},{9,17},{17,25},{25,1},{2,10},{10... | collective-permute-start | bytes 983048 | tf_op jit(solution)/shard_map/ppermute | solution.py:96
  53.5 8.4 %collective-permute-start.12 = (bf16[2,128,512]{2,1,0:T(8,128)(2,1)S(1)}, bf16[2,128,512]{2,1,0:T(8,128)(2,1)S(1)}, u32[]{:S(2)}, u32[]{:S(2)}) collective-permute-start(bf16[2,128,512]{2,1,0:T(8,128)(2,1)S(1)} %slice_bitcast_fusion.5), channel_id=1, source_target_pairs={{0,4},{4,0},{1,5},{5,1},{2,6},{6,2},{3,7},{7,3},{8,12},{12,8},{9,1... | collective-permute-start | bytes 786440 | tf_op jit(solution)/shard_map/cond/branch_1_fun/ppermute | solution.py:17
  54.1 8.1 %collective-permute-start.14 = (bf16[2,128,512]{2,1,0:T(8,128)(2,1)S(1)}, bf16[2,128,512]{2,1,0:T(8,128)(2,1)S(1)}, u32[]{:S(2)}, u32[]{:S(2)}) collective-permute-start(bf16[2,128,512]{2,1,0:T(8,128)(2,1)S(1)} %slice_bitcast_fusion.3), channel_id=1, source_target_pairs={{0,2},{2,0},{1,3},{3,1},{4,6},{6,4},{5,7},{7,5},{8,10},{10,8},{9,1... | collective-permute-start | bytes 786440 | tf_op jit(solution)/shard_map/cond/branch_1_fun/ppermute | solution.py:17
  70.9 25.3 %collective-permute-start.48 = (bf16[256,640]{1,0:T(8,128)(2,1)S(1)}, bf16[256,640]{1,0:T(8,128)(2,1)S(1)}, u32[]{:S(2)}, u32[]{:S(2)}) collective-permute-start(bf16[256,640]{1,0:T(8,128)(2,1)S(1)} %collective-permute-done.47.rest_2_), channel_id=1, source_target_pairs={{0,8},{8,16},{16,24},{24,0},{1,9},{9,17},{17,25},{25,1},{2,10},{10... | collective-permute-start | bytes 983048 | tf_op jit(solution)/shard_map/ppermute | solution.py:96
  74.2 9.7 %collective-permute-start.1 = (bf16[256,1024]{1,0:T(8,128)(2,1)}, bf16[256,1024]{1,0:T(8,128)(2,1)}, u32[]{:S(2)}, u32[]{:S(2)}) collective-permute-start(bf16[256,1024]{1,0:T(8,128)(2,1)} %get-tuple-element.205), channel_id=1, source_target_pairs={{0,1},{1,0},{2,3},{3,2},{4,5},{5,4},{6,7},{7,6},{8,9},{9,8},{10,11... | collective-permute-start | bytes 1572872 | tf_op jit(solution)/shard_map/cond/branch_1_fun/ppermute | solution.py:17
  117.9 111.2 %reduce-scatter.5.cloned.1.call-start = ((), (), s32[]{:S(2)}) async-start(), calls=%async_computation.4 | async-start | bytes 983040 | tf_op jit(solution)/shard_map/reduce_scatter | solution.py:748
  133.9 9.2 %collective-permute-start.25 = (bf16[2,128,512]{2,1,0:T(8,128)(2,1)S(1)}, bf16[2,128,512]{2,1,0:T(8,128)(2,1)S(1)}, u32[]{:S(2)}, u32[]{:S(2)}) collective-permute-start(bf16[2,128,512]{2,1,0:T(8,128)(2,1)S(1)} %slice_bitcast_fusion.19), channel_id=1, source_target_pairs={{0,4},{4,0},{1,5},{5,1},{2,6},{6,2},{3,7},{7,3},{8,12},{12,8},{9,1... | collective-permute-start | bytes 786440 | tf_op jit(solution)/shard_map/cond/branch_1_fun/ppermute | solution.py:17
  135.6 9.3 %collective-permute-start.27 = (bf16[2,128,512]{2,1,0:T(8,128)(2,1)S(1)}, bf16[2,128,512]{2,1,0:T(8,128)(2,1)S(1)}, u32[]{:S(2)}, u32[]{:S(2)}) collective-permute-start(bf16[2,128,512]{2,1,0:T(8,128)(2,1)S(1)} %slice_bitcast_fusion.17), channel_id=1, source_target_pairs={{0,2},{2,0},{1,3},{3,1},{4,6},{6,4},{5,7},{7,5},{8,10},{10,8},{9,1... | collective-permute-start | bytes 786440 | tf_op jit(solution)/shard_map/cond/branch_1_fun/ppermute | solution.py:17
  137.5 11.2 %collective-permute-start.35 = (bf16[2,128,512]{2,1,0:T(8,128)(2,1)S(1)}, bf16[2,128,512]{2,1,0:T(8,128)(2,1)S(1)}, u32[]{:S(2)}, u32[]{:S(2)}) collective-permute-start(bf16[2,128,512]{2,1,0:T(8,128)(2,1)S(1)} %slice_bitcast_fusion.15), channel_id=1, source_target_pairs={{0,4},{4,0},{1,5},{5,1},{2,6},{6,2},{3,7},{7,3},{8,12},{12,8},{9,1... | collective-permute-start | bytes 786440 | tf_op jit(solution)/shard_map/cond/branch_1_fun/ppermute | solution.py:17
  138.0 12.5 %collective-permute-start.37 = (bf16[2,128,512]{2,1,0:T(8,128)(2,1)S(1)}, bf16[2,128,512]{2,1,0:T(8,128)(2,1)S(1)}, u32[]{:S(2)}, u32[]{:S(2)}) collective-permute-start(bf16[2,128,512]{2,1,0:T(8,128)(2,1)S(1)} %slice_bitcast_fusion.13), channel_id=1, source_target_pairs={{0,2},{2,0},{1,3},{3,1},{4,6},{6,4},{5,7},{7,5},{8,10},{10,8},{9,1... | collective-permute-start | bytes 786440 | tf_op jit(solution)/shard_map/cond/branch_1_fun/ppermute | solution.py:17
  174.9 14.9 %collective-permute-start.39 = (bf16[128,1024]{1,0:T(8,128)(2,1)}, bf16[128,1024]{1,0:T(8,128)(2,1)S(1)}, u32[]{:S(2)}, u32[]{:S(2)}) collective-permute-start(bf16[128,1024]{1,0:T(8,128)(2,1)} %get-tuple-element.568), channel_id=1, source_target_pairs={{0,2},{2,0},{1,3},{3,1},{4,6},{6,4},{5,7},{7,5},{8,10},{10,8},{9,1... | collective-permute-start | bytes 786440 | tf_op jit(solution)/shard_map/cond/branch_1_fun/ppermute | solution.py:17
  195.8 21.4 %collective-permute-start.49 = (bf16[2,128,1024]{2,1,0:T(8,128)(2,1)}, bf16[2,128,1024]{2,1,0:T(8,128)(2,1)S(1)}, u32[]{:S(2)}, u32[]{:S(2)}) collective-permute-start(bf16[2,128,1024]{2,1,0:T(8,128)(2,1)} %get-tuple-element.444), channel_id=1, source_target_pairs={{0,1},{1,0},{2,3},{3,2},{4,5},{5,4},{6,7},{7,6},{8,9},{9,8},{10,11... | collective-permute-start | bytes 1572872 | tf_op jit(solution)/shard_map/ppermute | solution.py:17
  201.2 8.7 %collective-permute-start.18 = (bf16[2,128,512]{2,1,0:T(8,128)(2,1)S(1)}, bf16[2,128,512]{2,1,0:T(8,128)(2,1)S(1)}, u32[]{:S(2)}, u32[]{:S(2)}) collective-permute-start(bf16[2,128,512]{2,1,0:T(8,128)(2,1)S(1)} %slice_bitcast_fusion.27), channel_id=1, source_target_pairs={{0,4},{4,0},{1,5},{5,1},{2,6},{6,2},{3,7},{7,3},{8,12},{12,8},{9,1... | collective-permute-start | bytes 786440 | tf_op jit(solution)/shard_map/cond/branch_1_fun/ppermute | solution.py:17
  203.0 8.1 %collective-permute-start.19 = (bf16[2,128,512]{2,1,0:T(8,128)(2,1)S(1)}, bf16[2,128,512]{2,1,0:T(8,128)(2,1)S(1)}, u32[]{:S(2)}, u32[]{:S(2)}) collective-permute-start(bf16[2,128,512]{2,1,0:T(8,128)(2,1)S(1)} %slice_bitcast_fusion.26), channel_id=1, source_target_pairs={{0,2},{2,0},{1,3},{3,1},{4,6},{6,4},{5,7},{7,5},{8,10},{10,8},{9,1... | collective-permute-start | bytes 786440 | tf_op jit(solution)/shard_map/cond/branch_1_fun/ppermute | solution.py:17
  217.2 24.8 %collective-permute-start.50 = (bf16[256,1792]{1,0:T(8,128)(2,1)S(1)}, bf16[256,1792]{1,0:T(8,128)(2,1)S(1)}, u32[]{:S(2)}, u32[]{:S(2)}) collective-permute-start(bf16[256,1792]{1,0:T(8,128)(2,1)S(1)} %copy-done.1), channel_id=1, source_target_pairs={{0,4},{4,0},{1,5},{5,1},{2,6},{6,2},{3,7},{7,3},{8,12},{12,8},{9,1... | collective-permute-start | bytes 2752520 | tf_op jit(solution)/shard_map/ppermute | solution.py:17
  229.1 12.9 %collective-permute-start.51 = (bf16[256,384]{1,0:T(8,128)(2,1)}, bf16[256,384]{1,0:T(8,128)(2,1)S(1)}, u32[]{:S(2)}, u32[]{:S(2)}) collective-permute-start(bf16[256,384]{1,0:T(8,128)(2,1)} %reduce-scatter.5.cloned.1.call-done.mine), channel_id=1, source_target_pairs={{0,4},{4,0},{1,5},{5,1},{2,6},{6,2},{3,7},{7,3},{8,12},{12,8},{9,1... | collective-permute-start | bytes 589832 | tf_op jit(solution)/shard_map/ppermute | solution.py:17
  (65 other events, 427.7 us)
Sparse Core Ops, SparseCore 0:
  35.2 64.5 all-gather.1
  118.0 68.6 reduce-scatter.2
  196.0 22.8 reduce-scatter.4
